TPU v7x, 32 devices: a whole 2x2x4 slice. The times are simulated.
32 devices in a mesh: ctx: 8 (over z, x), ch: 4 (over y, core).
Axes of the slice: x: 2, y: 2, z: 4, core: 2. Of those that a mesh axis runs over, the one named last changes fastest.
Arguments:
- x_first: bfloat16 [4096, 2048], P('ch', 'ctx'), may hold values from -6 to 6
- x_second: bfloat16 [4096, 2048], P('ch', 'ctx'), may hold values from -6 to 6
- x_value: bfloat16 [4096, 2048], P('ch', 'ctx'), may hold values from -6 to 6
- short_filter: float32 [3, 3, 4096], P(None, None, 'ch'), may hold values from -4 to 4
- long_filter: bfloat16 [4096, 2048], P('ch', 'ctx'), may hold values from -0.125 to 0.125
- skip_bias: float32 [4096], P('ch'), may hold values from -4 to 4
- norm_gain: float32 [4096], P('ch'), may hold values from 0.1 to 1.9
- cotangent: bfloat16 [4096, 2048], P('ch', 'ctx'), may hold values from -6 to 6
Outputs:
- output: bfloat16 [4096, 2048], P('ch', 'ctx')
- d_first: bfloat16 [4096, 2048], P('ch', 'ctx')
- d_second: bfloat16 [4096, 2048], P('ch', 'ctx')
- d_value: bfloat16 [4096, 2048], P('ch', 'ctx')
- d_long: float32 [4096, 2048], P(('ch', 'ctx'))
- d_short: float32 [3, 3, 4096], P(None, None, ('ch', 'ctx'))
- d_bias: float32 [4096], P(('ch', 'ctx'))
- d_gain: float32 [4096], P(('ch', 'ctx'))
All inputs are finite; a program needn't handle non-finite values.
Results may differ from a plain program's by a relative error of at most 0.012.
Values may be sent and summed in bfloat16 or wider, within the bound.
No kernel may reach another device: no remote copies, remote signals or barrier semaphores. Data moves between devices by JAX's collectives and lax.ppermute only.
A program may use at most 128 MiB of HBM per device.

v0:
```python
import math

import jax
import jax.numpy as jnp
from jax import lax
from jax.sharding import PartitionSpec as P

EPS = 1e-06
HIGH = lax.Precision.HIGHEST


def shifted(value, axis, steps):
    count = lax.axis_size(axis)
    first, last = (max(0, -steps), min(count, count - steps))
    return lax.ppermute(value, axis, [(source, source + steps) for source in range(first, last)])


def factor_pair(total):
    start = int(math.isqrt(total))
    first = total
    for cand in range(max(start, 2), total + 1):
        if cand % 2 == 0 and total % cand == 0:
            first = cand
            break
    return (first, total // first)


def angle_grid(count, rows, cols):
    prod = (
        jnp.arange(rows, dtype=jnp.int32)[:, None]
        * jnp.arange(cols, dtype=jnp.int32)[None, :]
        % count
    )
    return prod.astype(jnp.float32) * (2.0 * math.pi / count)


def split_table(table):
    upper = lax.optimization_barrier(table.astype(jnp.bfloat16))
    lower = (table - upper.astype(jnp.float32)).astype(jnp.bfloat16)
    return (upper, lower)


def make_tables(total):
    first, second = factor_pair(total)
    outer = angle_grid(first, first, first // 2)
    twist = angle_grid(total, first, second)
    inner = angle_grid(second, second, second)
    cos_a = jnp.cos(outer)
    sin_a = jnp.sin(outer)
    cos_upper, cos_lower = split_table(cos_a)
    sin_upper, sin_lower = split_table(sin_a)
    return (
        first,
        second,
        cos_a,
        sin_a,
        jnp.cos(twist),
        jnp.sin(twist),
        jnp.cos(inner),
        jnp.sin(inner),
        total,
        cos_upper,
        cos_lower,
        sin_upper,
        sin_lower,
    )


def split_product(upper, lower, shaped):
    return jnp.einsum(
        "kn,cnm->ckm", upper, shaped, preferred_element_type=jnp.float32
    ) + jnp.einsum("kn,cnm->ckm", lower, shaped, preferred_element_type=jnp.float32)


def forward_spectrum(values, tables):
    (
        first,
        second,
        cos_a,
        sin_a,
        cos_t,
        sin_t,
        cos_b,
        sin_b,
        total,
        cos_upper,
        cos_lower,
        sin_upper,
        sin_lower,
    ) = tables
    shaped = values.reshape(values.shape[0], first // 2, second)
    real_a = split_product(cos_upper, cos_lower, shaped)
    imag_a = -split_product(sin_upper, sin_lower, shaped)
    real_t = real_a * cos_t + imag_a * sin_t
    imag_t = imag_a * cos_t - real_a * sin_t
    real_b = jnp.einsum("ckm,mj->ckj", real_t, cos_b, precision=HIGH) + jnp.einsum(
        "ckm,mj->ckj", imag_t, sin_b, precision=HIGH
    )
    imag_b = jnp.einsum("ckm,mj->ckj", imag_t, cos_b, precision=HIGH) - jnp.einsum(
        "ckm,mj->ckj", real_t, sin_b, precision=HIGH
    )
    return (real_b, imag_b)


def inverse_half(real_s, imag_s, tables):
    first, second, cos_a, sin_a, cos_t, sin_t, cos_b, sin_b, total = tables[:9]
    real_z = jnp.einsum("ckj,jm->ckm", real_s, cos_b, precision=HIGH) - jnp.einsum(
        "ckj,jm->ckm", imag_s, sin_b, precision=HIGH
    )
    imag_z = jnp.einsum("ckj,jm->ckm", imag_s, cos_b, precision=HIGH) + jnp.einsum(
        "ckj,jm->ckm", real_s, sin_b, precision=HIGH
    )
    real_t = real_z * cos_t - imag_z * sin_t
    imag_t = imag_z * cos_t + real_z * sin_t
    result = jnp.einsum("kn,ckm->cnm", cos_a, real_t, precision=HIGH) - jnp.einsum(
        "kn,ckm->cnm", sin_a, imag_t, precision=HIGH
    )
    return result.reshape(result.shape[0], first // 2 * second) / total


def spec_product(left, right):
    return (left[0] * right[0] - left[1] * right[1], left[0] * right[1] + left[1] * right[0])


def spec_conj_product(left, right):
    return (left[0] * right[0] + left[1] * right[1], left[0] * right[1] - left[1] * right[0])


def local(x_first, x_second, x_value, short_filter, long_filter, skip_bias, norm_gain, cotangent):
    chans, steps_dev = x_first.shape
    width = chans * lax.axis_size("ch")
    length = steps_dev * lax.axis_size("ctx")
    tables = make_tables(2 * length)
    inputs = jnp.stack([x_first, x_second, x_value])
    before = shifted(inputs[:, :, steps_dev - 2 :], "ctx", 1)
    padded = jnp.concatenate([before, inputs], axis=2).astype(jnp.float32)
    taps = short_filter[:, :, :, None]
    shorts = (
        taps[:, 0] * padded[:, :, 2:]
        + taps[:, 1] * padded[:, :, 1:-1]
        + taps[:, 2] * padded[:, :, :-2]
    ).astype(jnp.bfloat16)
    first_s = shorts[0]
    second_s = shorts[1]
    third_s = shorts[2]
    gated = (second_s.astype(jnp.float32) * third_s.astype(jnp.float32)).astype(jnp.bfloat16)
    bias_col = skip_bias[:, None]
    gain_col = norm_gain[:, None]
    gated_cm, filter_cm = (
        lax.all_to_all(gated, "ctx", split_axis=0, concat_axis=1, tiled=True),
        lax.all_to_all(long_filter, "ctx", split_axis=0, concat_axis=1, tiled=True),
    )
    filt_spec = forward_spectrum(filter_cm, tables)
    gate_spec = forward_spectrum(gated_cm, tables)
    conv_cm = inverse_half(*spec_product(gate_spec, filt_spec), tables).astype(jnp.bfloat16)
    conv = lax.all_to_all(conv_cm, "ctx", split_axis=1, concat_axis=0, tiled=True)
    inner = conv.astype(jnp.float32) + bias_col * gated.astype(jnp.float32)
    mixed = first_s.astype(jnp.float32) * inner
    scaled = cotangent.astype(jnp.float32) * gain_col
    sum_sq, dotted = lax.psum(
        (jnp.sum(mixed * mixed, axis=0), jnp.sum(scaled * mixed, axis=0)), "ch"
    )
    recip = lax.rsqrt(sum_sq / width + EPS)
    output = (mixed * recip * gain_col).astype(jnp.bfloat16)
    d_mixed = recip * scaled - mixed * recip**3 * (dotted / width)
    d_inner = (d_mixed * first_s.astype(jnp.float32)).astype(jnp.bfloat16)
    grad_first = (d_mixed * inner).astype(jnp.bfloat16)
    gain_part = jnp.sum(cotangent.astype(jnp.float32) * mixed * recip, axis=1)
    bias_part = jnp.sum(d_inner.astype(jnp.float32) * gated.astype(jnp.float32), axis=1)
    d_inner_cm = lax.all_to_all(d_inner, "ctx", split_axis=0, concat_axis=1, tiled=True)
    grad_spec = forward_spectrum(d_inner_cm, tables)
    back_cm = inverse_half(*spec_conj_product(filt_spec, grad_spec), tables).astype(jnp.bfloat16)
    d_long = inverse_half(*spec_conj_product(gate_spec, grad_spec), tables)
    back = lax.all_to_all(back_cm, "ctx", split_axis=1, concat_axis=0, tiled=True)
    d_gated = (bias_col * d_inner.astype(jnp.float32) + back.astype(jnp.float32)).astype(
        jnp.bfloat16
    )
    grad_second = (d_gated.astype(jnp.float32) * third_s.astype(jnp.float32)).astype(jnp.bfloat16)
    grad_third = (d_gated.astype(jnp.float32) * second_s.astype(jnp.float32)).astype(jnp.bfloat16)
    grads = jnp.stack([grad_first, grad_second, grad_third])
    after = shifted(grads[:, :, :2], "ctx", -1)
    grad_pad = jnp.concatenate([grads, after], axis=2).astype(jnp.float32)
    d_inputs = (
        taps[:, 0] * grad_pad[:, :, :-2]
        + taps[:, 1] * grad_pad[:, :, 1:-1]
        + taps[:, 2] * grad_pad[:, :, 2:]
    ).astype(jnp.bfloat16)
    grads_f = grads.astype(jnp.float32)
    filter_part = jnp.stack(
        [jnp.sum(grads_f * padded[:, :, 2 - k : 2 - k + steps_dev], axis=2) for k in range(3)],
        axis=1,
    )
    d_short, d_bias, d_gain = (
        lax.psum_scatter(filter_part, "ctx", scatter_dimension=2, tiled=True),
        lax.psum_scatter(bias_part, "ctx", scatter_dimension=0, tiled=True),
        lax.psum_scatter(gain_part, "ctx", scatter_dimension=0, tiled=True),
    )
    return (output, d_inputs[0], d_inputs[1], d_inputs[2], d_long, d_short, d_bias, d_gain)


def solution(mesh):
    return jax.shard_map(
        local,
        mesh=mesh,
        in_specs=(
            P("ch", "ctx"),
            P("ch", "ctx"),
            P("ch", "ctx"),
            P(None, None, "ch"),
            P("ch", "ctx"),
            P("ch"),
            P("ch"),
            P("ch", "ctx"),
        ),
        out_specs=(
            P("ch", "ctx"),
            P("ch", "ctx"),
            P("ch", "ctx"),
            P("ch", "ctx"),
            P(("ch", "ctx"), None),
            P(None, None, ("ch", "ctx")),
            P(("ch", "ctx")),
            P(("ch", "ctx")),
        ),
        check_vma=False,
    )
```

profile of v0, /device:TPU:0, one launch (start us, length us, event | category | flops | bytes accessed | tf_op | source)
XLA Modules:
  0.0 352.0 jit_solution(12579834896259514697)
XLA Ops:
  9.0 4.8 %collective-permute-start = (bf16[3,1024,2]{1,2,0:T(2,128)(2,1)S(1)}, bf16[3,1024,2]{1,2,0:T(2,128)(2,1)S(1)}, u32[]{:S(2)}, u32[]{:S(2)}) collective-permute-start(bf16[3,1024,2]{1,2,0:T(2,128)(2,1)S(1)} %copy.127), channel_id=1, source_target_pairs={{0,4},{4,8},{8,12},{12,16},{16,20},{20,24},{24,28},{1,5},{5,9},{9,... | collective-permute-start | bytes 36872 | tf_op jit(solution)/shard_map/ppermute | solution.py:15
  13.9 4.9 %all-to-all-start.1 = ((bf16[8,128,256]{2,1,0:T(8,128)(2,1)}), bf16[8,128,256]{2,1,0:T(8,128)(2,1)S(1)}, u32[]{:S(2)}, u32[]{:S(2)}) async-start(bf16[8,128,256]{2,1,0:T(8,128)(2,1)} %bitcast.279), calls=%async_computation.1 | async-start | bytes 1048576 | tf_op jit(solution)/shard_map/all_to_all | solution.py:151
  24.8 8.2 %all-to-all-done.1 = bf16[8,128,256]{2,1,0:T(8,128)(2,1)S(1)} async-done(((bf16[8,128,256]{2,1,0:T(8,128)(2,1)}), bf16[8,128,256]{2,1,0:T(8,128)(2,1)S(1)}, u32[]{:S(2)}, u32[]{:S(2)}) %all-to-all-start.1) | async-done | bytes 524320 | tf_op jit(solution)/shard_map/all_to_all | solution.py:151
  33.0 3.8 %all-to-all-start = ((bf16[8,128,256]{2,1,0:T(8,128)(2,1)}), bf16[8,128,256]{2,1,0:T(8,128)(2,1)S(1)}, u32[]{:S(2)}, u32[]{:S(2)}) async-start(bf16[8,128,256]{2,1,0:T(8,128)(2,1)} %bitcast.5), calls=%async_computation | async-start | bytes 1048576 | tf_op jit(solution)/shard_map/all_to_all | solution.py:150
  47.0 5.0 %fusion.64 = f32[128,64,64]{0,2,1:T(8,128)} fusion(f32[128,64,64]{0,2,1:T(8,128)S(1)} %fusion.44, f32[128,64,64]{0,1,2:T(8,128)S(1)} %get-tuple-element.53), kind=kOutput, calls=%fused_computation.94 | convolution fusion | flops 403234816 | bytes 6291456 | tf_op jit(solution)/shard_map/ckm,mj->ckj/dot_general | solution.py:96
  52.0 4.7 %fusion.67 = f32[128,64,64]{0,2,1:T(8,128)} fusion(f32[128,64,64]{0,2,1:T(8,128)S(1)} %fusion.42, f32[128,64,64]{0,1,2:T(8,128)S(1)} %get-tuple-element.53), kind=kOutput, calls=%fused_computation.95 | convolution fusion | flops 403234816 | bytes 6291456 | tf_op jit(solution)/shard_map/ckm,mj->ckj/dot_general | solution.py:99
  60.2 3.3 fusion.52
  63.5 3.7 %fusion.50 = f32[128,64,64]{0,2,1:T(8,128)S(1)} fusion(f32[128,64,64]{0,1,2:T(8,128)S(1)} %get-tuple-element.56), kind=kOutput, calls=%fused_computation.84 | convolution fusion | flops 402710528 | bytes 4194304 | tf_op jit(solution)/shard_map/ckm,mj->ckj/dot_general | solution.py:99
  67.3 3.4 fusion.58
  70.7 5.5 %multiply_subtract_fusion.2 = (f32[128,64,64]{0,2,1:T(8,128)S(1)}, f32[128,64,64]{0,2,1:T(8,128)S(1)}, f32[128,64,64]{0,2,1:T(8,128)}) fusion(f32[128,64,64]{0,2,1:T(8,128)S(1)} %copy-done.7, f32[128,64,64]{0,2,1:T(8,128)S(1)} %fusion.58, f32[128,64,64]{0,2,1:T(8,128)S(1)} %copy-done.5, f32[128,64,64]{0,2,1:T(8,128)S(1)} %fusion.50, ...), kind=kOutput, calls=%fused_computation.63 | convolution fusion | flops 406380544 | bytes 16777216 | tf_op jit(solution)/shard_map/ckm,mj->ckj/dot_general | solution.py:99
  85.0 7.7 %fusion.26 = f32[128,64,32]{0,2,1:T(8,128)S(1)} fusion(f32[64,64]{0,1:T(8,128)S(1)} %get-tuple-element.72, f32[64,64]{0,1:T(8,128)S(1)} %get-tuple-element.73, f32[128,64,64]{0,2,1:T(8,128)S(1)} %fusion.173, f32[128,64,64]{0,2,1:T(8,128)S(1)} %fusion.191, f32[128,64,64]{0,2,1:T(8,128)S(1)} %fusion.171, f32[128,64,64]{0,2,1:T(8,128)S(1)} %fusion.189), kind=kOutput, calls=%fused_computation.54 | convolution fusion | flops 203976704 | bytes 9469952 | tf_op jit(solution)/shard_map/kn,ckm->cnm/dot_general | solution.py:115
  92.7 9.7 %fusion.109 = bf16[128,32,64]{0,1,2:T(8,128)(2,1)S(1)} fusion(f32[128,64,32]{0,2,1:T(8,128)S(1)} %fusion.26, f32[64,64]{0,1:T(8,128)S(1)} %get-tuple-element.72, f32[64,64]{0,1:T(8,128)S(1)} %get-tuple-element.73, f32[128,64,64]{0,2,1:T(8,128)S(1)} %fusion.173, f32[128,64,64]{0,2,1:T(8,128)S(1)} %fusion.191, f32[128,64,64]{0,2,1:T(8,128)S(1)} %fusion.171, ...), kind=kOutput, calls=%fused_computation.127 | convolution fusion | flops 204763136 | bytes 9994240 | tf_op jit(solution)/shard_map/kn,ckm->cnm/dot_general | solution.py:115
  102.6 19.7 %all_to_all.65 = bf16[128,8,256]{0,2,1:T(8,128)(2,1)S(1)} all-to-all(bf16[128,8,256]{0,2,1:T(8,128)(2,1)S(1)} %bitcast.277), channel_id=1, replica_groups=mesh['ctx'=8,'ch'=4] {'ctx'}, dimensions={1} | all-to-all | bytes 1048576 | tf_op jit(solution)/shard_map/all_to_all | solution.py:156
  126.3 5.6 %psum.14 = f32[256]{0:T(256)S(1)} all-reduce(f32[256]{0:T(256)S(1)} %get-tuple-element.43), channel_id=1, replica_groups=mesh['ctx'=8,'ch'=4] {'ch'}, use_global_device_ids=true, to_apply=%region_1.2 | all-reduce | flops 256 | bytes 2048 | tf_op jit(solution)/shard_map/psum | solution.py:160
  133.6 6.6 %psum.15 = f32[256]{0:T(256)S(1)} all-reduce(f32[256]{0:T(256)S(1)} %get-tuple-element.36), channel_id=1, replica_groups=mesh['ctx'=8,'ch'=4] {'ch'}, use_global_device_ids=true, to_apply=%region_3.4 | all-reduce | flops 256 | bytes 2048 | tf_op jit(solution)/shard_map/psum | solution.py:160
  143.3 3.6 %all-to-all-start.3 = ((bf16[8,128,256]{2,1,0:T(8,128)(2,1)}), bf16[8,128,256]{2,1,0:T(8,128)(2,1)S(1)}, u32[]{:S(2)}, u32[]{:S(2)}) async-start(bf16[8,128,256]{2,1,0:T(8,128)(2,1)} %bitcast.266), calls=%async_computation.3 | async-start | bytes 1048576 | tf_op jit(solution)/shard_map/all_to_all | solution.py:170
  148.2 22.5 %all-reduce.2 = (f32[1024]{0:T(1024)S(1)}, f32[1024]{0:T(1024)S(1)}) all-reduce(f32[1024]{0:T(1024)S(1)} %get-tuple-element.39, f32[1024]{0:T(1024)S(1)} %get-tuple-element.35), channel_id=3, replica_groups=mesh['ctx'=8,'ch'=4] {'ctx'}, use_global_device_ids=true, to_apply=%region_9.10.clone | all-reduce | flops 2048 | bytes 16384
  175.4 3.3 fusion.36
  182.1 3.6 %fusion.70 = f32[128,64,64]{0,2,1:T(8,128)S(1)} fusion(f32[128,64,64]{0,2,1:T(8,128)S(1)} %fusion.36, f32[128,64,64]{0,1,2:T(8,128)S(1)} %get-tuple-element.51), kind=kOutput, calls=%fused_computation.96 | convolution fusion | flops 403234816 | bytes 6291456 | tf_op jit(solution)/shard_map/ckm,mj->ckj/dot_general | solution.py:96
  185.7 4.6 %multiply_add_fusion = (f32[128,64,64]{0,2,1:T(8,128)S(1)}, f32[128,64,64]{0,2,1:T(8,128)S(1)}, f32[128,64,64]{0,2,1:T(8,128)S(1)}, f32[128,64,64]{0,2,1:T(8,128)S(1)}) fusion(f32[128,64,64]{0,2,1:T(8,128)S(1)} %copy-done.11, f32[128,64,64]{0,2,1:T(8,128)S(1)} %copy-done.10, f32[128,64,64]{0,2,1:T(8,128)S(1)} %fusion.70, f32[128,64,64]{0,2,1:T(8,128)S(1)} %copy-done.8, ...), kind=kOutput, calls=%fused_computation.42 | convolution fusion | flops 409526272 | bytes 23068672 | tf_op jit(solution)/shard_map/ckm,mj->ckj/dot_general | solution.py:99
  199.4 3.5 fusion.163
  202.8 3.4 fusion.179
  206.3 3.5 fusion.161
  209.7 3.4 fusion.181
  213.2 7.6 %fusion.18 = f32[128,64,32]{0,2,1:T(8,128)S(1)} fusion(f32[64,64]{0,1:T(8,128)S(1)} %get-tuple-element.72, f32[64,64]{0,1:T(8,128)S(1)} %get-tuple-element.73, f32[128,64,64]{0,2,1:T(8,128)S(1)} %fusion.167, f32[128,64,64]{0,2,1:T(8,128)S(1)} %fusion.185, f32[128,64,64]{0,2,1:T(8,128)S(1)} %fusion.165, f32[128,64,64]{0,2,1:T(8,128)S(1)} %fusion.183), kind=kOutput, calls=%fused_computation.43 | convolution fusion | flops 203976704 | bytes 9469952 | tf_op jit(solution)/shard_map/kn,ckm->cnm/dot_general | solution.py:115
  220.8 9.7 %fusion.106 = bf16[128,32,64]{0,1,2:T(8,128)(2,1)S(1)} fusion(f32[128,64,32]{0,2,1:T(8,128)S(1)} %fusion.18, f32[64,64]{0,1:T(8,128)S(1)} %get-tuple-element.72, f32[64,64]{0,1:T(8,128)S(1)} %get-tuple-element.73, f32[128,64,64]{0,2,1:T(8,128)S(1)} %fusion.167, f32[128,64,64]{0,2,1:T(8,128)S(1)} %fusion.185, f32[128,64,64]{0,2,1:T(8,128)S(1)} %fusion.165, ...), kind=kOutput, calls=%fused_computation.126 | convolution fusion | flops 204763136 | bytes 9994240 | tf_op jit(solution)/shard_map/kn,ckm->cnm/dot_general | solution.py:115
  231.5 4.1 %all-to-all-start.4 = ((bf16[128,8,256]{0,2,1:T(8,128)(2,1)}), bf16[128,8,256]{0,2,1:T(8,128)(2,1)}, u32[]{:S(2)}, u32[]{:S(2)}) async-start(bf16[128,8,256]{0,2,1:T(8,128)(2,1)} %bitcast.37), calls=%async_computation.4 | async-start | bytes 1048576 | tf_op jit(solution)/shard_map/all_to_all | solution.py:174
  235.8 11.7 %fusion.10 = f32[128,64,32]{0,2,1:T(8,128)S(1)} fusion(f32[64,64]{0,1:T(8,128)S(1)} %get-tuple-element.72, f32[64,64]{0,1:T(8,128)S(1)} %get-tuple-element.73, f32[128,64,64]{0,2,1:T(8,128)} %fusion.163, f32[128,64,64]{0,2,1:T(8,128)} %fusion.181, f32[128,64,64]{0,2,1:T(8,128)} %fusion.161, f32[128,64,64]{0,2,1:T(8,128)} %fusion.179), kind=kOutput, calls=%fused_computation.33 | convolution fusion | flops 203976704 | bytes 9469952 | tf_op jit(solution)/shard_map/kn,ckm->cnm/dot_general | solution.py:115
  247.5 7.5 %fusion.88 = f32[128,32,64]{0,1,2:T(8,128)S(1)} fusion(f32[128,64,32]{0,2,1:T(8,128)S(1)} %fusion.10, f32[64,64]{0,1:T(8,128)S(1)} %get-tuple-element.72, f32[64,64]{0,1:T(8,128)S(1)} %get-tuple-element.73, f32[128,64,64]{0,2,1:T(8,128)S(1)} %copy-done.1, f32[128,64,64]{0,2,1:T(8,128)S(1)} %copy-done.4, f32[128,64,64]{0,2,1:T(8,128)S(1)} %copy-done.3, ...), kind=kOutput, calls=%fused_computation.106 | convolution fusion | flops 204500992 | bytes 10518528 | tf_op jit(solution)/shard_map/kn,ckm->cnm/dot_general | solution.py:115
  263.3 6.5 %fusion = (f32[3,1024]{1,0:T(4,128)S(1)}, f32[3,1024]{1,0:T(4,128)S(1)}, f32[3,1024]{1,0:T(4,128)S(1)}) fusion(f32[3,1024,258]{2,1,0:T(8,128)} %copy-done, bf16[1,1024,256]{2,1,0:T(8,128)(2,1)S(1)} %fusion.137, bf16[1,1024,256]{2,1,0:T(8,128)(2,1)S(1)} %get-tuple-element.41, bf16[1,1024,256]{2,1,0:T(8,128)(2,1)S(1)} %bitcast.263), kind=kLoop, calls=%fused_computation.3 | loop fusion | flops 7068672 | bytes 11046912 | tf_op jit(solution)/shard_map/reduce_sum | solution.py:190
  275.5 3.3 reshape.132
  284.1 59.1 %reduce-scatter.4.cloned.1.call-done = f32[128,9]{1,0:T(8,128)} async-done(((f32[1024,9]{1,0:T(8,128)}), f32[128,9]{1,0:T(8,128)}) %reduce-scatter.4.cloned.1.call-update) | async-done | bytes 4624
  (117 shorter events, 78.5 us)
Async XLA Ops:
  7.2 11.8 %copy-start.18 = (f32[3,3,1024]{2,1,0:T(4,128)S(1)}, f32[3,3,1024]{2,1,0:T(4,128)}, u32[]{:S(2)}) copy-start(f32[3,3,1024]{2,1,0:T(4,128)} %param.11) | copy-start | bytes 110596
  7.2 12.4 %copy-start.14 = (bf16[1024,256]{1,0:T(8,128)(2,1)S(1)}, bf16[1024,256]{1,0:T(8,128)(2,1)}, u32[]{:S(2)}) copy-start(bf16[1024,256]{1,0:T(8,128)(2,1)} %param.10) | copy-start | bytes 1572868
  7.2 12.4 %copy-start.15 = (bf16[1024,256]{1,0:T(8,128)(2,1)S(1)}, bf16[1024,256]{1,0:T(8,128)(2,1)}, u32[]{:S(2)}) copy-start(bf16[1024,256]{1,0:T(8,128)(2,1)} %param.9) | copy-start | bytes 1572868
  7.2 12.4 %copy-start.16 = (bf16[1024,256]{1,0:T(8,128)(2,1)S(1)}, bf16[1024,256]{1,0:T(8,128)(2,1)}, u32[]{:S(2)}) copy-start(bf16[1024,256]{1,0:T(8,128)(2,1)} %param.8) | copy-start | bytes 1572868
  9.0 10.1 %collective-permute-start = (bf16[3,1024,2]{1,2,0:T(2,128)(2,1)S(1)}, bf16[3,1024,2]{1,2,0:T(2,128)(2,1)S(1)}, u32[]{:S(2)}, u32[]{:S(2)}) collective-permute-start(bf16[3,1024,2]{1,2,0:T(2,128)(2,1)S(1)} %copy.127), channel_id=1, source_target_pairs={{0,4},{4,8},{8,12},{12,16},{16,20},{20,24},{24,28},{1,5},{5,9},{9,... | collective-permute-start | bytes 36872 | tf_op jit(solution)/shard_map/ppermute | solution.py:15
  13.9 19.1 %all-to-all-start.1 = ((bf16[8,128,256]{2,1,0:T(8,128)(2,1)}), bf16[8,128,256]{2,1,0:T(8,128)(2,1)S(1)}, u32[]{:S(2)}, u32[]{:S(2)}) async-start(bf16[8,128,256]{2,1,0:T(8,128)(2,1)} %bitcast.279), calls=%async_computation.1 | async-start | bytes 1048576 | tf_op jit(solution)/shard_map/all_to_all | solution.py:151
  20.6 3.2 copy-start
  33.0 23.7 %all-to-all-start = ((bf16[8,128,256]{2,1,0:T(8,128)(2,1)}), bf16[8,128,256]{2,1,0:T(8,128)(2,1)S(1)}, u32[]{:S(2)}, u32[]{:S(2)}) async-start(bf16[8,128,256]{2,1,0:T(8,128)(2,1)} %bitcast.5), calls=%async_computation | async-start | bytes 1048576 | tf_op jit(solution)/shard_map/all_to_all | solution.py:150
  67.3 3.4 copy-start.5
  67.3 3.4 copy-start.7
  70.7 5.5 %copy-start.9 = (f32[128,64,64]{0,2,1:T(8,128)}, f32[128,64,64]{0,2,1:T(8,128)S(1)}, u32[]{:S(2)}) copy-start(f32[128,64,64]{0,2,1:T(8,128)S(1)} %fusion.58) | copy-start | bytes 6291460
  122.3 2.6 copy-start.17
  124.9 7.0 %copy-start.13 = (bf16[1024,256]{1,0:T(8,128)(2,1)S(1)}, bf16[1024,256]{1,0:T(8,128)(2,1)}, u32[]{:S(2)}) copy-start(bf16[1024,256]{1,0:T(8,128)(2,1)} %param.15) | copy-start | bytes 1572868
  125.0 7.0 %copy-start.19 = (f32[1024]{0:T(1024)S(1)}, f32[1024]{0:T(1024)}, u32[]{:S(2)}) copy-start(f32[1024]{0:T(1024)} %param.14) | copy-start | bytes 12292
  140.3 6.7 %copy-start.20 = (u32[32]{0:T(128)S(1)}, u32[32]{0:T(128)}, u32[]{:S(2)}) copy-start(u32[32]{0:T(128)} %constant.53) | copy-start | bytes 388
  143.3 28.6 %all-to-all-start.3 = ((bf16[8,128,256]{2,1,0:T(8,128)(2,1)}), bf16[8,128,256]{2,1,0:T(8,128)(2,1)S(1)}, u32[]{:S(2)}, u32[]{:S(2)}) async-start(bf16[8,128,256]{2,1,0:T(8,128)(2,1)} %bitcast.266), calls=%async_computation.3 | async-start | bytes 1048576 | tf_op jit(solution)/shard_map/all_to_all | solution.py:170
  178.7 6.9 %copy-start.11 = (f32[128,64,64]{0,2,1:T(8,128)S(1)}, f32[128,64,64]{0,2,1:T(8,128)}, u32[]{:S(2)}) copy-start(f32[128,64,64]{0,2,1:T(8,128)} %get-tuple-element.69) | copy-start | bytes 6291460
  182.1 3.6 %copy-start.6 = (f32[128,64,64]{0,2,1:T(8,128)S(1)}, f32[128,64,64]{0,2,1:T(8,128)}, u32[]{:S(2)}) copy-start(f32[128,64,64]{0,2,1:T(8,128)} %fusion.64) | copy-start | bytes 6291460
  182.1 3.6 %copy-start.8 = (f32[128,64,64]{0,2,1:T(8,128)S(1)}, f32[128,64,64]{0,2,1:T(8,128)}, u32[]{:S(2)}) copy-start(f32[128,64,64]{0,2,1:T(8,128)} %fusion.67) | copy-start | bytes 6291460
  182.1 3.6 %copy-start.10 = (f32[128,64,64]{0,2,1:T(8,128)S(1)}, f32[128,64,64]{0,2,1:T(8,128)}, u32[]{:S(2)}) copy-start(f32[128,64,64]{0,2,1:T(8,128)} %copy-done.9) | copy-start | bytes 6291460
  231.5 25.4 %all-to-all-start.4 = ((bf16[128,8,256]{0,2,1:T(8,128)(2,1)}), bf16[128,8,256]{0,2,1:T(8,128)(2,1)}, u32[]{:S(2)}, u32[]{:S(2)}) async-start(bf16[128,8,256]{0,2,1:T(8,128)(2,1)} %bitcast.37), calls=%async_computation.4 | async-start | bytes 1048576 | tf_op jit(solution)/shard_map/all_to_all | solution.py:174
  235.7 107.5 %reduce-scatter.4.cloned.1.call-start = ((), (), s32[]{:S(2)}) async-start(), calls=%async_computation.6 | async-start | bytes 589824
  235.7 11.7 %copy-start.1 = (f32[128,64,64]{0,2,1:T(8,128)S(1)}, f32[128,64,64]{0,2,1:T(8,128)}, u32[]{:S(2)}) copy-start(f32[128,64,64]{0,2,1:T(8,128)} %fusion.163) | copy-start | bytes 6291460
  235.7 11.7 %copy-start.2 = (f32[128,64,64]{0,2,1:T(8,128)S(1)}, f32[128,64,64]{0,2,1:T(8,128)}, u32[]{:S(2)}) copy-start(f32[128,64,64]{0,2,1:T(8,128)} %fusion.179) | copy-start | bytes 6291460
  235.8 11.7 %copy-start.3 = (f32[128,64,64]{0,2,1:T(8,128)S(1)}, f32[128,64,64]{0,2,1:T(8,128)}, u32[]{:S(2)}) copy-start(f32[128,64,64]{0,2,1:T(8,128)} %fusion.161) | copy-start | bytes 6291460
  235.8 11.7 %copy-start.4 = (f32[128,64,64]{0,2,1:T(8,128)S(1)}, f32[128,64,64]{0,2,1:T(8,128)}, u32[]{:S(2)}) copy-start(f32[128,64,64]{0,2,1:T(8,128)} %fusion.181) | copy-start | bytes 6291460
  256.9 4.7 %copy-start.12 = (bf16[1024,256]{1,0:T(8,128)(2,1)S(1)}, bf16[1024,256]{1,0:T(8,128)(2,1)}, u32[]{:S(2)}) copy-start(bf16[1024,256]{1,0:T(8,128)(2,1)} %get-tuple-element.40) | copy-start | bytes 1572868
  272.4 6.5 %collective-permute-start.1 = (bf16[3,1024,2]{1,2,0:T(2,128)(2,1)S(1)}, bf16[3,1024,2]{1,2,0:T(2,128)(2,1)S(1)}, u32[]{:S(2)}, u32[]{:S(2)}) collective-permute-start(bf16[3,1024,2]{1,2,0:T(2,128)(2,1)S(1)} %copy.168), channel_id=1, source_target_pairs={{4,0},{8,4},{12,8},{16,12},{20,16},{24,20},{28,24},{5,1},{9,5},{13... | collective-permute-start | bytes 36872 | tf_op jit(solution)/shard_map/ppermute | solution.py:15
Sparse Core Ops, SparseCore 0:
  279.0 64.1 reduce-scatter.3
where the time goes:
time: 356 us; the launch traced here: 352 us
  matrix products  142 us (40%)
  waiting for transfers between devices  67.3 us (19%)
  blocking collectives  54.5 us (15%)
  other arithmetic  28.2 us (8%)
  starting transfers between devices  22.6 us (6%)
  local copies, waits for them, and re-layouts  21.5 us (6%)
  between operations  15.6 us (4%)
    unnamed x2, waiting for transfers between devices  59.1 us
    dot_general x3, matrix products, inverse_half(): jnp.einsum('kn,ckm->cnm', sin_a, imag_t, precision=HIGH)  27 us
    dot_general x3, matrix products, inverse_half(): jnp.einsum('kn,ckm->cnm', cos_a, real_t, precision=HIGH)  26.9 us
    unnamed x1, blocking collectives  22.5 us
    all_to_all x1, blocking collectives, local(): lax.all_to_all(conv_cm, 'ctx', split_axis=1, concat_axis=0, tiled=True)  19.7 us
    dot_general x3, matrix products, forward_spectrum(): jnp.einsum('ckm,mj->ckj', real_t, sin_b, precision=HIGH)  14.9 us
    psum x2, blocking collectives, local(): lax.psum((jnp.sum(mixed * mixed, axis=0), jnp.sum(scaled * mixed, axis=0)...  12.3 us
    dot_general x3, matrix products, forward_spectrum(): jnp.einsum('ckm,mj->ckj', real_t, cos_b, precision=HIGH)  11.9 us
  transfers between devices with their start and end apart: 7, of which 2 were waited for; matrix products, arithmetic and copies ran while one was open for 17% of the time, Pallas kernels for 0%

commit v1 on v0

v1 whole, which is shorter than its diff:
```python
import math

import jax
import jax.numpy as jnp
import numpy as np
from jax import lax
from jax.experimental import pallas as pl
from jax.experimental.pallas import tpu as pltpu
from jax.sharding import PartitionSpec as P

EPS = 1e-06
LANES = 128
ROWS = 16
HALF = 8


def shifted(value, axis, steps):
    count = lax.axis_size(axis)
    first, last = (max(0, -steps), min(count, count - steps))
    return lax.ppermute(value, axis, [(source, source + steps) for source in range(first, last)])


def root(angle):
    return math.cos(2 * math.pi * angle), math.sin(2 * math.pi * angle)


def slab_angles(slabs):
    angles = [-0.25]
    while len(angles) < slabs:
        angles = [a / 2 + extra for a in angles for extra in (0.0, 0.5)]
    return angles


def split_angles(slabs):
    levels, angles = [], [-0.25]
    while len(angles) < slabs:
        levels.append([a / 2 for a in angles])
        angles = [a / 2 + extra for a in angles for extra in (0.0, 0.5)]
    return levels


def slabs_forward(xs):
    slabs = len(xs)
    data = None
    for level, turns in enumerate(split_angles(slabs)):
        size = slabs >> level
        half = size // 2
        new = [None] * slabs
        for b, turn in enumerate(turns):
            c, s = root(turn)
            for n in range(half):
                lo, hi = b * size + n, b * size + n + half
                if data is None:
                    tr, ti = xs[hi] * c, xs[hi] * s
                    new[lo] = (xs[lo] + tr, ti)
                    new[hi] = (xs[lo] - tr, -ti)
                else:
                    (ar, ai), (br, bi) = data[lo], data[hi]
                    tr, ti = br * c - bi * s, br * s + bi * c
                    new[lo] = (ar + tr, ai + ti)
                    new[hi] = (ar - tr, ai - ti)
        data = new
    return data


def slabs_inverse(data):
    slabs = len(data)
    levels = split_angles(slabs)
    for level in range(len(levels) - 1, -1, -1):
        size = slabs >> level
        half = size // 2
        new = [None] * slabs
        for b, turn in enumerate(levels[level]):
            c, s = root(turn)
            for n in range(half):
                lo, hi = b * size + n, b * size + n + half
                (ur, ui), (vr, vi) = data[lo], data[hi]
                dr, di = ur - vr, ui - vi
                if level == 0:
                    new[lo] = ur + vr
                    new[hi] = dr * c + di * s
                else:
                    new[lo] = (ur + vr, ui + vi)
                    new[hi] = (dr * c + di * s, di * c - dr * s)
        data = new
    return data


def make_tables(length):
    slabs = length // LANES
    angle = np.array(slab_angles(slabs))[:, None] * np.arange(LANES)[None, :] / LANES
    twist = np.stack([np.cos(2 * np.pi * angle), np.sin(2 * np.pi * angle)], 1).astype(np.float32)
    grid = np.arange(LANES)[:, None] * np.arange(LANES)[None, :] % LANES * (2 * np.pi / LANES)
    cos, sin = np.cos(grid), np.sin(grid)
    fwd = np.block([[cos, -sin], [sin, cos]]).astype(np.float32)
    inv = np.block([[cos, sin], [-sin, cos]]).astype(np.float32)

    def two(mat):
        upper = mat.astype(jnp.bfloat16)
        lower = (mat - upper.astype(np.float32)).astype(jnp.bfloat16)
        return np.stack([upper, lower])

    return jnp.asarray(twist), jnp.asarray(two(fwd)), jnp.asarray(two(inv))


def split_dot(value, mat_ref):
    upper = value.astype(jnp.bfloat16)
    lower = (value - upper.astype(jnp.float32)).astype(jnp.bfloat16)
    dot = lambda a, b: jnp.dot(a, b, preferred_element_type=jnp.float32)
    return dot(upper, mat_ref[0]) + (dot(lower, mat_ref[0]) + dot(upper, mat_ref[1]))


def forward_group(x_ref, row, twist_ref, mat_ref, work):
    parts, _, width = x_ref.shape
    per = width // LANES
    slabs = parts * per
    xs = [
        x_ref[s // per, row : row + ROWS, s % per * LANES : (s % per + 1) * LANES].astype(jnp.float32)
        for s in range(slabs)
    ]
    for h in range(0, ROWS, HALF):
        data = slabs_forward([x[h : h + HALF] for x in xs])
        for j, (re, im) in enumerate(data):
            tc, ts = twist_ref[j, 0:1], twist_ref[j, 1:2]
            work[j * ROWS + h : j * ROWS + h + HALF, :LANES] = re * tc - im * ts
            work[j * ROWS + h : j * ROWS + h + HALF, LANES:] = re * ts + im * tc
    return split_dot(work[...], mat_ref)


def inverse_group(spec, scale, twist_ref, mat_ref, work, store):
    slabs = spec.shape[0] // ROWS
    work[...] = split_dot(spec * scale, mat_ref)
    for h in range(0, ROWS, HALF):
        data = []
        for j in range(slabs):
            tc, ts = twist_ref[j, 0:1], twist_ref[j, 1:2]
            re = work[j * ROWS + h : j * ROWS + h + HALF, :LANES]
            im = work[j * ROWS + h : j * ROWS + h + HALF, LANES:]
            data.append((re * tc + im * ts, im * tc - re * ts))
        for s, value in enumerate(slabs_inverse(data)):
            store(s, h, value)


def product(a, b):
    ar, ai, br, bi = a[:, :LANES], a[:, LANES:], b[:, :LANES], b[:, LANES:]
    return jnp.concatenate([ar * br - ai * bi, ar * bi + ai * br], 1)


def conj_product(a, b):
    ar, ai, br, bi = a[:, :LANES], a[:, LANES:], b[:, :LANES], b[:, LANES:]
    return jnp.concatenate([ar * br + ai * bi, ar * bi - ai * br], 1)


def spectrum_kernel(x_ref, twist_ref, mat_ref, spec_ref, work):
    for g in range(spec_ref.shape[0]):
        spec_ref[g] = forward_group(x_ref, g * ROWS, twist_ref, mat_ref, work.at[g])


def filter_kernel(conj, scale, x_ref, filt_ref, twist_ref, fwd_ref, inv_ref, out_ref, spec_ref, work, outs):
    per = x_ref.shape[2] // LANES
    for g in range(spec_ref.shape[0]):
        spec = forward_group(x_ref, g * ROWS, twist_ref, fwd_ref, work.at[g])
        spec_ref[g] = spec
        mixed = (conj_product if conj else product)(filt_ref[g], spec)

        def store(s, h, value):
            outs[g, s, h : h + HALF] = value

        inverse_group(mixed, scale, twist_ref, inv_ref, work.at[g], store)
        for s in range(outs.shape[1]):
            out_ref[s // per, g * ROWS : (g + 1) * ROWS, s % per * LANES : (s % per + 1) * LANES] = outs[g, s].astype(
                out_ref.dtype
            )


def lags_kernel(scale, gate_ref, grad_ref, twist_ref, inv_ref, out_ref, work):
    for g in range(gate_ref.shape[0]):

        def store(s, h, value):
            out_ref[g * ROWS + h : g * ROWS + h + HALF, s * LANES : (s + 1) * LANES] = value

        inverse_group(conj_product(gate_ref[g], grad_ref[g]), scale, twist_ref, inv_ref, work.at[g], store)


def transforms(parts, chans, width):
    length = parts * width
    slabs = length // LANES
    groups = chans // ROWS
    per = 2 if groups % 2 == 0 else 1
    grid = (groups // per,)
    twist, fwd, inv = make_tables(length)
    scale = 1.0 / length
    x_spec = pl.BlockSpec((parts, per * ROWS, width), lambda i: (0, i, 0))
    s_spec = pl.BlockSpec((per, slabs * ROWS, 2 * LANES), lambda i: (i, 0, 0))
    l_spec = pl.BlockSpec((per * ROWS, length), lambda i: (i, 0))
    t_spec = pl.BlockSpec(twist.shape, lambda i: (0, 0, 0))
    m_spec = pl.BlockSpec(fwd.shape, lambda i: (0, 0, 0))
    s_shape = jax.ShapeDtypeStruct((groups, slabs * ROWS, 2 * LANES), jnp.float32)
    work = pltpu.VMEM((per, slabs * ROWS, 2 * LANES), jnp.float32)
    outs = pltpu.VMEM((per, slabs, ROWS, LANES), jnp.float32)
    params = pltpu.CompilerParams(vmem_limit_bytes=48 * 2**20)
    flops = 2 * 3 * groups * slabs * ROWS * 256 * 256
    cost = lambda n: pl.CostEstimate(flops=n * flops * 4, bytes_accessed=6 * 2**20, transcendentals=0)

    def spectrum(x):
        return pl.pallas_call(
            spectrum_kernel,
            grid=grid,
            in_specs=[x_spec, t_spec, m_spec],
            out_specs=s_spec,
            out_shape=s_shape,
            scratch_shapes=[work],
            compiler_params=params,
            cost_estimate=cost(1),
            name="spectrum",
        )(x, twist, fwd)

    def apply(x, filt, conj):
        return pl.pallas_call(
            lambda *refs: filter_kernel(conj, scale, *refs),
            grid=grid,
            in_specs=[x_spec, s_spec, t_spec, m_spec, m_spec],
            out_specs=(x_spec, s_spec),
            out_shape=(jax.ShapeDtypeStruct(x.shape, jnp.bfloat16), s_shape),
            scratch_shapes=[work, outs],
            compiler_params=params,
            cost_estimate=cost(2),
            name="correlate" if conj else "convolve",
        )(x, filt, twist, fwd, inv)

    def lags(gate, grad):
        return pl.pallas_call(
            lambda *refs: lags_kernel(scale, *refs),
            grid=grid,
            in_specs=[s_spec, s_spec, t_spec, m_spec],
            out_specs=l_spec,
            out_shape=jax.ShapeDtypeStruct((chans, length), jnp.float32),
            scratch_shapes=[work],
            compiler_params=params,
            cost_estimate=cost(1),
            name="lags",
        )(gate, grad, twist, inv)

    return spectrum, apply, lags


def exchange(value):
    return lax.all_to_all(value, "ctx", split_axis=0, concat_axis=0, tiled=True)


def scatter_sum(value):
    count = lax.axis_size("ctx")
    me = lax.axis_index("ctx")
    bit = 1
    while bit < count:
        pairs = value.reshape((value.shape[0] // 2, 2) + value.shape[1:])
        mine = me // bit % 2
        keep = lax.dynamic_index_in_dim(pairs, mine, 1, False)
        send = lax.dynamic_index_in_dim(pairs, 1 - mine, 1, False)
        value = keep + lax.ppermute(send, "ctx", [(i, i ^ bit) for i in range(count)])
        bit *= 2
    return value[0]


def local(x_first, x_second, x_value, short_filter, long_filter, skip_bias, norm_gain, cotangent):
    chans, steps_dev = x_first.shape
    n_ctx = lax.axis_size("ctx")
    n_ch = lax.axis_size("ch")
    width = chans * n_ch
    own = chans // n_ctx
    spectrum, apply, lags = transforms(n_ctx, own, steps_dev)
    f32 = lambda v: v.astype(jnp.float32)
    bf16 = lambda v: v.astype(jnp.bfloat16)
    by_dev = lambda v: v.reshape(n_ctx, own, steps_dev)
    by_pos = lambda v: v.reshape(chans, steps_dev)

    filter_cm = exchange(by_dev(long_filter))
    inputs = jnp.stack([x_first, x_second, x_value])
    before = shifted(inputs[:, :, steps_dev - 2 :], "ctx", 1)
    padded = f32(jnp.concatenate([before, inputs], axis=2))
    taps = short_filter[:, :, :, None]
    shorts = bf16(taps[:, 0] * padded[:, :, 2:] + taps[:, 1] * padded[:, :, 1:-1] + taps[:, 2] * padded[:, :, :-2])
    first_s, second_s, third_s = shorts[0], shorts[1], shorts[2]
    gated = bf16(f32(second_s) * f32(third_s))
    bias_col = skip_bias[:, None]
    gain_col = norm_gain[:, None]
    gated_cm = exchange(by_dev(gated))
    filt_spec = spectrum(filter_cm)
    conv_cm, gate_spec = apply(gated_cm, filt_spec, False)
    conv = by_pos(exchange(conv_cm))
    inner = f32(conv) + bias_col * f32(gated)
    mixed = f32(first_s) * inner
    scaled = f32(cotangent) * gain_col
    sums = jnp.stack([jnp.sum(mixed * mixed, axis=0), jnp.sum(scaled * mixed, axis=0)])
    total = sums
    for k in range(1, n_ch):
        total = total + lax.ppermute(sums, "ch", [(i, (i + k) % n_ch) for i in range(n_ch)])
    sum_sq, dotted = total[0], total[1]
    recip = lax.rsqrt(sum_sq / width + EPS)
    output = bf16(mixed * recip * gain_col)
    d_mixed = recip * scaled - mixed * recip**3 * (dotted / width)
    d_inner = bf16(d_mixed * f32(first_s))
    d_inner_cm = exchange(by_dev(d_inner))
    grad_first = bf16(d_mixed * inner)
    gain_part = jnp.sum(f32(cotangent) * mixed * recip, axis=1)
    bias_part = jnp.sum(f32(d_inner) * f32(gated), axis=1)
    back_cm, grad_spec = apply(d_inner_cm, filt_spec, True)
    back = by_pos(exchange(back_cm))
    d_long = lags(gate_spec, grad_spec)
    d_gated = bf16(bias_col * f32(d_inner) + f32(back))
    grad_second = bf16(f32(d_gated) * f32(third_s))
    grad_third = bf16(f32(d_gated) * f32(second_s))
    grads = jnp.stack([grad_first, grad_second, grad_third])
    after = shifted(grads[:, :, :2], "ctx", -1)
    grad_pad = f32(jnp.concatenate([grads, after], axis=2))
    d_inputs = bf16(
        taps[:, 0] * grad_pad[:, :, :-2] + taps[:, 1] * grad_pad[:, :, 1:-1] + taps[:, 2] * grad_pad[:, :, 2:]
    )
    grads_f = f32(grads)
    parts = [jnp.sum(grads_f * padded[:, :, 2 - k : 2 - k + steps_dev], axis=2) for k in range(3)]
    rows = jnp.concatenate([jnp.concatenate(parts, 0), bias_part[None], gain_part[None]], 0)
    rows = rows.reshape(11, n_ctx, own).transpose(1, 0, 2)
    done = scatter_sum(rows)
    d_short = done[:9].reshape(3, 3, own).transpose(1, 0, 2)
    return (output, d_inputs[0], d_inputs[1], d_inputs[2], d_long, d_short, done[9], done[10])


def solution(mesh):
    seq = P("ch", "ctx")
    own = ("ch", "ctx")
    return jax.shard_map(
        local,
        mesh=mesh,
        in_specs=(seq, seq, seq, P(None, None, "ch"), seq, P("ch"), P("ch"), seq),
        out_specs=(seq, seq, seq, seq, P(own, None), P(None, None, own), P(own), P(own)),
        check_vma=False,
    )
```

time: 356 us -> 156 us (0.44)
  matrix products: 142 us -> 0 us
  blocking collectives: 54.5 us -> 18.7 us
  waiting for transfers between devices: 67.3 us -> 46.2 us
  between operations: 15.6 us -> 1.06 us
  Pallas kernels: 0 us -> 14.5 us
  other arithmetic: 28.2 us -> 14 us
  starting transfers between devices: 22.6 us -> 31.3 us
  local copies, waits for them, and re-layouts: 21.5 us -> 28.9 us
    dot_general x42 -> x0, matrix products: 142 us -> none  [the longest x3 27 us: inverse_half(): jnp.einsum('kn,ckm->cnm', sin_a, imag_t, precision=HIGH)]
    unnamed x2 -> x0, waiting for transfers between devices: 59.1 us -> none
    all_to_all x4, waiting for transfers between devices: 8.25 us -> 41.7 us  [exchange(): return lax.all_to_all(value, 'ctx', split_axis=0, concat_axis=0, tiled=True)]
    unnamed x1 -> x0, blocking collectives: 22.5 us -> none
    pallas_call x0 -> x4, Pallas kernels: none -> 14.5 us  [the longest x2 9.28 us: apply(): pl.pallas_call(lambda *refs: filter_kernel(conj, scale, *refs), grid=grid...]
    psum x2 -> x0, blocking collectives: 12.3 us -> none  [local(): lax.psum((jnp.sum(mixed * mixed, axis=0), jnp.sum(scaled * mixed, axis=0)...]
    unnamed x52 -> x63, local copies, waits for them, and re-layouts: 9.98 us -> 21.5 us
    ppermute x0 -> x6, starting transfers between devices: none -> 9.02 us  [the longest x3 5.99 us: scatter_sum(): lax.ppermute(send, 'ctx', [(i, i ^ bit) for i in range(count)])]
  transfers between devices with their start and end apart: 7 -> 12, of which waited for: 2 -> 10; matrix products, arithmetic and copies ran while one was open for 17% -> 7% of each run, Pallas kernels for 0% -> 3%
where the time goes in v1:
time: 156 us; the launch traced here: 155 us
  waiting for transfers between devices  46.2 us (30%)
  starting transfers between devices  31.3 us (20%)
  local copies, waits for them, and re-layouts  28.9 us (19%)
  blocking collectives  18.7 us (12%)
  Pallas kernels  14.5 us (9%)
  other arithmetic  14 us (9%)
    all_to_all x4, waiting for transfers between devices, exchange(): return lax.all_to_all(value, 'ctx', split_axis=0, concat_axis=0, tiled=True)  41.7 us
    unnamed x63, local copies, waits for them, and re-layouts  21.5 us
    all_to_all x1, blocking collectives, exchange(): return lax.all_to_all(value, 'ctx', split_axis=0, concat_axis=0, tiled=True)  18.7 us
    all_to_all x4, starting transfers between devices, exchange(): return lax.all_to_all(value, 'ctx', split_axis=0, concat_axis=0, tiled=True)  15.9 us
    pallas_call x2, Pallas kernels, apply(): pl.pallas_call(lambda *refs: filter_kernel(conj, scale, *refs), grid=grid...  9.28 us
    ppermute x2, starting transfers between devices, shifted(): lax.ppermute(value, axis, [(source, source + steps) for source in range(f...  6.32 us
    ppermute x3, starting transfers between devices, scatter_sum(): lax.ppermute(send, 'ctx', [(i, i ^ bit) for i in range(count)])  5.99 us
    convert_element_type x2, local copies, waits for them, and re-layouts, local(): f32 = lambda v: v.astype(jnp.float32)  4.3 us
  transfers between devices with their start and end apart: 12, of which 10 were waited for; matrix products, arithmetic and copies ran while one was open for 7% of the time, Pallas kernels for 3%

profile of v1, /device:TPU:0, one launch (start us, length us, event | category | flops | bytes accessed | tf_op | source)
XLA Modules:
  0.0 154.7 jit_solution(14351627059094562718)
XLA Ops:
  4.4 4.8 %collective-permute-start = (bf16[3,1024,2]{1,2,0:T(2,128)(2,1)S(1)}, bf16[3,1024,2]{1,2,0:T(2,128)(2,1)S(1)}, u32[]{:S(2)}, u32[]{:S(2)}) collective-permute-start(bf16[3,1024,2]{1,2,0:T(2,128)(2,1)S(1)} %pad_maximum_fusion.1), channel_id=1, source_target_pairs={{0,4},{4,8},{8,12},{12,16},{16,20},{20,24},{24,28},{1,5},{5,9},{9,... | collective-permute-start | bytes 36872 | tf_op jit(solution)/shard_map/ppermute | solution.py:20
  9.3 4.9 %all-to-all-start.1 = ((bf16[8,128,256]{2,1,0:T(8,128)(2,1)}), bf16[8,128,256]{2,1,0:T(8,128)(2,1)S(1)}, u32[]{:S(2)}, u32[]{:S(2)}) async-start(bf16[8,128,256]{2,1,0:T(8,128)(2,1)} %bitcast.6), calls=%async_computation.1 | async-start | bytes 1048576 | tf_op jit(solution)/shard_map/all_to_all | solution.py:248
  17.7 10.7 %all-to-all-done.1.x_ref = bf16[8,128,256]{2,1,0:T(8,128)(2,1)S(1)} async-done(((bf16[8,128,256]{2,1,0:T(8,128)(2,1)}), bf16[8,128,256]{2,1,0:T(8,128)(2,1)S(1)}, u32[]{:S(2)}, u32[]{:S(2)}) %all-to-all-start.1) | async-done | bytes 524320 | tf_op jit(solution)/shard_map/all_to_all | solution.py:248
  28.4 3.6 %all-to-all-start = ((bf16[8,128,256]{2,1,0:T(8,128)(2,1)}), bf16[8,128,256]{2,1,0:T(8,128)(2,1)S(1)}, u32[]{:S(2)}, u32[]{:S(2)}) async-start(bf16[8,128,256]{2,1,0:T(8,128)(2,1)} %bitcast.116), calls=%async_computation | async-start | bytes 1048576 | tf_op jit(solution)/shard_map/all_to_all | solution.py:248
  32.1 2.2 %spectrum.1.refs_1_ = f32[8,256,256]{2,1,0:T(8,128)S(1)} custom-call(bf16[8,128,256]{2,1,0:T(8,128)(2,1)S(1)} %all-to-all-done.1.x_ref, f32[16,2,128]{2,1,0:T(2,128)S(1)} %copy-done.2, bf16[2,256,256]{2,1,0:T(8,128)(2,1)S(1)} %copy-done.1), custom_call_target="tpu_custom_call" | custom-call | flops 3221225472 | bytes 6291456 | tf_op jit(solution)/shard_map/spectrum/pallas_call | solution.py:206
  34.3 1.3 copy-done.7
  35.7 10.9 %all-to-all-done.refs_0_ = bf16[8,128,256]{2,1,0:T(8,128)(2,1)S(1)} async-done(((bf16[8,128,256]{2,1,0:T(8,128)(2,1)}), bf16[8,128,256]{2,1,0:T(8,128)(2,1)S(1)}, u32[]{:S(2)}, u32[]{:S(2)}) %all-to-all-start) | async-done | bytes 524320 | tf_op jit(solution)/shard_map/all_to_all | solution.py:248
  46.5 1.6 %copy-done.8 = f32[8,256,256]{2,1,0:T(8,128)S(1)} copy-done((f32[8,256,256]{2,1,0:T(8,128)S(1)}, f32[8,256,256]{2,1,0:T(8,128)}, u32[]{:S(2)}) %copy-start.8) | copy-done | bytes 2097176
  48.1 4.6 %convolve.1 = (bf16[8,128,256]{2,1,0:T(8,128)(2,1)}, f32[8,256,256]{2,1,0:T(8,128)S(1)}) custom-call(bf16[8,128,256]{2,1,0:T(8,128)(2,1)S(1)} %all-to-all-done.refs_0_, f32[8,256,256]{2,1,0:T(8,128)S(1)} %copy-done.8, f32[16,2,128]{2,1,0:T(2,128)S(1)} %copy-done.2, bf16[2,256,256]{2,1,0:T(8,128)(2,1)S(1)} %copy-done.1, bf16[2,256,256]{2,1,0:T(8,128)(2,1)S(1)} %copy-done), custom_call_target="tpu_custom_call" | custom-call | flops 6442450944 | bytes 6291456 | tf_op jit(solution)/shard_map/convolve/pallas_call | solution.py:219
  52.8 1.3 copy-done.3
  54.1 3.8 %all-to-all-start.2 = ((bf16[8,128,256]{2,1,0:T(8,128)(2,1)}), bf16[8,128,256]{2,1,0:T(8,128)(2,1)S(1)}, u32[]{:S(2)}, u32[]{:S(2)}) async-start(bf16[8,128,256]{2,1,0:T(8,128)(2,1)} %get-tuple-element.12), calls=%async_computation.2 | async-start | bytes 1048576 | tf_op jit(solution)/shard_map/all_to_all | solution.py:248
  57.9 2.0 %copy.26 = bf16[1024,256]{0,1:T(8,128)(2,1)} copy(bf16[1024,256]{1,0:T(8,128)(2,1)} %param.18) | data formatting | bytes 1048576 | tf_op args[7]
  59.9 12.6 %all-to-all-done.2 = bf16[8,128,256]{2,1,0:T(8,128)(2,1)S(1)} async-done(((bf16[8,128,256]{2,1,0:T(8,128)(2,1)}), bf16[8,128,256]{2,1,0:T(8,128)(2,1)S(1)}, u32[]{:S(2)}, u32[]{:S(2)}) %all-to-all-start.2) | async-done | bytes 524320 | tf_op jit(solution)/shard_map/all_to_all | solution.py:248
  73.6 1.6 %copy.25 = f32[1024,256]{0,1:T(8,128)S(1)} copy(f32[1024,256]{1,0:T(8,128)} %bitcast_convert_fusion.1) | data formatting | bytes 2097152 | tf_op jit(solution)/shard_map/convert_element_type | solution.py:272
  75.2 1.6 %multiply_reduce_fusion = (f32[256]{0:T(256)S(1)}, f32[256]{0:T(256)S(1)}, f32[1024,256]{0,1:T(8,128)S(1)}) fusion(f32[1024]{0:T(1024)S(1)} %copy-done.23, bf16[1024,256]{0,1:T(8,128)(2,1)} %copy.26, f32[1024,256]{0,1:T(8,128)S(1)} %copy.25, bf16[3,1024,256]{1,2,0:T(8,128)(2,1)S(1)} %add_convert_fusion, f32[1024]{0:T(1024)S(1)} %copy-done.18), kind=kLoop, calls=%fused_computation.46 | loop fusion | flops 3931648 | bytes 4204544 | tf_op jit(solution)/shard_map/reduce_sum | solution.py:294
  76.9 1.6 %collective-permute-start.2 = (f32[2,256]{1,0:T(2,128)S(1)}, f32[2,256]{1,0:T(2,128)S(1)}, u32[]{:S(2)}, u32[]{:S(2)}) collective-permute-start(f32[2,256]{1,0:T(2,128)S(1)} %pad_maximum_fusion.3), channel_id=1, source_target_pairs={{0,2},{1,3},{2,0},{3,1},{4,6},{5,7},{6,4},{7,5},{8,10},{9,11},{10,... | collective-permute-start | bytes 6152 | tf_op jit(solution)/shard_map/ppermute | solution.py:297
  78.5 1.4 collective-permute-start.3
  81.3 2.6 %fusion.18 = (f32[1024]{0:T(1024)}, bf16[1024,256]{0,1:T(8,128)(2,1)}, bf16[1,1024,256]{1,2,0:T(8,128)(2,1)}, f32[1024]{0:T(1024)}, bf16[1024,256]{0,1:T(8,128)(2,1)}) fusion(bf16[3,1024,256]{1,2,0:T(8,128)(2,1)S(1)} %add_convert_fusion, f32[256]{0:T(256)S(1)} %bitcast.137, f32[1024,256]{0,1:T(8,128)S(1)} %get-tuple-element.51, f32[256]{0:T(256)S(1)} %bitcast.135, ...), kind=kLoop, calls=%fused_computation.40 | loop fusion | flops 7075840 | bytes 5786624 | tf_op jit(solution)/shard_map/reduce_sum | solution.py:306
  85.1 18.7 %all_to_all.25.refs_0_ = bf16[8,128,256]{2,1,0:T(8,128)(2,1)S(1)} all-to-all(bf16[8,128,256]{2,1,0:T(8,128)(2,1)S(1)} %bitcast.117), channel_id=1, replica_groups=mesh['ctx'=8,'ch'=4] {'ctx'}, dimensions={0} | all-to-all | bytes 1048576 | tf_op jit(solution)/shard_map/all_to_all | solution.py:248
  103.8 1.6 %copy-done.9 = f32[8,256,256]{2,1,0:T(8,128)S(1)} copy-done((f32[8,256,256]{2,1,0:T(8,128)S(1)}, f32[8,256,256]{2,1,0:T(8,128)}, u32[]{:S(2)}) %copy-start.9) | copy-done | bytes 2097176
  105.4 4.6 %correlate.1 = (bf16[8,128,256]{2,1,0:T(8,128)(2,1)}, f32[8,256,256]{2,1,0:T(8,128)S(1)}) custom-call(bf16[8,128,256]{2,1,0:T(8,128)(2,1)S(1)} %all_to_all.25.refs_0_, f32[8,256,256]{2,1,0:T(8,128)S(1)} %copy-done.9, f32[16,2,128]{2,1,0:T(2,128)S(1)} %copy-done.2, bf16[2,256,256]{2,1,0:T(8,128)(2,1)S(1)} %copy-done.1, bf16[2,256,256]{2,1,0:T(8,128)(2,1)S(1)} %copy-done), custom_call_target="tpu_custom_call" | custom-call | flops 6442450944 | bytes 6291456 | tf_op jit(solution)/shard_map/correlate/pallas_call | solution.py:219
  110.0 1.3 copy-done.5
  111.4 3.6 %all-to-all-start.4 = ((bf16[8,128,256]{2,1,0:T(8,128)(2,1)}), bf16[8,128,256]{2,1,0:T(8,128)(2,1)S(1)}, u32[]{:S(2)}, u32[]{:S(2)}) async-start(bf16[8,128,256]{2,1,0:T(8,128)(2,1)} %get-tuple-element.13), calls=%async_computation.4 | async-start | bytes 1048576 | tf_op jit(solution)/shard_map/all_to_all | solution.py:248
  116.0 1.6 %copy-done.4 = f32[8,256,256]{2,1,0:T(8,128)S(1)} copy-done((f32[8,256,256]{2,1,0:T(8,128)S(1)}, f32[8,256,256]{2,1,0:T(8,128)}, u32[]{:S(2)}) %copy-start.4) | copy-done | bytes 2097176
  117.6 1.6 %copy-done.6 = f32[8,256,256]{2,1,0:T(8,128)S(1)} copy-done((f32[8,256,256]{2,1,0:T(8,128)S(1)}, f32[8,256,256]{2,1,0:T(8,128)}, u32[]{:S(2)}) %copy-start.6) | copy-done | bytes 2097176
  119.2 3.0 %lags.1 = f32[128,2048]{1,0:T(8,128)} custom-call(f32[8,256,256]{2,1,0:T(8,128)S(1)} %copy-done.4, f32[8,256,256]{2,1,0:T(8,128)S(1)} %copy-done.6, f32[16,2,128]{2,1,0:T(2,128)S(1)} %copy-done.2, bf16[2,256,256]{2,1,0:T(8,128)(2,1)S(1)} %copy-done), custom_call_target="tpu_custom_call" | custom-call | flops 3221225472 | bytes 6291456 | tf_op jit(solution)/shard_map/lags/pallas_call | solution.py:232
  122.2 7.5 %all-to-all-done.4 = bf16[8,128,256]{2,1,0:T(8,128)(2,1)S(1)} async-done(((bf16[8,128,256]{2,1,0:T(8,128)(2,1)}), bf16[8,128,256]{2,1,0:T(8,128)(2,1)S(1)}, u32[]{:S(2)}, u32[]{:S(2)}) %all-to-all-start.4) | async-done | bytes 524320 | tf_op jit(solution)/shard_map/all_to_all | solution.py:248
  130.8 2.7 %copy.28 = f32[1024,256]{0,1:T(8,128)} copy(f32[1024,256]{1,0:T(8,128)} %bitcast_convert_fusion) | data formatting | bytes 2097152 | tf_op jit(solution)/shard_map/convert_element_type | solution.py:272
  133.5 1.8 %fusion.24 = (bf16[1,1024,256]{1,2,0:T(8,128)(2,1)S(1)}, bf16[1024,256]{0,1:T(8,128)(2,1)S(1)}) fusion(bf16[3,1024,256]{1,2,0:T(8,128)(2,1)} %copy-done.12, f32[1024,256]{0,1:T(8,128)} %copy.28, bf16[1024,256]{0,1:T(8,128)(2,1)} %get-tuple-element.46, f32[1024]{0:T(1024)S(1)} %copy-done.19), kind=kLoop, calls=%fused_computation.49 | loop fusion | flops 2097152 | bytes 3149824 | tf_op jit(solution)/shard_map/stack | solution.py:313
  138.1 1.5 collective-permute-start.4
  139.7 2.7 %collective-permute-start.5 = (f32[4,11,128]{2,0,1:T(4,128)S(1)}, f32[4,11,128]{2,0,1:T(4,128)S(1)}, u32[]{:S(2)}, u32[]{:S(2)}) collective-permute-start(f32[4,11,128]{2,0,1:T(4,128)S(1)} %bitcast.129), channel_id=1, source_target_pairs={{0,4},{4,0},{8,12},{12,8},{16,20},{20,16},{24,28},{28,24},{1,5},{5... | collective-permute-start | bytes 67592 | tf_op jit(solution)/shard_map/ppermute | solution.py:260
  144.3 3.0 %collective-permute-start.6 = (f32[2,11,128]{2,0,1:T(2,128)S(1)}, f32[2,11,128]{2,0,1:T(2,128)S(1)}, u32[]{:S(2)}, u32[]{:S(2)}) collective-permute-start(f32[2,11,128]{2,0,1:T(2,128)S(1)} %bitcast.130), channel_id=1, source_target_pairs={{0,8},{4,12},{8,0},{12,4},{16,24},{20,28},{24,16},{28,20},{1,9},{5... | collective-permute-start | bytes 33800 | tf_op jit(solution)/shard_map/ppermute | solution.py:260
  (94 shorter events, 25.1 us)
Async XLA Ops:
  0.6 13.6 %copy-start.20 = (f32[3,3,1024]{2,1,0:T(4,128)S(1)}, f32[3,3,1024]{2,1,0:T(4,128)}, u32[]{:S(2)}) copy-start(f32[3,3,1024]{2,1,0:T(4,128)} %param.14) | copy-start | bytes 110596
  4.4 9.8 %collective-permute-start = (bf16[3,1024,2]{1,2,0:T(2,128)(2,1)S(1)}, bf16[3,1024,2]{1,2,0:T(2,128)(2,1)S(1)}, u32[]{:S(2)}, u32[]{:S(2)}) collective-permute-start(bf16[3,1024,2]{1,2,0:T(2,128)(2,1)S(1)} %pad_maximum_fusion.1), channel_id=1, source_target_pairs={{0,4},{4,8},{8,12},{12,16},{16,20},{20,24},{24,28},{1,5},{5,9},{9,... | collective-permute-start | bytes 36872 | tf_op jit(solution)/shard_map/ppermute | solution.py:20
  9.3 19.1 %all-to-all-start.1 = ((bf16[8,128,256]{2,1,0:T(8,128)(2,1)}), bf16[8,128,256]{2,1,0:T(8,128)(2,1)S(1)}, u32[]{:S(2)}, u32[]{:S(2)}) async-start(bf16[8,128,256]{2,1,0:T(8,128)(2,1)} %bitcast.6), calls=%async_computation.1 | async-start | bytes 1048576 | tf_op jit(solution)/shard_map/all_to_all | solution.py:248
  14.8 1.7 %copy-start.10 = (f32[3,1024,258]{1,2,0:T(8,128)}, f32[3,1024,258]{1,2,0:T(8,128)S(1)}, u32[]{:S(2)}) copy-start(f32[3,1024,258]{1,2,0:T(8,128)S(1)} %maximum_convert_fusion) | copy-start | bytes 9510916
  16.4 64.9 %copy-start.12 = (bf16[3,1024,256]{1,2,0:T(8,128)(2,1)}, bf16[3,1024,256]{1,2,0:T(8,128)(2,1)S(1)}, u32[]{:S(2)}) copy-start(bf16[3,1024,256]{1,2,0:T(8,128)(2,1)S(1)} %add_convert_fusion) | copy-start | bytes 4718596
  16.4 15.7 %copy-start.1 = (bf16[2,256,256]{2,1,0:T(8,128)(2,1)S(1)}, bf16[2,256,256]{2,1,0:T(8,128)(2,1)}, u32[]{:S(2)}) copy-start(bf16[2,256,256]{2,1,0:T(8,128)(2,1)} %constant.93.clone.mat_ref.refs_3_) | copy-start | bytes 786436
  16.4 15.7 %copy-start.2 = (f32[16,2,128]{2,1,0:T(2,128)S(1)}, f32[16,2,128]{2,1,0:T(2,128)}, u32[]{:S(2)}) copy-start(f32[16,2,128]{2,1,0:T(2,128)} %constant.92.clone.twist_ref.refs_2_) | copy-start | bytes 49156
  28.4 18.1 %all-to-all-start = ((bf16[8,128,256]{2,1,0:T(8,128)(2,1)}), bf16[8,128,256]{2,1,0:T(8,128)(2,1)S(1)}, u32[]{:S(2)}, u32[]{:S(2)}) async-start(bf16[8,128,256]{2,1,0:T(8,128)(2,1)} %bitcast.116), calls=%async_computation | async-start | bytes 1048576 | tf_op jit(solution)/shard_map/all_to_all | solution.py:248
  32.1 14.5 %copy-start = (bf16[2,256,256]{2,1,0:T(8,128)(2,1)S(1)}, bf16[2,256,256]{2,1,0:T(8,128)(2,1)}, u32[]{:S(2)}) copy-start(bf16[2,256,256]{2,1,0:T(8,128)(2,1)} %constant.94.clone.refs_4_.refs_3_) | copy-start | bytes 786436
  46.5 1.6 %copy-start.8 = (f32[8,256,256]{2,1,0:T(8,128)S(1)}, f32[8,256,256]{2,1,0:T(8,128)}, u32[]{:S(2)}) copy-start(f32[8,256,256]{2,1,0:T(8,128)} %copy-done.7) | copy-start | bytes 6291460
  54.1 21.1 %copy-start.18 = (f32[1024]{0:T(1024)S(1)}, f32[1024]{0:T(1024)}, u32[]{:S(2)}) copy-start(f32[1024]{0:T(1024)} %param.16) | copy-start | bytes 12292
  54.1 21.1 %copy-start.23 = (f32[1024]{0:T(1024)S(1)}, f32[1024]{0:T(1024)}, u32[]{:S(2)}) copy-start(f32[1024]{0:T(1024)} %param.17) | copy-start | bytes 12292
  54.1 18.4 %all-to-all-start.2 = ((bf16[8,128,256]{2,1,0:T(8,128)(2,1)}), bf16[8,128,256]{2,1,0:T(8,128)(2,1)S(1)}, u32[]{:S(2)}, u32[]{:S(2)}) async-start(bf16[8,128,256]{2,1,0:T(8,128)(2,1)} %get-tuple-element.12), calls=%async_computation.2 | async-start | bytes 1048576 | tf_op jit(solution)/shard_map/all_to_all | solution.py:248
  75.2 6.1 %copy-start.14 = (bf16[1024,256]{0,1:T(8,128)(2,1)S(1)}, bf16[1024,256]{0,1:T(8,128)(2,1)}, u32[]{:S(2)}) copy-start(bf16[1024,256]{0,1:T(8,128)(2,1)} %copy.26) | copy-start | bytes 1572868
  76.9 3.1 %collective-permute-start.1 = (f32[2,256]{1,0:T(2,128)S(1)}, f32[2,256]{1,0:T(2,128)S(1)}, u32[]{:S(2)}, u32[]{:S(2)}) collective-permute-start(f32[2,256]{1,0:T(2,128)S(1)} %pad_maximum_fusion.3), channel_id=1, source_target_pairs={{0,1},{1,2},{2,3},{3,0},{4,5},{5,6},{6,7},{7,4},{8,9},{9,10},{10,1... | collective-permute-start | bytes 6152 | tf_op jit(solution)/shard_map/ppermute | solution.py:297
  76.9 3.7 %collective-permute-start.2 = (f32[2,256]{1,0:T(2,128)S(1)}, f32[2,256]{1,0:T(2,128)S(1)}, u32[]{:S(2)}, u32[]{:S(2)}) collective-permute-start(f32[2,256]{1,0:T(2,128)S(1)} %pad_maximum_fusion.3), channel_id=1, source_target_pairs={{0,2},{1,3},{2,0},{3,1},{4,6},{5,7},{6,4},{7,5},{8,10},{9,11},{10,... | collective-permute-start | bytes 6152 | tf_op jit(solution)/shard_map/ppermute | solution.py:297
  78.5 2.7 %collective-permute-start.3 = (f32[2,256]{1,0:T(2,128)S(1)}, f32[2,256]{1,0:T(2,128)S(1)}, u32[]{:S(2)}, u32[]{:S(2)}) collective-permute-start(f32[2,256]{1,0:T(2,128)S(1)} %pad_maximum_fusion.3), channel_id=1, source_target_pairs={{0,3},{1,0},{2,1},{3,2},{4,7},{5,4},{6,5},{7,6},{8,11},{9,8},{10,9... | collective-permute-start | bytes 6152 | tf_op jit(solution)/shard_map/ppermute | solution.py:297
  103.8 1.6 %copy-start.9 = (f32[8,256,256]{2,1,0:T(8,128)S(1)}, f32[8,256,256]{2,1,0:T(8,128)}, u32[]{:S(2)}) copy-start(f32[8,256,256]{2,1,0:T(8,128)} %copy-done.7) | copy-start | bytes 6291460
  105.4 9.6 %copy-start.15 = (bf16[1024,256]{0,1:T(8,128)(2,1)S(1)}, bf16[1024,256]{0,1:T(8,128)(2,1)}, u32[]{:S(2)}) copy-start(bf16[1024,256]{0,1:T(8,128)(2,1)} %get-tuple-element.57) | copy-start | bytes 1572868
  111.4 18.3 %all-to-all-start.4 = ((bf16[8,128,256]{2,1,0:T(8,128)(2,1)}), bf16[8,128,256]{2,1,0:T(8,128)(2,1)S(1)}, u32[]{:S(2)}, u32[]{:S(2)}) async-start(bf16[8,128,256]{2,1,0:T(8,128)(2,1)} %get-tuple-element.13), calls=%async_computation.4 | async-start | bytes 1048576 | tf_op jit(solution)/shard_map/all_to_all | solution.py:248
  116.0 1.6 %copy-start.4 = (f32[8,256,256]{2,1,0:T(8,128)S(1)}, f32[8,256,256]{2,1,0:T(8,128)}, u32[]{:S(2)}) copy-start(f32[8,256,256]{2,1,0:T(8,128)} %copy-done.3) | copy-start | bytes 6291460
  117.6 1.6 %copy-start.6 = (f32[8,256,256]{2,1,0:T(8,128)S(1)}, f32[8,256,256]{2,1,0:T(8,128)}, u32[]{:S(2)}) copy-start(f32[8,256,256]{2,1,0:T(8,128)} %copy-done.5) | copy-start | bytes 6291460
  122.2 11.4 %copy-start.19 = (f32[1024]{0:T(1024)S(1)}, f32[1024]{0:T(1024)}, u32[]{:S(2)}) copy-start(f32[1024]{0:T(1024)} %param.16) | copy-start | bytes 12292
  130.8 5.8 %copy-start.11 = (f32[3,1024,258]{1,2,0:T(8,128)S(1)}, f32[3,1024,258]{1,2,0:T(8,128)}, u32[]{:S(2)}) copy-start(f32[3,1024,258]{1,2,0:T(8,128)} %copy-done.10) | copy-start | bytes 9510916
  133.5 3.1 %copy-start.13 = (bf16[1,1024,256]{1,2,0:T(8,128)(2,1)S(1)}, bf16[1,1024,256]{1,2,0:T(8,128)(2,1)}, u32[]{:S(2)}) copy-start(bf16[1,1024,256]{1,2,0:T(8,128)(2,1)} %get-tuple-element.52) | copy-start | bytes 1572868
  137.9 1.7 %copy-start.22 = (f32[1024]{0:T(1024)S(1)}, f32[1024]{0:T(1024)}, u32[]{:S(2)}) copy-start(f32[1024]{0:T(1024)} %get-tuple-element.45) | copy-start | bytes 12292
  137.9 1.8 %copy-start.21 = (f32[1024]{0:T(1024)S(1)}, f32[1024]{0:T(1024)}, u32[]{:S(2)}) copy-start(f32[1024]{0:T(1024)} %get-tuple-element.53) | copy-start | bytes 12292
  138.1 9.2 %copy-start.17 = (f32[3,1,1024,1]{2,0,1,3:T(4,128)S(1)}, f32[3,1,1024,1]{2,0,1,3:T(4,128)}, u32[]{:S(2)}) copy-start(f32[3,1,1024,1]{2,0,1,3:T(4,128)} %copy-done.16) | copy-start | bytes 36868
  138.1 5.6 %collective-permute-start.4 = (bf16[3,1024,2]{1,2,0:T(2,128)(2,1)S(1)}, bf16[3,1024,2]{1,2,0:T(2,128)(2,1)S(1)}, u32[]{:S(2)}, u32[]{:S(2)}) collective-permute-start(bf16[3,1024,2]{1,2,0:T(2,128)(2,1)S(1)} %slice.108), channel_id=1, source_target_pairs={{4,0},{8,4},{12,8},{16,12},{20,16},{24,20},{28,24},{5,1},{9,5},{13... | collective-permute-start | bytes 36872 | tf_op jit(solution)/shard_map/ppermute | solution.py:20
  139.7 4.5 %collective-permute-start.5 = (f32[4,11,128]{2,0,1:T(4,128)S(1)}, f32[4,11,128]{2,0,1:T(4,128)S(1)}, u32[]{:S(2)}, u32[]{:S(2)}) collective-permute-start(f32[4,11,128]{2,0,1:T(4,128)S(1)} %bitcast.129), channel_id=1, source_target_pairs={{0,4},{4,0},{8,12},{12,8},{16,20},{20,16},{24,28},{28,24},{1,5},{5... | collective-permute-start | bytes 67592 | tf_op jit(solution)/shard_map/ppermute | solution.py:260
  144.3 4.6 %collective-permute-start.6 = (f32[2,11,128]{2,0,1:T(2,128)S(1)}, f32[2,11,128]{2,0,1:T(2,128)S(1)}, u32[]{:S(2)}, u32[]{:S(2)}) collective-permute-start(f32[2,11,128]{2,0,1:T(2,128)S(1)} %bitcast.130), channel_id=1, source_target_pairs={{0,8},{4,12},{8,0},{12,4},{16,24},{20,28},{24,16},{28,20},{1,9},{5... | collective-permute-start | bytes 33800 | tf_op jit(solution)/shard_map/ppermute | solution.py:260
  148.9 4.6 %collective-permute-start.7 = (f32[1,11,128]{2,0,1:T(1,128)S(1)}, f32[1,11,128]{2,0,1:T(1,128)S(1)}, u32[]{:S(2)}, u32[]{:S(2)}) collective-permute-start(f32[1,11,128]{2,0,1:T(1,128)S(1)} %constant_dynamic-slice_fusion), channel_id=1, source_target_pairs={{0,16},{4,20},{8,24},{12,28},{16,0},{20,4},{24,8},{28,12},{1,17},{... | collective-permute-start | bytes 16904 | tf_op jit(solution)/shard_map/ppermute | solution.py:260
  (4 other events, 4.6 us)

commit v2 on v1

v2 whole, which is shorter than its diff:
```python
import math

import jax
import jax.numpy as jnp
import numpy as np
from jax import lax
from jax.experimental import pallas as pl
from jax.experimental.pallas import tpu as pltpu
from jax.sharding import PartitionSpec as P

EPS = 1e-06
LANES = 128
ROWS = 16
HALF = 8
VMEM_MOST = 24 * 2**20
VMEM_ALL = 60 * 2**20
PARTS = 4


def f32(value):
    return value.astype(jnp.float32)


def bf16(value):
    return value.astype(jnp.bfloat16)


def shifted(value, axis, steps):
    count = lax.axis_size(axis)
    first, last = (max(0, -steps), min(count, count - steps))
    return lax.ppermute(value, axis, [(source, source + steps) for source in range(first, last)])


def root(angle):
    return math.cos(2 * math.pi * angle), math.sin(2 * math.pi * angle)


def slab_angles(slabs):
    angles = [-0.25]
    while len(angles) < slabs:
        angles = [a / 2 + extra for a in angles for extra in (0.0, 0.5)]
    return angles


def split_angles(slabs):
    levels, angles = [], [-0.25]
    while len(angles) < slabs:
        levels.append([a / 2 for a in angles])
        angles = [a / 2 + extra for a in angles for extra in (0.0, 0.5)]
    return levels


def slabs_forward(xs):
    slabs = len(xs)
    data = None
    for level, turns in enumerate(split_angles(slabs)):
        size = slabs >> level
        half = size // 2
        new = [None] * slabs
        for b, turn in enumerate(turns):
            c, s = root(turn)
            for n in range(half):
                lo, hi = b * size + n, b * size + n + half
                if data is None:
                    tr, ti = xs[hi] * c, xs[hi] * s
                    new[lo] = (xs[lo] + tr, ti)
                    new[hi] = (xs[lo] - tr, -ti)
                else:
                    (ar, ai), (br, bi) = data[lo], data[hi]
                    tr, ti = br * c - bi * s, br * s + bi * c
                    new[lo] = (ar + tr, ai + ti)
                    new[hi] = (ar - tr, ai - ti)
        data = new
    return data


def slabs_inverse(data):
    slabs = len(data)
    levels = split_angles(slabs)
    for level in range(len(levels) - 1, -1, -1):
        size = slabs >> level
        half = size // 2
        new = [None] * slabs
        for b, turn in enumerate(levels[level]):
            c, s = root(turn)
            for n in range(half):
                lo, hi = b * size + n, b * size + n + half
                (ur, ui), (vr, vi) = data[lo], data[hi]
                dr, di = ur - vr, ui - vi
                if level == 0:
                    new[lo] = ur + vr
                    new[hi] = dr * c + di * s
                else:
                    new[lo] = (ur + vr, ui + vi)
                    new[hi] = (dr * c + di * s, di * c - dr * s)
        data = new
    return data


def make_tables(length):
    slabs = length // LANES
    angle = np.array(slab_angles(slabs))[:, None] * np.arange(LANES)[None, :] / LANES
    twist = np.stack([np.cos(2 * np.pi * angle), np.sin(2 * np.pi * angle)], 1).astype(np.float32)
    grid = np.arange(LANES)[:, None] * np.arange(LANES)[None, :] % LANES * (2 * np.pi / LANES)
    cos, sin = np.cos(grid), np.sin(grid)
    fwd = np.block([[cos, -sin], [sin, cos]]).astype(np.float32)
    inv = np.block([[cos, sin], [-sin, cos]]).astype(np.float32)

    def two(mat):
        upper = mat.astype(jnp.bfloat16)
        lower = (mat - upper.astype(np.float32)).astype(jnp.bfloat16)
        return np.stack([upper, lower])

    return jnp.asarray(np.stack([twist, twist / length])), jnp.asarray(two(fwd)), jnp.asarray(two(inv))


def split_dot(value, mat_ref):
    upper = value.astype(jnp.bfloat16)
    lower = (value - upper.astype(jnp.float32)).astype(jnp.bfloat16)
    dot = lambda a, b: jnp.dot(a, b, preferred_element_type=jnp.float32)
    return dot(upper, mat_ref[0]) + (dot(lower, mat_ref[0]) + dot(upper, mat_ref[1]))


def forward_group(x_ref, row, twist_ref, mat_ref, work):
    parts, _, width = x_ref.shape
    per = width // LANES
    slabs = parts * per
    xs = [f32(x_ref[s // per, pl.ds(row, ROWS), s % per * LANES : (s % per + 1) * LANES]) for s in range(slabs)]
    for h in range(0, ROWS, HALF):
        data = slabs_forward([x[h : h + HALF] for x in xs])
        for j, (re, im) in enumerate(data):
            tc, ts = twist_ref[j, 0:1], twist_ref[j, 1:2]
            work[j * ROWS + h : j * ROWS + h + HALF, :LANES] = re * tc - im * ts
            work[j * ROWS + h : j * ROWS + h + HALF, LANES:] = re * ts + im * tc
    return split_dot(work[...], mat_ref)


def inverse_group(spec, twist_ref, mat_ref, work, store):
    slabs = spec.shape[0] // ROWS
    work[...] = split_dot(spec, mat_ref)
    for h in range(0, ROWS, HALF):
        data = []
        for j in range(slabs):
            tc, ts = twist_ref[j, 0:1], twist_ref[j, 1:2]
            re = work[j * ROWS + h : j * ROWS + h + HALF, :LANES]
            im = work[j * ROWS + h : j * ROWS + h + HALF, LANES:]
            data.append((re * tc + im * ts, im * tc - re * ts))
        for s, value in enumerate(slabs_inverse(data)):
            store(s, h, value)


def product(a, b):
    ar, ai, br, bi = a[:, :LANES], a[:, LANES:], b[:, :LANES], b[:, LANES:]
    return jnp.concatenate([ar * br - ai * bi, ar * bi + ai * br], 1)


def conj_product(a, b):
    ar, ai, br, bi = a[:, :LANES], a[:, LANES:], b[:, :LANES], b[:, LANES:]
    return jnp.concatenate([ar * br + ai * bi, ar * bi - ai * br], 1)


def spectrum_pair(filt_ref, gate_ref, row, twist_ref, fwd_ref, work):
    one = forward_group(filt_ref, row, twist_ref.at[0], fwd_ref, work.at[0])
    return one, forward_group(gate_ref, row, twist_ref.at[0], fwd_ref, work.at[1])


def put_slabs(out_ref, row, slabs_ref):
    per = out_ref.shape[2] // LANES
    for s in range(slabs_ref.shape[0]):
        lanes = slice(s % per * LANES, (s % per + 1) * LANES)
        out_ref[s // per, pl.ds(row, ROWS), lanes] = bf16(slabs_ref[s])


def storing(slabs_ref):
    def store(s, h, value):
        slabs_ref[s, h : h + HALF] = value

    return store


def over_groups(count, per, body, done):
    def step(i, carry):
        for g in range(per):
            body(g, pl.multiple_of((i * per + g) * ROWS, ROWS))
        done(i)
        return carry

    lax.fori_loop(0, count // per, step, 0)


def column(cols_ref, rows, k):
    return cols_ref[rows, k : k + 1]


def tap(cols_ref, rows, branch, k):
    return column(cols_ref, rows, 3 * branch + k)


BIAS, GAIN = 9, 10


def after_wrap(now, before, steps):
    lanes = lax.broadcasted_iota(jnp.int32, now.shape, 1)
    return jnp.where(lanes < steps, before, now)


def short_slabs(x_ref, row, taps):
    parts, _, width = x_ref.shape
    per = width // LANES
    result, last = [], [0.0, 0.0]
    for s in range(parts * per):
        x = f32(x_ref[s // per, pl.ds(row, ROWS), s % per * LANES : (s % per + 1) * LANES])
        moved = [pltpu.roll(x, k, 1) for k in (1, 2)]
        one, two = (after_wrap(moved[k], last[k], k + 1) for k in range(2))
        result.append(bf16(taps[0] * x + taps[1] * one + taps[2] * two))
        last = moved
    return result


def convolve_kernel(pack_ref, cols_ref, twist_ref, fwd_ref, inv_ref, out_ref, spec_ref, gate_ref, token_ref, work, slabs, sent):
    chans = out_ref.shape[1]
    per = out_ref.shape[2] // LANES
    filt_ref, x1_ref, x2_ref = (pack_ref.at[:, k * chans : (k + 1) * chans] for k in range(3))

    def body(g, row):
        rows = pl.ds(row, ROWS)
        s1, s2 = (
            short_slabs(ref, row, [tap(cols_ref, rows, b, k) for k in range(3)]) for b, ref in ((1, x1_ref), (2, x2_ref))
        )
        for s, (one, two) in enumerate(zip(s1, s2)):
            gate_ref[s // per, rows, s % per * LANES : (s % per + 1) * LANES] = bf16(f32(one) * f32(two))
        filt, gate = spectrum_pair(filt_ref, gate_ref, row, twist_ref, fwd_ref, work.at[g])
        spec_ref[row // ROWS] = filt
        inverse_group(product(filt, gate), twist_ref.at[1], inv_ref, work.at[g, 0], storing(slabs.at[g]))
        put_slabs(out_ref, row, slabs.at[g])

    over_groups(chans // ROWS, work.shape[0], body, sent)
    token_ref[...] = jnp.zeros_like(token_ref)


def correlate_kernel(grad_ref, spec_ref, early_ref, twist_ref, fwd_ref, inv_ref, out_ref, work, slabs, sent):
    parts, chans, width = grad_ref.shape
    groups, per = chans // ROWS, work.shape[0]

    def body(g, row):
        grad = forward_group(grad_ref, row, twist_ref.at[0], fwd_ref, work.at[g, 0])
        mixed = conj_product(spec_ref[row // ROWS], grad)
        inverse_group(mixed, twist_ref.at[1], inv_ref, work.at[g, 0], storing(slabs.at[g]))
        put_slabs(out_ref, row, slabs.at[g])

    def done(i):
        for g in range(per):
            sent(i * per + g)

    over_groups(groups, per, body, done)
    for part in range(parts):
        sums = early_ref[:4, part * chans : (part + 1) * chans]
        upper = f32(bf16(sums))
        if part + 1 < parts:
            tips = to_rows([(0, 0), (1, 1), (2, 0), (3, 1)], out_ref[part + 1, :chans, :LANES])[:4]
        else:
            tips = jnp.zeros((4, chans), jnp.float32)
        rows = jnp.concatenate([tips, upper, sums - upper, jnp.zeros((4, chans), jnp.float32)], 0)
        rows = jnp.concatenate([rows, jnp.zeros((ROWS, width - chans), jnp.float32)], 1)
        out_ref[part, chans:] = bf16(rows)
    sent(groups)


def grads_kernel(back_ref, inner_ref, pack_ref, gate_ref, cols_ref, rows_ref, tiles, sent):
    parts, chans, _ = inner_ref.shape
    block = min(32, chans)
    for row in range(0, chans, block):
        rows = slice(row, row + block)
        taps = [[tap(cols_ref, rows, b, k) for k in range(3)] for b in range(3)]
        bias = column(cols_ref, rows, BIAS)
        totals, last = [None] * 7, [[None] * 2, [None] * 2]
        for part in range(parts):
            moved, shorts = [], []
            for b in (1, 2):
                x = f32(pack_ref[part, b * chans + row : b * chans + row + block])
                turns = [pltpu.roll(x, k, 1) for k in (1, 2)]
                fixed = []
                for k in range(2):
                    before = 0.0 if part == 0 else last[b - 1][k]
                    head = after_wrap(turns[k][:, :LANES], before, k + 1)
                    fixed.append(jnp.concatenate([head, turns[k][:, LANES:]], 1))
                    last[b - 1][k] = turns[k][:, :LANES]
                moved.append([x] + fixed)
                shorts.append(f32(bf16(taps[b][0] * x + taps[b][1] * fixed[0] + taps[b][2] * fixed[1])))
            inner = f32(inner_ref[part, rows])
            d_gated = f32(bf16(bias * inner + f32(back_ref[part, rows])))
            terms = []
            for b in (1, 2):
                g = f32(bf16(d_gated * shorts[2 - b]))
                terms += [fold(g * moved[b - 1][k]) for k in range(3)]
            terms.append(fold(inner * f32(gate_ref[part, rows])))
            totals = [t if total is None else total + t for total, t in zip(totals, terms)]
        for k in range(7):
            tiles[k, rows] = totals[k]
    rows_ref[...] = sum([sum_rows(k, tiles.at[k]) for k in range(7)])[:8]


def lags_kernel(gate_ref, grad_ref, twist_ref, fwd_ref, inv_ref, out_ref, token_ref, work, sent):
    chans = out_ref.shape[0]
    def body(g, row):
        def store(s, h, value):
            out_ref[pl.ds(pl.multiple_of(row + h, HALF), HALF), s * LANES : (s + 1) * LANES] = value

        gate, grad = spectrum_pair(gate_ref, grad_ref, row, twist_ref, fwd_ref, work.at[g])
        inverse_group(conj_product(gate, grad), twist_ref.at[1], inv_ref, work.at[g, 0], store)

    over_groups(chans // ROWS, work.shape[0], body, sent)
    token_ref[...] = jnp.zeros_like(token_ref)


def place(kernel, name, outs, args, scratch=(), flops=10**6, after=(), vmem=VMEM_MOST):
    n_args, n_outs = len(args), len(outs)
    far = [k for k in range(n_outs) if len(outs[k]) == 4]

    def body(*refs):
        out_refs = list(refs[n_args + len(after) :][:n_outs])
        rest = refs[n_args + len(after) + n_outs :]
        own, stages, sems = rest[: len(scratch)], rest[len(scratch) :][: len(far)], rest[len(scratch) + len(far) :]

        def copy(j, i):
            axis, pieces = outs[far[j]][2:]
            size = outs[far[j]][0][axis] // pieces
            start = i * size if isinstance(i, int) else pl.multiple_of(i * size, size)
            at = (slice(None),) * axis + (pl.ds(start, size),)
            return pltpu.make_async_copy(stages[j].at[at], out_refs[far[j]].at[at], sems[j].at[i])

        def sent(i):
            for j in range(len(far)):
                copy(j, i).start()

        shown = list(out_refs)
        for j, k in enumerate(far):
            shown[k] = stages[j]
        kernel(*refs[:n_args], *shown, *own, sent=sent)
        for j, k in enumerate(far):
            for i in range(outs[k][3]):
                copy(j, i).wait()

    near = pl.BlockSpec(memory_space=pltpu.VMEM)
    away = pl.BlockSpec(memory_space=pltpu.HBM)
    return pl.pallas_call(
        body,
        in_specs=[near] * n_args + [away] * len(after),
        out_specs=[away if k in far else near for k in range(n_outs)],
        out_shape=[jax.ShapeDtypeStruct(*o[:2]) for o in outs],
        scratch_shapes=list(scratch)
        + [pltpu.VMEM(*outs[k][:2]) for k in far]
        + [pltpu.SemaphoreType.DMA((outs[k][3],)) for k in far],
        compiler_params=pltpu.CompilerParams(vmem_limit_bytes=vmem),
        cost_estimate=pl.CostEstimate(flops=flops, bytes_accessed=4 * 2**20, transcendentals=0),
        name=name,
    )(*args, *after)


TOKEN = ((8, LANES), jnp.float32)


def transforms(parts, chans, width):
    length = parts * width
    slabs = length // LANES
    groups = chans // ROWS
    per = math.gcd(groups, 4)
    tables = make_tables(length)
    work = pltpu.VMEM((per, 2, slabs * ROWS, 2 * LANES), jnp.float32)
    outs = pltpu.VMEM((per, slabs, ROWS, LANES), jnp.float32)
    flops = 2 * 3 * 4 * groups * slabs * ROWS * 256 * 256
    pieces = groups // per
    result = ((parts, chans, width), jnp.bfloat16, 1, pieces)
    spec = ((groups, slabs * ROWS, 2 * LANES), jnp.float32, 0, pieces)

    longer = ((parts, chans + ROWS, width), jnp.bfloat16, 1, groups + 1)

    def convolve(pack, cols, after):
        args = (pack, cols, *tables)
        return place(convolve_kernel, "convolve", [result, spec, result, TOKEN], args, [work, outs], 3 * flops, after)

    def correlate(grad, spec, early):
        args = (grad, spec, early, *tables)
        return place(correlate_kernel, "correlate", [longer], args, [work, outs], 2 * flops, vmem=VMEM_ALL)[0]

    def lags(gate, grad):
        out = ((chans, length), jnp.float32, 0, pieces)
        return place(lags_kernel, "lags", [out, TOKEN], (gate, grad, *tables), [work], 3 * flops)

    def grads(back, inner, pack, gate, cols):
        tiles = pltpu.VMEM((7, chans, LANES), jnp.float32)
        out = ((8, chans), jnp.float32)
        return place(grads_kernel, "grads", [out], (back, inner, pack, gate, cols), [tiles], flops)[0]

    return convolve, correlate, lags, grads


def picks(pairs):
    rows = lax.broadcasted_iota(jnp.int32, (ROWS, LANES), 0)
    lanes = lax.broadcasted_iota(jnp.int32, (ROWS, LANES), 1)
    hit = None
    for row, lane in pairs:
        here = (rows == row) & (lanes == lane)
        hit = here if hit is None else hit | here
    return hit.astype(jnp.float32).astype(jnp.bfloat16)


def to_rows(pairs, tile):
    return lax.dot_general(picks(pairs), tile, (((1,), (1,)), ((), ())), preferred_element_type=jnp.float32)


def to_lanes(pairs, rows):
    return lax.dot_general(rows, picks(pairs), (((0,), (0,)), ((), ())), preferred_element_type=jnp.float32)


def sum_rows(row, tile_ref):
    tile = tile_ref[...]
    upper = bf16(tile)
    lower = bf16(tile - f32(upper))
    ones = bf16((lax.broadcasted_iota(jnp.int32, (ROWS, LANES), 0) == row).astype(jnp.float32))
    dot = lambda v: lax.dot_general(ones, v, (((1,), (1,)), ((), ())), preferred_element_type=jnp.float32)
    return dot(upper) + dot(lower)


def fold(value):
    tile = value[:, :LANES]
    for k in range(1, value.shape[1] // LANES):
        tile = tile + value[:, k * LANES : (k + 1) * LANES]
    return tile


def fill_earlier(fill, slot, branch, edge):
    for steps in (1, 2):
        fill[slot, steps - 1] = to_lanes([(2 * branch + 2 - steps + i, i) for i in range(steps)], edge)


def fill_later(fill, slot, branch, edge):
    for steps in (1, 2):
        fill[slot, steps - 1] = to_lanes([(2 * branch + i, LANES - steps + i) for i in range(steps)], edge)


def earlier(value, fill, slot, rows, steps):
    moved = pltpu.roll(value, steps, 1)
    lanes = lax.broadcasted_iota(jnp.int32, (value.shape[0], LANES), 1)
    first = jnp.where(lanes < steps, fill[slot, steps - 1, rows], moved[:, :LANES])
    return jnp.concatenate([first, moved[:, LANES:]], 1)


def later(value, fill, slot, rows, steps):
    count = value.shape[1]
    moved = pltpu.roll(value, count - steps, 1)
    lanes = lax.broadcasted_iota(jnp.int32, (value.shape[0], LANES), 1)
    last = jnp.where(lanes >= LANES - steps, fill[slot, steps - 1, rows], moved[:, count - LANES :])
    return jnp.concatenate([moved[:, : count - LANES], last], 1)


def over_rows(ref, body, done=None, block=32):
    piece = ref.shape[0] // PARTS
    for row in range(0, ref.shape[0], block):
        body(slice(row, row + block))
        if done and (row + block) % piece == 0:
            done(row // piece)


def edge_kernel(x0_ref, x1_ref, x2_ref, edge_ref):
    total = None
    for b, ref in enumerate((x0_ref, x1_ref, x2_ref)):
        tile = ref[:, ref.shape[1] - LANES :]
        rows = to_rows([(2 * b, LANES - 2), (2 * b + 1, LANES - 1)], tile)
        total = rows if total is None else total + rows
    edge_ref[...] = bf16(total)


def gate_kernel(x0_ref, x1_ref, x2_ref, edge_ref, cols_ref, s0_ref, s1_ref, s2_ref, gated_ref, tips_ref, fill, sent):
    edge = edge_ref[...]
    for b in range(3):
        fill_earlier(fill, b, b, edge)

    def body(rows):
        shorts = []
        for b, (x_ref, s_ref) in enumerate(((x0_ref, s0_ref), (x1_ref, s1_ref), (x2_ref, s2_ref))):
            x = f32(x_ref[rows])
            total = tap(cols_ref, rows, b, 0) * x + tap(cols_ref, rows, b, 1) * earlier(x, fill, b, rows, 1)
            shorts.append(bf16(total + tap(cols_ref, rows, b, 2) * earlier(x, fill, b, rows, 2)))
            s_ref[rows] = shorts[b]
        gated_ref[rows] = bf16(f32(shorts[1]) * f32(shorts[2]))

    over_rows(gated_ref, body, sent)
    tips = to_rows([(0, 0), (1, 1)], s2_ref[:, :LANES]) + to_rows([(2, 0), (3, 1)], s1_ref[:, :LANES])
    tips_ref[...] = bf16(tips)


def mix(rows, conv_ref, s0_ref, gated_ref, cot_ref, cols_ref):
    inner = f32(conv_ref[rows]) + column(cols_ref, rows, BIAS) * f32(gated_ref[rows])
    return inner, f32(s0_ref[rows]) * inner, f32(cot_ref[rows])


def sums_kernel(conv_ref, s0_ref, gated_ref, cot_ref, cols_ref, out_ref, sent):
    lump = lambda v: jnp.sum(v.reshape(v.shape[0] // 8, 8, v.shape[1]), 0)
    total = [jnp.zeros((8, conv_ref.shape[1]), jnp.float32)] * 2

    def body(rows):
        _, mixed, cot = mix(rows, conv_ref, s0_ref, gated_ref, cot_ref, cols_ref)
        total[0] = total[0] + lump(mixed * mixed)
        total[1] = total[1] + lump(cot * column(cols_ref, rows, GAIN) * mixed)

    over_rows(conv_ref, body)

    for k in range(2):
        out_ref[k : k + 1] = jnp.sum(total[k], 0, keepdims=True)


def norm_terms(width, part_refs):
    total = part_refs[0][...]
    for ref in part_refs[1:]:
        total = total + ref[...]
    recip = lax.rsqrt(total[0:1] / width + EPS)
    return recip, recip * recip * recip * (total[1:2] / width)


def inner_kernel(width, n_ch, *refs, sent):
    parts, (conv_ref, s0_ref, gated_ref, cot_ref, cols_ref, out_ref) = refs[:n_ch], refs[n_ch:]
    recip, cubed = norm_terms(width, parts)

    def body(rows):
        _, mixed, cot = mix(rows, conv_ref, s0_ref, gated_ref, cot_ref, cols_ref)
        d_mixed = recip * (cot * column(cols_ref, rows, GAIN)) - mixed * cubed
        out_ref[rows] = bf16(d_mixed * f32(s0_ref[rows]))

    over_rows(out_ref, body, sent)


def output_kernel(width, n_ch, *refs, sent):
    parts, refs = refs[:n_ch], refs[n_ch:]
    conv_ref, s0_ref, gated_ref, cot_ref, cols_ref, x0_ref, edge_ref, inner_ref = refs[:8]
    out_ref, g0_ref, rows_ref, after_ref, fill, tiles = refs[8:]
    recip, cubed = norm_terms(width, parts)
    fill_earlier(fill, 0, 0, edge_ref[...])

    def body(rows):
        inner, mixed, cot = mix(rows, conv_ref, s0_ref, gated_ref, cot_ref, cols_ref)
        gain = column(cols_ref, rows, GAIN)
        normed = mixed * recip
        out_ref[rows] = bf16(normed * gain)
        g0 = bf16((recip * (cot * gain) - mixed * cubed) * inner)
        g0_ref[rows] = g0
        x, g = f32(x0_ref[rows]), f32(g0)
        tiles[0, rows] = fold(g * x)
        tiles[1, rows] = fold(g * earlier(x, fill, 0, rows, 1))
        tiles[2, rows] = fold(g * earlier(x, fill, 0, rows, 2))
        tiles[3, rows] = fold(cot * normed)

    over_rows(out_ref, body, sent)
    rows_ref[...] = sum([sum_rows(k, tiles.at[k]) for k in range(4)])[:8]
    after = to_rows([(0, 0), (1, 1), (2, 0), (3, 1)], inner_ref[:, :LANES])
    after_ref[...] = bf16(after + to_rows([(4, 0), (5, 1)], g0_ref[:, :LANES]))


def adjoint(g, branch, fill, slot, rows, cols_ref):
    total = tap(cols_ref, rows, branch, 0) * g + tap(cols_ref, rows, branch, 1) * later(g, fill, slot, rows, 1)
    return bf16(total + tap(cols_ref, rows, branch, 2) * later(g, fill, slot, rows, 2))


def first_kernel(g0_ref, edge_ref, cols_ref, out_ref, token_ref, fill, sent):
    fill_later(fill, 0, 2, edge_ref[...])

    def body(rows):
        out_ref[rows] = adjoint(f32(g0_ref[rows]), 0, fill, 0, rows, cols_ref)

    over_rows(out_ref, body, sent)
    token_ref[...] = jnp.zeros_like(token_ref)


def pair_kernel(
    back_ref, inner_ref, s1_ref, s2_ref, cols_ref, tips_ref, next_ref, bias_ref, grads_ref, d1_ref, d2_ref, *refs, sent
):
    short_ref, gain_ref, fill, edge = refs
    parts, longer, _ = back_ref.shape
    own = longer - ROWS
    sums = None
    for part in range(parts):
        lanes = slice(part * own, (part + 1) * own)
        extra = f32(back_ref[part, own:, :own])
        d_gated = f32(bf16(bias_ref[:, lanes] * f32(next_ref[:, lanes]) + extra))
        edge[:, lanes] = bf16(d_gated * f32(tips_ref[:, lanes]))
        terms = extra[4:8] + extra[8:12]
        sums = terms if sums is None else sums + terms
    for k in range(2):
        fill_later(fill, k, k, edge[...])
    short_ref[0] = sums[:3]
    short_ref[1] = grads_ref[:3]
    short_ref[2] = grads_ref[3:6]
    gain_ref[...] = sums[3:4]

    def body(rows):
        part, row = rows.start // own, rows.start % own
        back = f32(back_ref[part, row : row + rows.stop - rows.start])
        d_gated = f32(bf16(column(cols_ref, rows, BIAS) * f32(inner_ref[rows]) + back))
        for b, s_ref, d_ref in ((1, s2_ref, d1_ref), (2, s1_ref, d2_ref)):
            g = f32(bf16(d_gated * f32(s_ref[rows])))
            d_ref[rows] = adjoint(g, b, fill, b - 1, rows, cols_ref)

    over_rows(d1_ref, body, sent, min(32, own))


def exchange(value):
    return lax.all_to_all(value, "ctx", split_axis=0, concat_axis=0, tiled=True)


def local(x_first, x_second, x_value, short_filter, long_filter, skip_bias, norm_gain, cotangent):
    chans, steps_dev = x_first.shape
    n_ctx = lax.axis_size("ctx")
    n_ch = lax.axis_size("ch")
    width = chans * n_ch
    own = chans // n_ctx
    convolve, correlate, lags, grads = transforms(n_ctx, own, steps_dev)
    by_dev = lambda v: v.reshape(n_ctx, own, steps_dev)
    by_pos = lambda v: v.reshape(chans, steps_dev)

    array = ((chans, steps_dev), jnp.bfloat16, 0, PARTS)
    edges = ((ROWS, chans), jnp.bfloat16)
    rows8 = ((8, chans), jnp.float32)
    fills = lambda n: pltpu.VMEM((n, 2, chans, LANES), jnp.float32)
    tiles = lambda n: pltpu.VMEM((n, chans, LANES), jnp.float32)

    pack = exchange(jnp.concatenate([by_dev(v) for v in (long_filter, x_second, x_value)], 1))
    tip = pl.BlockSpec((chans, LANES), lambda i: (0, steps_dev // LANES - 1))
    edge = pl.pallas_call(
        edge_kernel,
        grid=(1,),
        in_specs=[tip] * 3,
        out_specs=pl.BlockSpec((ROWS, chans), lambda i: (0, 0)),
        out_shape=jax.ShapeDtypeStruct(*edges),
        name="edge",
    )(x_first, x_second, x_value)
    edge = shifted(edge, "ctx", 1)
    cols = jnp.concatenate([short_filter.reshape(9, chans), skip_bias[None], norm_gain[None]], 0)
    cols = jnp.pad(cols, ((0, ROWS - 11), (0, 0))).T
    own_cols = lax.dynamic_slice_in_dim(cols, lax.axis_index("ctx") * own, own, 0)
    conv_cm, filt_spec, gated_cm, conv_done = convolve(pack, own_cols, (edge,))
    first_s, second_s, third_s, gated, tips = place(
        gate_kernel, "gate", [array] * 4 + [edges], (x_first, x_second, x_value, edge, cols), [fills(3)], after=(conv_done,), vmem=VMEM_ALL
    )
    tips = shifted(tips, "ctx", -1)
    conv = by_pos(exchange(conv_cm))
    mix_args = (conv, first_s, gated, cotangent, cols)
    sums = place(sums_kernel, "sums", [((2, steps_dev), jnp.float32)], mix_args)[0]
    parts = [sums]
    for k in range(1, n_ch):
        parts.append(lax.ppermute(sums, "ch", [(i, i ^ k) for i in range(n_ch)]))
    inner_part = lambda *refs, sent: inner_kernel(width, n_ch, *refs, sent=sent)
    d_inner = place(inner_part, "inner", [array], (*parts, *mix_args))[0]
    d_inner_cm = exchange(by_dev(d_inner))
    output, grad_first, early_rows, after = place(
        lambda *refs, sent: output_kernel(width, n_ch, *refs, sent=sent),
        "output",
        [array, array, rows8, edges],
        (*parts, *mix_args, x_first, edge, d_inner),
        [fills(1), tiles(4)],
    )
    after = shifted(after, "ctx", -1)
    back_cm = correlate(d_inner_cm, filt_spec, early_rows)
    back = exchange(back_cm)
    d_first, first_done = place(first_kernel, "first", [array, TOKEN], (grad_first, after, cols), [fills(1)])
    own_rows = grads(back_cm, d_inner_cm, pack, gated_cm, own_cols)
    d_long, lags_done = lags(gated_cm, d_inner_cm)
    d_second, d_value, d_short, d_gain = place(
        pair_kernel,
        "pair",
        [array, array, ((3, 3, own), jnp.float32), ((1, own), jnp.float32)],
        (back, d_inner, second_s, third_s, cols, tips, after, skip_bias[None], own_rows),
        [fills(2), pltpu.VMEM(*edges)],
        after=(first_done, lags_done),
    )
    return (output, d_first, d_second, d_value, d_long, d_short, own_rows[6], d_gain[0])


def solution(mesh):
    seq = P("ch", "ctx")
    own = ("ch", "ctx")
    return jax.shard_map(
        local,
        mesh=mesh,
        in_specs=(seq, seq, seq, P(None, None, "ch"), seq, P("ch"), P("ch"), seq),
        out_specs=(seq, seq, seq, seq, P(own, None), P(None, None, own), P(own), P(own)),
        check_vma=False,
    )
```

time: 156 us -> 136 us (0.87)
  Pallas kernels: 14.5 us -> 46.8 us
  local copies, waits for them, and re-layouts: 28.9 us -> 7.87 us
  blocking collectives: 18.7 us -> 0 us
  other arithmetic: 14 us -> 2.67 us
  starting transfers between devices: 31.3 us -> 29.4 us
    pallas_call x4 -> x11, Pallas kernels: 14.5 us -> 46.8 us  [the longest x10 44.7 us: place(): pl.pallas_call(body, in_specs=[near] * n_args + [away] * len(after), out_...]
    all_to_all x1 -> x0, blocking collectives: 18.7 us -> none  [exchange(): return lax.all_to_all(value, 'ctx', split_axis=0, concat_axis=0, tiled=True)]
    unnamed x63 -> x60, local copies, waits for them, and re-layouts: 21.5 us -> 6.28 us
    ppermute x2 -> x3, waiting for transfers between devices: 1.28 us -> 10.6 us  [shifted(): lax.ppermute(value, axis, [(source, source + steps) for source in range(f...]
    all_to_all x4, waiting for transfers between devices: 41.7 us -> 34.6 us  [exchange(): return lax.all_to_all(value, 'ctx', split_axis=0, concat_axis=0, tiled=True)]
    ppermute x6 -> x3, starting transfers between devices: 9.02 us -> 1.92 us  [local(): parts.append(lax.ppermute(sums, 'ch', [(i, i ^ k) for i in range(n_ch)]))]
    convert_element_type x4 -> x0, local copies, waits for them, and re-layouts: 6.65 us -> none  [the longest x2 4.3 us: local(): f32 = lambda v: v.astype(jnp.float32)]
    reduce_sum x3 -> x0, other arithmetic: 5.49 us -> none  [the longest x1 2.61 us: local(): bias_part = jnp.sum(f32(d_inner) * f32(gated), axis=1)]
  transfers between devices with their start and end apart: 12 -> 10, of which waited for: 10 -> 8; matrix products, arithmetic and copies ran while one was open for 7% -> 1% of each run, Pallas kernels for 3% -> 23%
where the time goes in v2:
time: 136 us; the launch traced here: 135 us
  waiting for transfers between devices  47 us (35%)
  Pallas kernels  46.8 us (34%)
  starting transfers between devices  29.4 us (22%)
  local copies, waits for them, and re-layouts  7.87 us (6%)
  other arithmetic  2.67 us (2%)
    pallas_call x10, Pallas kernels, place(): pl.pallas_call(body, in_specs=[near] * n_args + [away] * len(after), out_...  44.7 us
    all_to_all x4, waiting for transfers between devices, exchange(): return lax.all_to_all(value, 'ctx', split_axis=0, concat_axis=0, tiled=True)  34.6 us
    all_to_all x4, starting transfers between devices, exchange(): return lax.all_to_all(value, 'ctx', split_axis=0, concat_axis=0, tiled=True)  20.8 us
    ppermute x3, waiting for transfers between devices, shifted(): lax.ppermute(value, axis, [(source, source + steps) for source in range(f...  10.6 us
    ppermute x3, starting transfers between devices, shifted(): lax.ppermute(value, axis, [(source, source + steps) for source in range(f...  6.65 us
    unnamed x60, local copies, waits for them, and re-layouts  6.28 us
  transfers between devices with their start and end apart: 10, of which 8 were waited for; matrix products, arithmetic and copies ran while one was open for 1% of the time, Pallas kernels for 23%

profile of v2, /device:TPU:0, one launch (start us, length us, event | category | flops | bytes accessed | tf_op | source)
XLA Modules:
  0.0 134.8 jit_solution(15019255155246824462)
XLA Ops:
  0.6 2.7 %pad_maximum_fusion = bf16[8,384,256]{2,1,0:T(8,128)(2,1)} fusion(bf16[8,128,256]{2,1,0:T(8,128)(2,1)} %bitcast.19, bf16[8,128,256]{2,1,0:T(8,128)(2,1)} %bitcast.20, bf16[8,128,256]{2,1,0:T(8,128)(2,1)} %bitcast.21), kind=kLoop, calls=%fused_computation | loop fusion | flops 4718592 | bytes 3145728 | tf_op jit(solution)/shard_map/concatenate | solution.py:626
  3.3 7.4 %all-to-all-start = ((bf16[8,384,256]{2,1,0:T(8,128)(2,1)}), bf16[8,384,256]{2,1,0:T(8,128)(2,1)S(1)}, u32[]{:S(2)}, u32[]{:S(2)}) async-start(bf16[8,384,256]{2,1,0:T(8,128)(2,1)} %pad_maximum_fusion), calls=%async_computation | async-start | bytes 3145728 | tf_op jit(solution)/shard_map/all_to_all | solution.py:607
  10.7 2.1 %edge.1 = bf16[16,1024]{1,0:T(8,128)(2,1)} custom-call(bf16[1024,256]{1,0:T(8,128)(2,1)} %refs_9_.1, bf16[1024,256]{1,0:T(8,128)(2,1)} %refs_1_.1, bf16[1024,256]{1,0:T(8,128)(2,1)} %refs_2_.3), custom_call_target="tpu_custom_call" | custom-call | tf_op jit(solution)/shard_map/edge/pallas_call | solution.py:628
  12.8 3.9 %collective-permute-start = (bf16[16,1024]{1,0:T(8,128)(2,1)}, bf16[16,1024]{1,0:T(8,128)(2,1)S(1)}, u32[]{:S(2)}, u32[]{:S(2)}) collective-permute-start(bf16[16,1024]{1,0:T(8,128)(2,1)} %edge.1), channel_id=1, source_target_pairs={{0,4},{4,8},{8,12},{12,16},{16,20},{20,24},{24,28},{1,5},{5,9},{9,... | collective-permute-start | bytes 98312 | tf_op jit(solution)/shard_map/ppermute | solution.py:31
  17.1 7.3 %collective-permute-done.refs_5_.refs_3_.refs_10_ = bf16[16,1024]{1,0:T(8,128)(2,1)S(1)} collective-permute-done((bf16[16,1024]{1,0:T(8,128)(2,1)}, bf16[16,1024]{1,0:T(8,128)(2,1)S(1)}, u32[]{:S(2)}, u32[]{:S(2)}) %collective-permute-start) | collective-permute-done | bytes 32800 | tf_op jit(solution)/shard_map/ppermute | solution.py:31
  24.3 23.4 %all-to-all-done.refs_0_.refs_2_ = bf16[8,384,256]{2,1,0:T(8,128)(2,1)S(1)} async-done(((bf16[8,384,256]{2,1,0:T(8,128)(2,1)}), bf16[8,384,256]{2,1,0:T(8,128)(2,1)S(1)}, u32[]{:S(2)}, u32[]{:S(2)}) %all-to-all-start) | async-done | bytes 1572896 | tf_op jit(solution)/shard_map/all_to_all | solution.py:607
  47.7 6.8 %convolve.1 = (bf16[8,128,256]{2,1,0:T(8,128)(2,1)}, f32[8,256,256]{2,1,0:T(8,128)S(1)}, bf16[8,128,256]{2,1,0:T(8,128)(2,1)S(1)}, f32[8,128]{1,0:T(8,128)S(1)}) custom-call(bf16[8,384,256]{2,1,0:T(8,128)(2,1)S(1)} %all-to-all-done.refs_0_.refs_2_, f32[128,16]{1,0:T(8,128)S(1)} %fusion.refs_1_.refs_4_, f32[2,16,2,128]{3,2,1,0:T(2,128)S(1)} %copy-done.21, ...), custom_call_target="tpu_custom_call" | custom-call | flops 9663676416 | bytes 4194304 | tf_op jit(solution)/shard_map/convolve/pallas_call | solution.py:346
  54.6 1.3 copy-done.26
  55.9 3.9 %all-to-all-start.1 = ((bf16[8,128,256]{2,1,0:T(8,128)(2,1)}), bf16[8,128,256]{2,1,0:T(8,128)(2,1)S(1)}, u32[]{:S(2)}, u32[]{:S(2)}) async-start(bf16[8,128,256]{2,1,0:T(8,128)(2,1)} %get-tuple-element.29), calls=%async_computation.1 | async-start | bytes 1048576 | tf_op jit(solution)/shard_map/all_to_all | solution.py:607
  59.8 0.8 pad_bitcast_fusion.refs_4_.refs_8_.refs_2_
  60.6 6.1 %gate.1 = (bf16[1024,256]{1,0:T(8,128)(2,1)}, bf16[1024,256]{1,0:T(8,128)(2,1)}, bf16[1024,256]{1,0:T(8,128)(2,1)}, bf16[1024,256]{1,0:T(8,128)(2,1)}, bf16[16,1024]{1,0:T(8,128)(2,1)}) custom-call(bf16[1024,256]{1,0:T(8,128)(2,1)} %refs_9_.1, bf16[1024,256]{1,0:T(8,128)(2,1)} %refs_1_.1, bf16[1024,256]{1,0:T(8,128)(2,1)} %refs_2_.3, ...), custom_call_target="tpu_custom_call" | custom-call | flops 1000000 | bytes 4194304 | tf_op jit(solution)/shard_map/gate/pallas_call | solution.py:346
  66.8 7.6 %all-to-all-done.1 = bf16[8,128,256]{2,1,0:T(8,128)(2,1)S(1)} async-done(((bf16[8,128,256]{2,1,0:T(8,128)(2,1)}), bf16[8,128,256]{2,1,0:T(8,128)(2,1)S(1)}, u32[]{:S(2)}, u32[]{:S(2)}) %all-to-all-start.1) | async-done | bytes 524320 | tf_op jit(solution)/shard_map/all_to_all | solution.py:607
  74.4 1.0 copy-done.3
  75.4 1.0 copy-done.5
  77.1 1.6 %collective-permute-start.2 = (f32[2,256]{1,0:T(2,128)S(1)}, f32[2,256]{1,0:T(2,128)S(1)}, u32[]{:S(2)}, u32[]{:S(2)}) collective-permute-start(f32[2,256]{1,0:T(2,128)S(1)} %sums.1.refs_0_), channel_id=1, source_target_pairs={{0,2},{1,3},{2,0},{3,1},{4,6},{5,7},{6,4},{7,5},{8,10},{9,11},{10,... | collective-permute-start | bytes 6152 | tf_op jit(solution)/shard_map/ppermute | solution.py:650
  78.9 1.1 collective-permute-done.3.refs_3_
  80.7 1.2 inner.1.refs_11_.refs_1_
  82.0 4.7 %all-to-all-start.2 = ((bf16[8,128,256]{2,1,0:T(8,128)(2,1)}), bf16[8,128,256]{2,1,0:T(8,128)(2,1)}, u32[]{:S(2)}, u32[]{:S(2)}) async-start(bf16[8,128,256]{2,1,0:T(8,128)(2,1)} %bitcast.8), calls=%async_computation.2 | async-start | bytes 1048576 | tf_op jit(solution)/shard_map/all_to_all | solution.py:607
  86.7 4.1 %output.1 = (bf16[1024,256]{1,0:T(8,128)(2,1)}, bf16[1024,256]{1,0:T(8,128)(2,1)S(1)}, f32[8,1024]{1,0:T(8,128)S(1)}, bf16[16,1024]{1,0:T(8,128)(2,1)S(1)}) custom-call(f32[2,256]{1,0:T(2,128)S(1)} %sums.1.refs_0_, f32[2,256]{1,0:T(2,128)S(1)} %collective-permute-done.1.refs_1_, f32[2,256]{1,0:T(2,128)S(1)} %collective-permute-done.2.refs_2_, ...), custom_call_target="tpu_custom_call" | custom-call | flops 1000000 | bytes 4194304 | tf_op jit(solution)/shard_map/output/pallas_call | solution.py:346
  91.4 1.3 collective-permute-start.4
  92.7 1.5 %collective-permute-start.5 = (bf16[16,1024]{1,0:T(8,128)(2,1)S(1)}, bf16[16,1024]{1,0:T(8,128)(2,1)S(1)}, u32[]{:S(2)}, u32[]{:S(2)}) collective-permute-start(bf16[16,1024]{1,0:T(8,128)(2,1)S(1)} %copy-done.29), channel_id=1, source_target_pairs={{4,0},{8,4},{12,8},{16,12},{20,16},{24,20},{28,24},{5,1},{9,5},{13... | collective-permute-start | bytes 98312 | tf_op jit(solution)/shard_map/ppermute | solution.py:31
  94.2 3.3 %collective-permute-done.4.refs_1_.refs_6_ = bf16[16,1024]{1,0:T(8,128)(2,1)S(1)} collective-permute-done((bf16[16,1024]{1,0:T(8,128)(2,1)S(1)}, bf16[16,1024]{1,0:T(8,128)(2,1)S(1)}, u32[]{:S(2)}, u32[]{:S(2)}) %collective-permute-start.4) | collective-permute-done | bytes 32800 | tf_op jit(solution)/shard_map/ppermute | solution.py:31
  97.5 1.8 %first.1 = (bf16[1024,256]{1,0:T(8,128)(2,1)}, f32[8,128]{1,0:T(8,128)S(1)}) custom-call(bf16[1024,256]{1,0:T(8,128)(2,1)S(1)} %get-tuple-element.34.refs_0_, bf16[16,1024]{1,0:T(8,128)(2,1)S(1)} %collective-permute-done.4.refs_1_.refs_6_, f32[1024,16]{1,0:T(8,128)S(1)} %copy-done), custom_call_target="tpu_custom_call" | custom-call | flops 1000000 | bytes 4194304 | tf_op jit(solution)/shard_map/first/pallas_call | solution.py:346
  99.4 2.8 %all-to-all-done.2.refs_0_.refs_1_ = bf16[8,128,256]{2,1,0:T(8,128)(2,1)} async-done(((bf16[8,128,256]{2,1,0:T(8,128)(2,1)}), bf16[8,128,256]{2,1,0:T(8,128)(2,1)}, u32[]{:S(2)}, u32[]{:S(2)}) %all-to-all-start.2) | async-done | bytes 524320 | tf_op jit(solution)/shard_map/all_to_all | solution.py:607
  102.2 6.0 %correlate.1.refs_0_ = bf16[8,144,256]{2,1,0:T(8,128)(2,1)} custom-call(bf16[8,128,256]{2,1,0:T(8,128)(2,1)} %all-to-all-done.2.refs_0_.refs_1_, f32[8,256,256]{2,1,0:T(8,128)} %copy-done.26, f32[8,1024]{1,0:T(8,128)} %copy-done.16, f32[2,16,2,128]{3,2,1,0:T(2,128)} %constant.20.clone.refs_2_.refs_3_, bf16[2,256,256]{2,1,0:T(8,128)(2,1)} %constant.21.clone.refs_3_.refs_4_, ...), custom_call_target="tpu_custom_call" | custom-call | flops 6442450944 | bytes 4194304 | tf_op jit(solution)/shard_map/correlate/pallas_call | solution.py:346
  108.2 4.9 %all-to-all-start.3 = ((bf16[8,144,256]{2,1,0:T(8,128)(2,1)}), bf16[8,144,256]{2,1,0:T(8,128)(2,1)S(1)}, u32[]{:S(2)}, u32[]{:S(2)}) async-start(bf16[8,144,256]{2,1,0:T(8,128)(2,1)} %correlate.1.refs_0_), calls=%async_computation.3 | async-start | bytes 1179648 | tf_op jit(solution)/shard_map/all_to_all | solution.py:607
  113.1 1.1 copy-done.9
  114.2 1.0 copy-done.24
  115.2 3.4 %grads.1.refs_8_ = f32[8,128]{1,0:T(8,128)S(1)} custom-call(bf16[8,144,256]{2,1,0:T(8,128)(2,1)S(1)} %copy-done.9, bf16[8,128,256]{2,1,0:T(8,128)(2,1)} %all-to-all-done.2.refs_0_.refs_1_, bf16[8,384,256]{2,1,0:T(8,128)(2,1)S(1)} %copy-done.8, bf16[8,128,256]{2,1,0:T(8,128)(2,1)S(1)} %copy-done.24, f32[128,16]{1,0:T(8,128)S(1)} %fusion.refs_1_.refs_4_), custom_call_target="tpu_custom_call" | custom-call | flops 3221225472 | bytes 4194304 | tf_op jit(solution)/shard_map/grads/pallas_call | solution.py:346
  118.7 7.3 %lags.1 = (f32[128,2048]{1,0:T(8,128)}, f32[8,128]{1,0:T(8,128)S(1)}) custom-call(bf16[8,128,256]{2,1,0:T(8,128)(2,1)S(1)} %copy-done.25, bf16[8,128,256]{2,1,0:T(8,128)(2,1)} %all-to-all-done.2.refs_0_.refs_1_, f32[2,16,2,128]{3,2,1,0:T(2,128)S(1)} %copy-done.22, bf16[2,256,256]{2,1,0:T(8,128)(2,1)S(1)} %copy-done.20, bf16[2,256,256]{2,1,0:T(8,128)(2,1)S(1)} %copy-done.18), custom_call_target="tpu_custom_call" | custom-call | flops 9663676416 | bytes 4194304 | tf_op jit(solution)/shard_map/lags/pallas_call | solution.py:346
  126.5 0.8 all-to-all-done.3.refs_0_
  127.4 7.3 %pair.1 = (bf16[1024,256]{1,0:T(8,128)(2,1)}, bf16[1024,256]{1,0:T(8,128)(2,1)}, f32[3,3,128]{2,1,0:T(4,128)}, f32[1,128]{1,0:T(1,128)}) custom-call(bf16[8,144,256]{2,1,0:T(8,128)(2,1)S(1)} %all-to-all-done.3.refs_0_, bf16[1024,256]{1,0:T(8,128)(2,1)} %inner.1.refs_11_.refs_1_, bf16[1024,256]{1,0:T(8,128)(2,1)S(1)} %copy-done.10, ...), custom_call_target="tpu_custom_call" | custom-call | flops 1000000 | bytes 4194304 | tf_op jit(solution)/shard_map/pair/pallas_call | solution.py:346
  (66 shorter events, 3.0 us)
Async XLA Ops:
  3.3 13.4 %copy-start.27 = (f32[3,3,1024]{2,1,0:T(4,128)S(1)}, f32[3,3,1024]{2,1,0:T(4,128)}, u32[]{:S(2)}) copy-start(f32[3,3,1024]{2,1,0:T(4,128)} %param.14) | copy-start | bytes 110596
  3.3 13.5 %copy-start.14 = (f32[1024]{0:T(1024)S(1)}, f32[1024]{0:T(1024)}, u32[]{:S(2)}) copy-start(f32[1024]{0:T(1024)} %param.16) | copy-start | bytes 12292
  3.3 13.5 %copy-start.28 = (f32[1024]{0:T(1024)S(1)}, f32[1024]{0:T(1024)}, u32[]{:S(2)}) copy-start(f32[1024]{0:T(1024)} %param.17) | copy-start | bytes 12292
  3.3 44.4 %all-to-all-start = ((bf16[8,384,256]{2,1,0:T(8,128)(2,1)}), bf16[8,384,256]{2,1,0:T(8,128)(2,1)S(1)}, u32[]{:S(2)}, u32[]{:S(2)}) async-start(bf16[8,384,256]{2,1,0:T(8,128)(2,1)} %pad_maximum_fusion), calls=%async_computation | async-start | bytes 3145728 | tf_op jit(solution)/shard_map/all_to_all | solution.py:607
  10.7 37.0 %copy-start.17 = (bf16[2,256,256]{2,1,0:T(8,128)(2,1)S(1)}, bf16[2,256,256]{2,1,0:T(8,128)(2,1)}, u32[]{:S(2)}) copy-start(bf16[2,256,256]{2,1,0:T(8,128)(2,1)} %constant.22.clone.refs_4_.refs_5_) | copy-start | bytes 786436
  10.7 37.0 %copy-start.19 = (bf16[2,256,256]{2,1,0:T(8,128)(2,1)S(1)}, bf16[2,256,256]{2,1,0:T(8,128)(2,1)}, u32[]{:S(2)}) copy-start(bf16[2,256,256]{2,1,0:T(8,128)(2,1)} %constant.21.clone.refs_3_.refs_4_) | copy-start | bytes 786436
  10.7 37.0 %copy-start.21 = (f32[2,16,2,128]{3,2,1,0:T(2,128)S(1)}, f32[2,16,2,128]{3,2,1,0:T(2,128)}, u32[]{:S(2)}) copy-start(f32[2,16,2,128]{3,2,1,0:T(2,128)} %constant.20.clone.refs_2_.refs_3_) | copy-start | bytes 98308
  12.8 11.5 %collective-permute-start = (bf16[16,1024]{1,0:T(8,128)(2,1)}, bf16[16,1024]{1,0:T(8,128)(2,1)S(1)}, u32[]{:S(2)}, u32[]{:S(2)}) collective-permute-start(bf16[16,1024]{1,0:T(8,128)(2,1)} %edge.1), channel_id=1, source_target_pairs={{0,4},{4,8},{8,12},{12,16},{16,20},{20,24},{24,28},{1,5},{5,9},{9,... | collective-permute-start | bytes 98312 | tf_op jit(solution)/shard_map/ppermute | solution.py:31
  24.3 30.2 %copy-start.12 = (bf16[16,1024]{1,0:T(8,128)(2,1)}, bf16[16,1024]{1,0:T(8,128)(2,1)S(1)}, u32[]{:S(2)}) copy-start(bf16[16,1024]{1,0:T(8,128)(2,1)S(1)} %collective-permute-done.refs_5_.refs_3_.refs_10_) | copy-start | bytes 98308
  47.7 6.9 %copy-start.7 = (bf16[8,384,256]{2,1,0:T(8,128)(2,1)}, bf16[8,384,256]{2,1,0:T(8,128)(2,1)S(1)}, u32[]{:S(2)}) copy-start(bf16[8,384,256]{2,1,0:T(8,128)(2,1)S(1)} %all-to-all-done.refs_0_.refs_2_) | copy-start | bytes 4718596
  55.9 4.7 %copy-start.15 = (f32[8,128]{1,0:T(8,128)}, f32[8,128]{1,0:T(8,128)S(1)}, u32[]{:S(2)}) copy-start(f32[8,128]{1,0:T(8,128)S(1)} %get-tuple-element.30.refs_5_) | copy-start | bytes 12292
  55.9 10.8 %copy-start.23 = (bf16[8,128,256]{2,1,0:T(8,128)(2,1)}, bf16[8,128,256]{2,1,0:T(8,128)(2,1)S(1)}, u32[]{:S(2)}) copy-start(bf16[8,128,256]{2,1,0:T(8,128)(2,1)S(1)} %get-tuple-element.42.refs_3_.refs_0_) | copy-start | bytes 1572868
  55.9 18.4 %copy-start.2 = (bf16[1024,256]{1,0:T(8,128)(2,1)S(1)}, bf16[1024,256]{1,0:T(8,128)(2,1)}, u32[]{:S(2)}) copy-start(bf16[1024,256]{1,0:T(8,128)(2,1)} %refs_7_.3) | copy-start | bytes 1572868
  55.9 18.4 %all-to-all-start.1 = ((bf16[8,128,256]{2,1,0:T(8,128)(2,1)}), bf16[8,128,256]{2,1,0:T(8,128)(2,1)S(1)}, u32[]{:S(2)}, u32[]{:S(2)}) async-start(bf16[8,128,256]{2,1,0:T(8,128)(2,1)} %get-tuple-element.29), calls=%async_computation.1 | async-start | bytes 1048576 | tf_op jit(solution)/shard_map/all_to_all | solution.py:607
  60.6 13.8 %copy-start = (f32[1024,16]{1,0:T(8,128)S(1)}, f32[1024,16]{1,0:T(8,128)}, u32[]{:S(2)}) copy-start(f32[1024,16]{1,0:T(8,128)} %pad_bitcast_fusion.refs_4_.refs_8_.refs_2_) | copy-start | bytes 196612
  76.5 4.3 %copy-start.4 = (bf16[1024,256]{1,0:T(8,128)(2,1)S(1)}, bf16[1024,256]{1,0:T(8,128)(2,1)}, u32[]{:S(2)}) copy-start(bf16[1024,256]{1,0:T(8,128)(2,1)} %get-tuple-element.31.refs_1_.refs_5_) | copy-start | bytes 1572868
  77.0 9.7 %copy-start.1 = (bf16[1024,256]{1,0:T(8,128)(2,1)S(1)}, bf16[1024,256]{1,0:T(8,128)(2,1)}, u32[]{:S(2)}) copy-start(bf16[1024,256]{1,0:T(8,128)(2,1)} %refs_9_.1) | copy-start | bytes 1572868
  77.0 9.7 %copy-start.6 = (bf16[1024,256]{1,0:T(8,128)(2,1)S(1)}, bf16[1024,256]{1,0:T(8,128)(2,1)}, u32[]{:S(2)}) copy-start(bf16[1024,256]{1,0:T(8,128)(2,1)} %get-tuple-element.32.refs_2_.refs_6_) | copy-start | bytes 1572868
  77.0 9.7 %copy-start.13 = (bf16[16,1024]{1,0:T(8,128)(2,1)S(1)}, bf16[16,1024]{1,0:T(8,128)(2,1)}, u32[]{:S(2)}) copy-start(bf16[16,1024]{1,0:T(8,128)(2,1)} %copy-done.12) | copy-start | bytes 98308
  77.0 3.1 %collective-permute-start.3 = (f32[2,256]{1,0:T(2,128)S(1)}, f32[2,256]{1,0:T(2,128)S(1)}, u32[]{:S(2)}, u32[]{:S(2)}) collective-permute-start(f32[2,256]{1,0:T(2,128)S(1)} %sums.1.refs_0_), channel_id=1, source_target_pairs={{0,3},{1,2},{2,1},{3,0},{4,7},{5,6},{6,5},{7,4},{8,11},{9,10},{10,... | collective-permute-start | bytes 6152 | tf_op jit(solution)/shard_map/ppermute | solution.py:650
  77.1 3.7 %collective-permute-start.2 = (f32[2,256]{1,0:T(2,128)S(1)}, f32[2,256]{1,0:T(2,128)S(1)}, u32[]{:S(2)}, u32[]{:S(2)}) collective-permute-start(f32[2,256]{1,0:T(2,128)S(1)} %sums.1.refs_0_), channel_id=1, source_target_pairs={{0,2},{1,3},{2,0},{3,1},{4,6},{5,7},{6,4},{7,5},{8,10},{9,11},{10,... | collective-permute-start | bytes 6152 | tf_op jit(solution)/shard_map/ppermute | solution.py:650
  78.7 2.1 %collective-permute-start.1 = (f32[2,256]{1,0:T(2,128)S(1)}, f32[2,256]{1,0:T(2,128)S(1)}, u32[]{:S(2)}, u32[]{:S(2)}) collective-permute-start(f32[2,256]{1,0:T(2,128)S(1)} %sums.1.refs_0_), channel_id=1, source_target_pairs={{0,1},{1,0},{2,3},{3,2},{4,5},{5,4},{6,7},{7,6},{8,9},{9,8},{10,11... | collective-permute-start | bytes 6152 | tf_op jit(solution)/shard_map/ppermute | solution.py:650
  82.0 20.2 %all-to-all-start.2 = ((bf16[8,128,256]{2,1,0:T(8,128)(2,1)}), bf16[8,128,256]{2,1,0:T(8,128)(2,1)}, u32[]{:S(2)}, u32[]{:S(2)}) async-start(bf16[8,128,256]{2,1,0:T(8,128)(2,1)} %bitcast.8), calls=%async_computation.2 | async-start | bytes 1048576 | tf_op jit(solution)/shard_map/all_to_all | solution.py:607
  86.7 6.0 %copy-start.29 = (bf16[16,1024]{1,0:T(8,128)(2,1)S(1)}, bf16[16,1024]{1,0:T(8,128)(2,1)}, u32[]{:S(2)}) copy-start(bf16[16,1024]{1,0:T(8,128)(2,1)} %get-tuple-element.41) | copy-start | bytes 98308
  91.4 6.1 %collective-permute-start.4 = (bf16[16,1024]{1,0:T(8,128)(2,1)S(1)}, bf16[16,1024]{1,0:T(8,128)(2,1)S(1)}, u32[]{:S(2)}, u32[]{:S(2)}) collective-permute-start(bf16[16,1024]{1,0:T(8,128)(2,1)S(1)} %get-tuple-element.35), channel_id=1, source_target_pairs={{4,0},{8,4},{12,8},{16,12},{20,16},{24,20},{28,24},{5,1},{9,5},{13... | collective-permute-start | bytes 98312 | tf_op jit(solution)/shard_map/ppermute | solution.py:31
  92.7 33.8 %collective-permute-start.5 = (bf16[16,1024]{1,0:T(8,128)(2,1)S(1)}, bf16[16,1024]{1,0:T(8,128)(2,1)S(1)}, u32[]{:S(2)}, u32[]{:S(2)}) collective-permute-start(bf16[16,1024]{1,0:T(8,128)(2,1)S(1)} %copy-done.29), channel_id=1, source_target_pairs={{4,0},{8,4},{12,8},{16,12},{20,16},{24,20},{28,24},{5,1},{9,5},{13... | collective-permute-start | bytes 98312 | tf_op jit(solution)/shard_map/ppermute | solution.py:31
  102.2 10.9 %copy-start.8 = (bf16[8,384,256]{2,1,0:T(8,128)(2,1)S(1)}, bf16[8,384,256]{2,1,0:T(8,128)(2,1)}, u32[]{:S(2)}) copy-start(bf16[8,384,256]{2,1,0:T(8,128)(2,1)} %copy-done.7) | copy-start | bytes 4718596
  108.2 19.1 %all-to-all-start.3 = ((bf16[8,144,256]{2,1,0:T(8,128)(2,1)}), bf16[8,144,256]{2,1,0:T(8,128)(2,1)S(1)}, u32[]{:S(2)}, u32[]{:S(2)}) async-start(bf16[8,144,256]{2,1,0:T(8,128)(2,1)} %correlate.1.refs_0_), calls=%async_computation.3 | async-start | bytes 1179648 | tf_op jit(solution)/shard_map/all_to_all | solution.py:607
  115.2 3.5 %copy-start.22 = (f32[2,16,2,128]{3,2,1,0:T(2,128)S(1)}, f32[2,16,2,128]{3,2,1,0:T(2,128)}, u32[]{:S(2)}) copy-start(f32[2,16,2,128]{3,2,1,0:T(2,128)} %constant.20.clone.refs_2_.refs_3_) | copy-start | bytes 98308
  115.2 3.5 %copy-start.25 = (bf16[8,128,256]{2,1,0:T(8,128)(2,1)S(1)}, bf16[8,128,256]{2,1,0:T(8,128)(2,1)}, u32[]{:S(2)}) copy-start(bf16[8,128,256]{2,1,0:T(8,128)(2,1)} %copy-done.23) | copy-start | bytes 1572868
  118.7 8.7 %copy-start.10 = (bf16[1024,256]{1,0:T(8,128)(2,1)S(1)}, bf16[1024,256]{1,0:T(8,128)(2,1)}, u32[]{:S(2)}) copy-start(bf16[1024,256]{1,0:T(8,128)(2,1)} %get-tuple-element.39.refs_2_) | copy-start | bytes 1572868
  118.7 8.7 %copy-start.11 = (bf16[1024,256]{1,0:T(8,128)(2,1)S(1)}, bf16[1024,256]{1,0:T(8,128)(2,1)}, u32[]{:S(2)}) copy-start(bf16[1024,256]{1,0:T(8,128)(2,1)} %get-tuple-element.40.refs_3_) | copy-start | bytes 1572868
  (8 other events, 13.0 us)

commit v3 on v2

--- a/solution.py
+++ b/solution.py
@@ -14,6 +14,7 @@
 HALF = 8
 VMEM_MOST = 24 * 2**20
 VMEM_ALL = 60 * 2**20
+VMEM_FFT = 50 * 2**20
 PARTS = 4
 
 
@@ -313,14 +314,39 @@
     token_ref[...] = jnp.zeros_like(token_ref)
 
 
-def place(kernel, name, outs, args, scratch=(), flops=10**6, after=(), vmem=VMEM_MOST):
+def place(kernel, name, outs, args, scratch=(), flops=10**6, after=(), vmem=VMEM_MOST, lazy=()):
     n_args, n_outs = len(args), len(outs)
+    drawn = [a[0] for a in lazy]
     far = [k for k in range(n_outs) if len(outs[k]) == 4]
 
     def body(*refs):
         out_refs = list(refs[n_args + len(after) :][:n_outs])
         rest = refs[n_args + len(after) + n_outs :]
-        own, stages, sems = rest[: len(scratch)], rest[len(scratch) :][: len(far)], rest[len(scratch) + len(far) :]
+        own, rest = rest[: len(scratch)], rest[len(scratch) :]
+        stages, rest = rest[: len(far)], rest[len(far) :]
+        sems, rest = rest[: len(far)], rest[len(far) :]
+        held, waits = rest[: len(lazy)], rest[len(lazy) :]
+        ins = list(refs[:n_args])
+
+        def fetch(j, i):
+            k, axis, pieces = lazy[j]
+            size = args[k].shape[axis] // pieces
+            start = i * size if isinstance(i, int) else pl.multiple_of(i * size, size)
+            at = (slice(None),) * axis + (pl.ds(start, size),)
+            return pltpu.make_async_copy(refs[k].at[at], held[j].at[at], waits[j].at[i])
+
+        for i in range(max([a[2] for a in lazy], default=0)):
+            for j in range(len(lazy)):
+                if i < lazy[j][2]:
+                    fetch(j, i).start()
+        for j, k in enumerate(drawn):
+            ins[k] = held[j]
+
+        def need(i=None):
+            for j in range(len(lazy)):
+                if (i is None) == (lazy[j][2] == 1):
+                    fetch(j, 0 if i is None else i).wait()
+
 
         def copy(j, i):
             axis, pieces = outs[far[j]][2:]
@@ -336,7 +362,8 @@
         shown = list(out_refs)
         for j, k in enumerate(far):
             shown[k] = stages[j]
-        kernel(*refs[:n_args], *shown, *own, sent=sent)
+        more = {"need": need} if lazy else {}
+        kernel(*ins, *shown, *own, sent=sent, **more)
         for j, k in enumerate(far):
             for i in range(outs[k][3]):
                 copy(j, i).wait()
@@ -345,12 +372,14 @@
     away = pl.BlockSpec(memory_space=pltpu.HBM)
     return pl.pallas_call(
         body,
-        in_specs=[near] * n_args + [away] * len(after),
+        in_specs=[away if k in drawn else near for k in range(n_args)] + [away] * len(after),
         out_specs=[away if k in far else near for k in range(n_outs)],
         out_shape=[jax.ShapeDtypeStruct(*o[:2]) for o in outs],
         scratch_shapes=list(scratch)
         + [pltpu.VMEM(*outs[k][:2]) for k in far]
-        + [pltpu.SemaphoreType.DMA((outs[k][3],)) for k in far],
+        + [pltpu.SemaphoreType.DMA((outs[k][3],)) for k in far]
+        + [pltpu.VMEM(args[k].shape, args[k].dtype) for k in drawn]
+        + [pltpu.SemaphoreType.DMA((a[2],)) for a in lazy],
         compiler_params=pltpu.CompilerParams(vmem_limit_bytes=vmem),
         cost_estimate=pl.CostEstimate(flops=flops, bytes_accessed=4 * 2**20, transcendentals=0),
         name=name,
@@ -377,7 +406,7 @@
 
     def convolve(pack, cols, after):
         args = (pack, cols, *tables)
-        return place(convolve_kernel, "convolve", [result, spec, result, TOKEN], args, [work, outs], 3 * flops, after)
+        return place(convolve_kernel, "convolve", [result, spec, result, TOKEN], args, [work, outs], 3 * flops, after, VMEM_FFT)
 
     def correlate(grad, spec, early):
         args = (grad, spec, early, *tables)
@@ -454,9 +483,11 @@
     return jnp.concatenate([moved[:, : count - LANES], last], 1)
 
 
-def over_rows(ref, body, done=None, block=32):
+def over_rows(ref, body, done=None, block=32, before=None):
     piece = ref.shape[0] // PARTS
     for row in range(0, ref.shape[0], block):
+        if before and row % piece == 0:
+            before(row // piece)
         body(slice(row, row + block))
         if done and (row + block) % piece == 0:
             done(row // piece)
@@ -572,7 +603,7 @@
 
 
 def pair_kernel(
-    back_ref, inner_ref, s1_ref, s2_ref, cols_ref, tips_ref, next_ref, bias_ref, grads_ref, d1_ref, d2_ref, *refs, sent
+    back_ref, inner_ref, s1_ref, s2_ref, cols_ref, tips_ref, next_ref, bias_ref, grads_ref, d1_ref, d2_ref, *refs, sent, need
 ):
     short_ref, gain_ref, fill, edge = refs
     parts, longer, _ = back_ref.shape
@@ -600,7 +631,7 @@
             g = f32(bf16(d_gated * f32(s_ref[rows])))
             d_ref[rows] = adjoint(g, b, fill, b - 1, rows, cols_ref)
 
-    over_rows(d1_ref, body, sent, min(32, own))
+    over_rows(d1_ref, body, sent, min(32, own), need)
 
 
 def exchange(value):
@@ -671,6 +702,7 @@
         (back, d_inner, second_s, third_s, cols, tips, after, skip_bias[None], own_rows),
         [fills(2), pltpu.VMEM(*edges)],
         after=(first_done, lags_done),
+        lazy=[(1, 0, PARTS)],
     )
     return (output, d_first, d_second, d_value, d_long, d_short, own_rows[6], d_gain[0])
 

time: 136 us -> 134 us (0.985)
    unnamed x60 -> x58, local copies, waits for them, and re-layouts: 6.28 us -> 4.96 us
where the time goes in v3:
time: 134 us; the launch traced here: 133 us
  waiting for transfers between devices  47 us (35%)
  Pallas kernels  46 us (34%)
  starting transfers between devices  29.4 us (22%)
  local copies, waits for them, and re-layouts  6.56 us (5%)
  other arithmetic  2.66 us (2%)
    pallas_call x10, Pallas kernels, place(): pl.pallas_call(body, in_specs=[away if k in drawn else near for k in rang...  43.9 us
    all_to_all x4, waiting for transfers between devices, exchange(): return lax.all_to_all(value, 'ctx', split_axis=0, concat_axis=0, tiled=True)  34.6 us
    all_to_all x4, starting transfers between devices, exchange(): return lax.all_to_all(value, 'ctx', split_axis=0, concat_axis=0, tiled=True)  20.8 us
    ppermute x3, waiting for transfers between devices, shifted(): lax.ppermute(value, axis, [(source, source + steps) for source in range(f...  10.6 us
    ppermute x3, starting transfers between devices, shifted(): lax.ppermute(value, axis, [(source, source + steps) for source in range(f...  6.65 us
    unnamed x58, local copies, waits for them, and re-layouts  4.96 us
  transfers between devices with their start and end apart: 10, of which 8 were waited for; matrix products, arithmetic and copies ran while one was open for 1% of the time, Pallas kernels for 23%

profile of v3, /device:TPU:0, one launch (start us, length us, event | category | flops | bytes accessed | tf_op | source)
XLA Modules:
  0.0 132.7 jit_solution(10674644590321958629)
XLA Ops:
  0.6 2.6 %pad_maximum_fusion = bf16[8,384,256]{2,1,0:T(8,128)(2,1)} fusion(bf16[8,128,256]{2,1,0:T(8,128)(2,1)} %bitcast.19, bf16[8,128,256]{2,1,0:T(8,128)(2,1)} %bitcast.20, bf16[8,128,256]{2,1,0:T(8,128)(2,1)} %bitcast.21), kind=kLoop, calls=%fused_computation | loop fusion | flops 4718592 | bytes 3145728 | tf_op jit(solution)/shard_map/concatenate | solution.py:657
  3.3 7.4 %all-to-all-start = ((bf16[8,384,256]{2,1,0:T(8,128)(2,1)}), bf16[8,384,256]{2,1,0:T(8,128)(2,1)S(1)}, u32[]{:S(2)}, u32[]{:S(2)}) async-start(bf16[8,384,256]{2,1,0:T(8,128)(2,1)} %pad_maximum_fusion), calls=%async_computation | async-start | bytes 3145728 | tf_op jit(solution)/shard_map/all_to_all | solution.py:638
  10.7 2.1 %edge.1 = bf16[16,1024]{1,0:T(8,128)(2,1)} custom-call(bf16[1024,256]{1,0:T(8,128)(2,1)} %refs_9_.1, bf16[1024,256]{1,0:T(8,128)(2,1)} %refs_1_.1, bf16[1024,256]{1,0:T(8,128)(2,1)} %refs_2_.3), custom_call_target="tpu_custom_call" | custom-call | tf_op jit(solution)/shard_map/edge/pallas_call | solution.py:659
  12.8 3.9 %collective-permute-start = (bf16[16,1024]{1,0:T(8,128)(2,1)}, bf16[16,1024]{1,0:T(8,128)(2,1)S(1)}, u32[]{:S(2)}, u32[]{:S(2)}) collective-permute-start(bf16[16,1024]{1,0:T(8,128)(2,1)} %edge.1), channel_id=1, source_target_pairs={{0,4},{4,8},{8,12},{12,16},{16,20},{20,24},{24,28},{1,5},{5,9},{9,... | collective-permute-start | bytes 98312 | tf_op jit(solution)/shard_map/ppermute | solution.py:32
  17.0 7.3 %collective-permute-done.refs_5_.refs_3_.refs_10_ = bf16[16,1024]{1,0:T(8,128)(2,1)S(1)} collective-permute-done((bf16[16,1024]{1,0:T(8,128)(2,1)}, bf16[16,1024]{1,0:T(8,128)(2,1)S(1)}, u32[]{:S(2)}, u32[]{:S(2)}) %collective-permute-start) | collective-permute-done | bytes 32800 | tf_op jit(solution)/shard_map/ppermute | solution.py:32
  24.3 23.4 %all-to-all-done.refs_0_.refs_2_ = bf16[8,384,256]{2,1,0:T(8,128)(2,1)S(1)} async-done(((bf16[8,384,256]{2,1,0:T(8,128)(2,1)}), bf16[8,384,256]{2,1,0:T(8,128)(2,1)S(1)}, u32[]{:S(2)}, u32[]{:S(2)}) %all-to-all-start) | async-done | bytes 1572896 | tf_op jit(solution)/shard_map/all_to_all | solution.py:638
  47.7 6.8 %convolve.1 = (bf16[8,128,256]{2,1,0:T(8,128)(2,1)}, f32[8,256,256]{2,1,0:T(8,128)}, bf16[8,128,256]{2,1,0:T(8,128)(2,1)S(1)}, f32[8,128]{1,0:T(8,128)S(1)}) custom-call(bf16[8,384,256]{2,1,0:T(8,128)(2,1)S(1)} %all-to-all-done.refs_0_.refs_2_, f32[128,16]{1,0:T(8,128)S(1)} %fusion.refs_1_.refs_4_, f32[2,16,2,128]{3,2,1,0:T(2,128)S(1)} %copy-done.21, ...), custom_call_target="tpu_custom_call" | custom-call | flops 9663676416 | bytes 4194304 | tf_op jit(solution)/shard_map/convolve/pallas_call | solution.py:373
  54.5 3.9 %all-to-all-start.1 = ((bf16[8,128,256]{2,1,0:T(8,128)(2,1)}), bf16[8,128,256]{2,1,0:T(8,128)(2,1)S(1)}, u32[]{:S(2)}, u32[]{:S(2)}) async-start(bf16[8,128,256]{2,1,0:T(8,128)(2,1)} %get-tuple-element.29), calls=%async_computation.1 | async-start | bytes 1048576 | tf_op jit(solution)/shard_map/all_to_all | solution.py:638
  58.4 0.8 pad_bitcast_fusion.refs_4_.refs_8_.refs_2_
  59.2 6.1 %gate.1 = (bf16[1024,256]{1,0:T(8,128)(2,1)}, bf16[1024,256]{1,0:T(8,128)(2,1)}, bf16[1024,256]{1,0:T(8,128)(2,1)}, bf16[1024,256]{1,0:T(8,128)(2,1)}, bf16[16,1024]{1,0:T(8,128)(2,1)}) custom-call(bf16[1024,256]{1,0:T(8,128)(2,1)} %refs_9_.1, bf16[1024,256]{1,0:T(8,128)(2,1)} %refs_1_.1, bf16[1024,256]{1,0:T(8,128)(2,1)} %refs_2_.3, ...), custom_call_target="tpu_custom_call" | custom-call | flops 1000000 | bytes 4194304 | tf_op jit(solution)/shard_map/gate/pallas_call | solution.py:373
  65.4 7.6 %all-to-all-done.1 = bf16[8,128,256]{2,1,0:T(8,128)(2,1)S(1)} async-done(((bf16[8,128,256]{2,1,0:T(8,128)(2,1)}), bf16[8,128,256]{2,1,0:T(8,128)(2,1)S(1)}, u32[]{:S(2)}, u32[]{:S(2)}) %all-to-all-start.1) | async-done | bytes 524320 | tf_op jit(solution)/shard_map/all_to_all | solution.py:638
  73.0 1.0 copy-done.3
  74.0 1.0 copy-done.5
  75.7 1.6 %collective-permute-start.2 = (f32[2,256]{1,0:T(2,128)S(1)}, f32[2,256]{1,0:T(2,128)S(1)}, u32[]{:S(2)}, u32[]{:S(2)}) collective-permute-start(f32[2,256]{1,0:T(2,128)S(1)} %sums.1.refs_0_), channel_id=1, source_target_pairs={{0,2},{1,3},{2,0},{3,1},{4,6},{5,7},{6,4},{7,5},{8,10},{9,11},{10,... | collective-permute-start | bytes 6152 | tf_op jit(solution)/shard_map/ppermute | solution.py:681
  77.6 1.1 collective-permute-done.3.refs_3_
  78.7 0.7 collective-permute-done.2.refs_2_
  79.4 1.2 inner.1.refs_11_.refs_1_
  80.6 4.7 %all-to-all-start.2 = ((bf16[8,128,256]{2,1,0:T(8,128)(2,1)}), bf16[8,128,256]{2,1,0:T(8,128)(2,1)}, u32[]{:S(2)}, u32[]{:S(2)}) async-start(bf16[8,128,256]{2,1,0:T(8,128)(2,1)} %bitcast.8), calls=%async_computation.2 | async-start | bytes 1048576 | tf_op jit(solution)/shard_map/all_to_all | solution.py:638
  85.3 4.1 %output.1 = (bf16[1024,256]{1,0:T(8,128)(2,1)}, bf16[1024,256]{1,0:T(8,128)(2,1)S(1)}, f32[8,1024]{1,0:T(8,128)S(1)}, bf16[16,1024]{1,0:T(8,128)(2,1)S(1)}) custom-call(f32[2,256]{1,0:T(2,128)S(1)} %sums.1.refs_0_, f32[2,256]{1,0:T(2,128)S(1)} %collective-permute-done.1.refs_1_, f32[2,256]{1,0:T(2,128)S(1)} %collective-permute-done.2.refs_2_, ...), custom_call_target="tpu_custom_call" | custom-call | flops 1000000 | bytes 4194304 | tf_op jit(solution)/shard_map/output/pallas_call | solution.py:373
  90.0 1.3 collective-permute-start.4
  91.3 1.5 %collective-permute-start.5 = (bf16[16,1024]{1,0:T(8,128)(2,1)S(1)}, bf16[16,1024]{1,0:T(8,128)(2,1)S(1)}, u32[]{:S(2)}, u32[]{:S(2)}) collective-permute-start(bf16[16,1024]{1,0:T(8,128)(2,1)S(1)} %copy-done.28), channel_id=1, source_target_pairs={{4,0},{8,4},{12,8},{16,12},{20,16},{24,20},{28,24},{5,1},{9,5},{13... | collective-permute-start | bytes 98312 | tf_op jit(solution)/shard_map/ppermute | solution.py:32
  92.8 3.3 %collective-permute-done.4.refs_1_.refs_6_ = bf16[16,1024]{1,0:T(8,128)(2,1)S(1)} collective-permute-done((bf16[16,1024]{1,0:T(8,128)(2,1)S(1)}, bf16[16,1024]{1,0:T(8,128)(2,1)S(1)}, u32[]{:S(2)}, u32[]{:S(2)}) %collective-permute-start.4) | collective-permute-done | bytes 32800 | tf_op jit(solution)/shard_map/ppermute | solution.py:32
  96.2 1.8 %first.1 = (bf16[1024,256]{1,0:T(8,128)(2,1)}, f32[8,128]{1,0:T(8,128)S(1)}) custom-call(bf16[1024,256]{1,0:T(8,128)(2,1)S(1)} %get-tuple-element.34.refs_0_, bf16[16,1024]{1,0:T(8,128)(2,1)S(1)} %collective-permute-done.4.refs_1_.refs_6_, f32[1024,16]{1,0:T(8,128)S(1)} %copy-done), custom_call_target="tpu_custom_call" | custom-call | flops 1000000 | bytes 4194304 | tf_op jit(solution)/shard_map/first/pallas_call | solution.py:373
  98.0 2.8 %all-to-all-done.2.refs_0_.refs_1_ = bf16[8,128,256]{2,1,0:T(8,128)(2,1)} async-done(((bf16[8,128,256]{2,1,0:T(8,128)(2,1)}), bf16[8,128,256]{2,1,0:T(8,128)(2,1)}, u32[]{:S(2)}, u32[]{:S(2)}) %all-to-all-start.2) | async-done | bytes 524320 | tf_op jit(solution)/shard_map/all_to_all | solution.py:638
  100.8 6.0 %correlate.1.refs_0_ = bf16[8,144,256]{2,1,0:T(8,128)(2,1)} custom-call(bf16[8,128,256]{2,1,0:T(8,128)(2,1)} %all-to-all-done.2.refs_0_.refs_1_, f32[8,256,256]{2,1,0:T(8,128)} %get-tuple-element.37.refs_1_, f32[8,1024]{1,0:T(8,128)} %copy-done.16, f32[2,16,2,128]{3,2,1,0:T(2,128)} %constant.20.clone.refs_2_.refs_3_, ...), custom_call_target="tpu_custom_call" | custom-call | flops 6442450944 | bytes 4194304 | tf_op jit(solution)/shard_map/correlate/pallas_call | solution.py:373
  106.9 4.9 %all-to-all-start.3 = ((bf16[8,144,256]{2,1,0:T(8,128)(2,1)}), bf16[8,144,256]{2,1,0:T(8,128)(2,1)S(1)}, u32[]{:S(2)}, u32[]{:S(2)}) async-start(bf16[8,144,256]{2,1,0:T(8,128)(2,1)} %correlate.1.refs_0_), calls=%async_computation.3 | async-start | bytes 1179648 | tf_op jit(solution)/shard_map/all_to_all | solution.py:638
  111.7 1.1 copy-done.9
  112.8 1.0 copy-done.24
  113.9 3.4 %grads.1.refs_8_ = f32[8,128]{1,0:T(8,128)S(1)} custom-call(bf16[8,144,256]{2,1,0:T(8,128)(2,1)S(1)} %copy-done.9, bf16[8,128,256]{2,1,0:T(8,128)(2,1)} %all-to-all-done.2.refs_0_.refs_1_, bf16[8,384,256]{2,1,0:T(8,128)(2,1)S(1)} %copy-done.8, bf16[8,128,256]{2,1,0:T(8,128)(2,1)S(1)} %copy-done.24, f32[128,16]{1,0:T(8,128)S(1)} %fusion.refs_1_.refs_4_), custom_call_target="tpu_custom_call" | custom-call | flops 3221225472 | bytes 4194304 | tf_op jit(solution)/shard_map/grads/pallas_call | solution.py:373
  117.4 7.3 %lags.1 = (f32[128,2048]{1,0:T(8,128)}, f32[8,128]{1,0:T(8,128)S(1)}) custom-call(bf16[8,128,256]{2,1,0:T(8,128)(2,1)S(1)} %copy-done.25, bf16[8,128,256]{2,1,0:T(8,128)(2,1)} %all-to-all-done.2.refs_0_.refs_1_, f32[2,16,2,128]{3,2,1,0:T(2,128)S(1)} %copy-done.22, bf16[2,256,256]{2,1,0:T(8,128)(2,1)S(1)} %copy-done.20, bf16[2,256,256]{2,1,0:T(8,128)(2,1)S(1)} %copy-done.18), custom_call_target="tpu_custom_call" | custom-call | flops 9663676416 | bytes 4194304 | tf_op jit(solution)/shard_map/lags/pallas_call | solution.py:373
  125.2 0.8 all-to-all-done.3.refs_0_
  126.0 6.5 %pair.1 = (bf16[1024,256]{1,0:T(8,128)(2,1)}, bf16[1024,256]{1,0:T(8,128)(2,1)}, f32[3,3,128]{2,1,0:T(4,128)}, f32[1,128]{1,0:T(1,128)}) custom-call(bf16[8,144,256]{2,1,0:T(8,128)(2,1)S(1)} %all-to-all-done.3.refs_0_, bf16[1024,256]{1,0:T(8,128)(2,1)} %inner.1.refs_11_.refs_1_, bf16[1024,256]{1,0:T(8,128)(2,1)S(1)} %copy-done.10, ...), custom_call_target="tpu_custom_call" | custom-call | flops 1000000 | bytes 4194304 | tf_op jit(solution)/shard_map/pair/pallas_call | solution.py:373
  (64 shorter events, 2.4 us)
Async XLA Ops:
  3.3 13.4 %copy-start.26 = (f32[3,3,1024]{2,1,0:T(4,128)S(1)}, f32[3,3,1024]{2,1,0:T(4,128)}, u32[]{:S(2)}) copy-start(f32[3,3,1024]{2,1,0:T(4,128)} %param.14) | copy-start | bytes 110596
  3.3 13.5 %copy-start.14 = (f32[1024]{0:T(1024)S(1)}, f32[1024]{0:T(1024)}, u32[]{:S(2)}) copy-start(f32[1024]{0:T(1024)} %param.16) | copy-start | bytes 12292
  3.3 13.5 %copy-start.27 = (f32[1024]{0:T(1024)S(1)}, f32[1024]{0:T(1024)}, u32[]{:S(2)}) copy-start(f32[1024]{0:T(1024)} %param.17) | copy-start | bytes 12292
  3.3 44.4 %all-to-all-start = ((bf16[8,384,256]{2,1,0:T(8,128)(2,1)}), bf16[8,384,256]{2,1,0:T(8,128)(2,1)S(1)}, u32[]{:S(2)}, u32[]{:S(2)}) async-start(bf16[8,384,256]{2,1,0:T(8,128)(2,1)} %pad_maximum_fusion), calls=%async_computation | async-start | bytes 3145728 | tf_op jit(solution)/shard_map/all_to_all | solution.py:638
  10.7 37.0 %copy-start.17 = (bf16[2,256,256]{2,1,0:T(8,128)(2,1)S(1)}, bf16[2,256,256]{2,1,0:T(8,128)(2,1)}, u32[]{:S(2)}) copy-start(bf16[2,256,256]{2,1,0:T(8,128)(2,1)} %constant.22.clone.refs_4_.refs_5_) | copy-start | bytes 786436
  10.7 37.0 %copy-start.19 = (bf16[2,256,256]{2,1,0:T(8,128)(2,1)S(1)}, bf16[2,256,256]{2,1,0:T(8,128)(2,1)}, u32[]{:S(2)}) copy-start(bf16[2,256,256]{2,1,0:T(8,128)(2,1)} %constant.21.clone.refs_3_.refs_4_) | copy-start | bytes 786436
  10.7 37.0 %copy-start.21 = (f32[2,16,2,128]{3,2,1,0:T(2,128)S(1)}, f32[2,16,2,128]{3,2,1,0:T(2,128)}, u32[]{:S(2)}) copy-start(f32[2,16,2,128]{3,2,1,0:T(2,128)} %constant.20.clone.refs_2_.refs_3_) | copy-start | bytes 98308
  12.8 11.5 %collective-permute-start = (bf16[16,1024]{1,0:T(8,128)(2,1)}, bf16[16,1024]{1,0:T(8,128)(2,1)S(1)}, u32[]{:S(2)}, u32[]{:S(2)}) collective-permute-start(bf16[16,1024]{1,0:T(8,128)(2,1)} %edge.1), channel_id=1, source_target_pairs={{0,4},{4,8},{8,12},{12,16},{16,20},{20,24},{24,28},{1,5},{5,9},{9,... | collective-permute-start | bytes 98312 | tf_op jit(solution)/shard_map/ppermute | solution.py:32
  24.3 30.2 %copy-start.12 = (bf16[16,1024]{1,0:T(8,128)(2,1)}, bf16[16,1024]{1,0:T(8,128)(2,1)S(1)}, u32[]{:S(2)}) copy-start(bf16[16,1024]{1,0:T(8,128)(2,1)S(1)} %collective-permute-done.refs_5_.refs_3_.refs_10_) | copy-start | bytes 98308
  47.7 6.8 %copy-start.7 = (bf16[8,384,256]{2,1,0:T(8,128)(2,1)}, bf16[8,384,256]{2,1,0:T(8,128)(2,1)S(1)}, u32[]{:S(2)}) copy-start(bf16[8,384,256]{2,1,0:T(8,128)(2,1)S(1)} %all-to-all-done.refs_0_.refs_2_) | copy-start | bytes 4718596
  54.5 4.7 %copy-start.15 = (f32[8,128]{1,0:T(8,128)}, f32[8,128]{1,0:T(8,128)S(1)}, u32[]{:S(2)}) copy-start(f32[8,128]{1,0:T(8,128)S(1)} %get-tuple-element.30.refs_5_) | copy-start | bytes 12292
  54.5 10.9 %copy-start.23 = (bf16[8,128,256]{2,1,0:T(8,128)(2,1)}, bf16[8,128,256]{2,1,0:T(8,128)(2,1)S(1)}, u32[]{:S(2)}) copy-start(bf16[8,128,256]{2,1,0:T(8,128)(2,1)S(1)} %get-tuple-element.42.refs_3_.refs_0_) | copy-start | bytes 1572868
  54.5 18.5 %copy-start.2 = (bf16[1024,256]{1,0:T(8,128)(2,1)S(1)}, bf16[1024,256]{1,0:T(8,128)(2,1)}, u32[]{:S(2)}) copy-start(bf16[1024,256]{1,0:T(8,128)(2,1)} %refs_7_.3) | copy-start | bytes 1572868
  54.5 18.5 %all-to-all-start.1 = ((bf16[8,128,256]{2,1,0:T(8,128)(2,1)}), bf16[8,128,256]{2,1,0:T(8,128)(2,1)S(1)}, u32[]{:S(2)}, u32[]{:S(2)}) async-start(bf16[8,128,256]{2,1,0:T(8,128)(2,1)} %get-tuple-element.29), calls=%async_computation.1 | async-start | bytes 1048576 | tf_op jit(solution)/shard_map/all_to_all | solution.py:638
  59.2 13.7 %copy-start = (f32[1024,16]{1,0:T(8,128)S(1)}, f32[1024,16]{1,0:T(8,128)}, u32[]{:S(2)}) copy-start(f32[1024,16]{1,0:T(8,128)} %pad_bitcast_fusion.refs_4_.refs_8_.refs_2_) | copy-start | bytes 196612
  75.1 4.3 %copy-start.4 = (bf16[1024,256]{1,0:T(8,128)(2,1)S(1)}, bf16[1024,256]{1,0:T(8,128)(2,1)}, u32[]{:S(2)}) copy-start(bf16[1024,256]{1,0:T(8,128)(2,1)} %get-tuple-element.31.refs_1_.refs_5_) | copy-start | bytes 1572868
  75.6 9.7 %copy-start.1 = (bf16[1024,256]{1,0:T(8,128)(2,1)S(1)}, bf16[1024,256]{1,0:T(8,128)(2,1)}, u32[]{:S(2)}) copy-start(bf16[1024,256]{1,0:T(8,128)(2,1)} %refs_9_.1) | copy-start | bytes 1572868
  75.6 9.7 %copy-start.6 = (bf16[1024,256]{1,0:T(8,128)(2,1)S(1)}, bf16[1024,256]{1,0:T(8,128)(2,1)}, u32[]{:S(2)}) copy-start(bf16[1024,256]{1,0:T(8,128)(2,1)} %get-tuple-element.32.refs_2_.refs_6_) | copy-start | bytes 1572868
  75.6 9.7 %copy-start.13 = (bf16[16,1024]{1,0:T(8,128)(2,1)S(1)}, bf16[16,1024]{1,0:T(8,128)(2,1)}, u32[]{:S(2)}) copy-start(bf16[16,1024]{1,0:T(8,128)(2,1)} %copy-done.12) | copy-start | bytes 98308
  75.6 3.1 %collective-permute-start.3 = (f32[2,256]{1,0:T(2,128)S(1)}, f32[2,256]{1,0:T(2,128)S(1)}, u32[]{:S(2)}, u32[]{:S(2)}) collective-permute-start(f32[2,256]{1,0:T(2,128)S(1)} %sums.1.refs_0_), channel_id=1, source_target_pairs={{0,3},{1,2},{2,1},{3,0},{4,7},{5,6},{6,5},{7,4},{8,11},{9,10},{10,... | collective-permute-start | bytes 6152 | tf_op jit(solution)/shard_map/ppermute | solution.py:681
  75.7 3.7 %collective-permute-start.2 = (f32[2,256]{1,0:T(2,128)S(1)}, f32[2,256]{1,0:T(2,128)S(1)}, u32[]{:S(2)}, u32[]{:S(2)}) collective-permute-start(f32[2,256]{1,0:T(2,128)S(1)} %sums.1.refs_0_), channel_id=1, source_target_pairs={{0,2},{1,3},{2,0},{3,1},{4,6},{5,7},{6,4},{7,5},{8,10},{9,11},{10,... | collective-permute-start | bytes 6152 | tf_op jit(solution)/shard_map/ppermute | solution.py:681
  77.3 2.1 %collective-permute-start.1 = (f32[2,256]{1,0:T(2,128)S(1)}, f32[2,256]{1,0:T(2,128)S(1)}, u32[]{:S(2)}, u32[]{:S(2)}) collective-permute-start(f32[2,256]{1,0:T(2,128)S(1)} %sums.1.refs_0_), channel_id=1, source_target_pairs={{0,1},{1,0},{2,3},{3,2},{4,5},{5,4},{6,7},{7,6},{8,9},{9,8},{10,11... | collective-permute-start | bytes 6152 | tf_op jit(solution)/shard_map/ppermute | solution.py:681
  80.6 20.2 %all-to-all-start.2 = ((bf16[8,128,256]{2,1,0:T(8,128)(2,1)}), bf16[8,128,256]{2,1,0:T(8,128)(2,1)}, u32[]{:S(2)}, u32[]{:S(2)}) async-start(bf16[8,128,256]{2,1,0:T(8,128)(2,1)} %bitcast.8), calls=%async_computation.2 | async-start | bytes 1048576 | tf_op jit(solution)/shard_map/all_to_all | solution.py:638
  85.3 6.0 %copy-start.28 = (bf16[16,1024]{1,0:T(8,128)(2,1)S(1)}, bf16[16,1024]{1,0:T(8,128)(2,1)}, u32[]{:S(2)}) copy-start(bf16[16,1024]{1,0:T(8,128)(2,1)} %get-tuple-element.41) | copy-start | bytes 98308
  90.0 6.1 %collective-permute-start.4 = (bf16[16,1024]{1,0:T(8,128)(2,1)S(1)}, bf16[16,1024]{1,0:T(8,128)(2,1)S(1)}, u32[]{:S(2)}, u32[]{:S(2)}) collective-permute-start(bf16[16,1024]{1,0:T(8,128)(2,1)S(1)} %get-tuple-element.35), channel_id=1, source_target_pairs={{4,0},{8,4},{12,8},{16,12},{20,16},{24,20},{28,24},{5,1},{9,5},{13... | collective-permute-start | bytes 98312 | tf_op jit(solution)/shard_map/ppermute | solution.py:32
  91.3 33.8 %collective-permute-start.5 = (bf16[16,1024]{1,0:T(8,128)(2,1)S(1)}, bf16[16,1024]{1,0:T(8,128)(2,1)S(1)}, u32[]{:S(2)}, u32[]{:S(2)}) collective-permute-start(bf16[16,1024]{1,0:T(8,128)(2,1)S(1)} %copy-done.28), channel_id=1, source_target_pairs={{4,0},{8,4},{12,8},{16,12},{20,16},{24,20},{28,24},{5,1},{9,5},{13... | collective-permute-start | bytes 98312 | tf_op jit(solution)/shard_map/ppermute | solution.py:32
  100.8 10.9 %copy-start.8 = (bf16[8,384,256]{2,1,0:T(8,128)(2,1)S(1)}, bf16[8,384,256]{2,1,0:T(8,128)(2,1)}, u32[]{:S(2)}) copy-start(bf16[8,384,256]{2,1,0:T(8,128)(2,1)} %copy-done.7) | copy-start | bytes 4718596
  106.9 19.1 %all-to-all-start.3 = ((bf16[8,144,256]{2,1,0:T(8,128)(2,1)}), bf16[8,144,256]{2,1,0:T(8,128)(2,1)S(1)}, u32[]{:S(2)}, u32[]{:S(2)}) async-start(bf16[8,144,256]{2,1,0:T(8,128)(2,1)} %correlate.1.refs_0_), calls=%async_computation.3 | async-start | bytes 1179648 | tf_op jit(solution)/shard_map/all_to_all | solution.py:638
  113.9 3.5 %copy-start.22 = (f32[2,16,2,128]{3,2,1,0:T(2,128)S(1)}, f32[2,16,2,128]{3,2,1,0:T(2,128)}, u32[]{:S(2)}) copy-start(f32[2,16,2,128]{3,2,1,0:T(2,128)} %constant.20.clone.refs_2_.refs_3_) | copy-start | bytes 98308
  113.9 3.5 %copy-start.25 = (bf16[8,128,256]{2,1,0:T(8,128)(2,1)S(1)}, bf16[8,128,256]{2,1,0:T(8,128)(2,1)}, u32[]{:S(2)}) copy-start(bf16[8,128,256]{2,1,0:T(8,128)(2,1)} %copy-done.23) | copy-start | bytes 1572868
  117.3 8.7 %copy-start.10 = (bf16[1024,256]{1,0:T(8,128)(2,1)S(1)}, bf16[1024,256]{1,0:T(8,128)(2,1)}, u32[]{:S(2)}) copy-start(bf16[1024,256]{1,0:T(8,128)(2,1)} %get-tuple-element.39.refs_2_) | copy-start | bytes 1572868
  117.3 8.7 %copy-start.11 = (bf16[1024,256]{1,0:T(8,128)(2,1)S(1)}, bf16[1024,256]{1,0:T(8,128)(2,1)}, u32[]{:S(2)}) copy-start(bf16[1024,256]{1,0:T(8,128)(2,1)} %get-tuple-element.40.refs_3_) | copy-start | bytes 1572868
  (7 other events, 11.7 us)

commit v4 on v3

--- a/solution.py
+++ b/solution.py
@@ -179,11 +179,18 @@
     return store
 
 
+def span_of(per):
+    return math.gcd(per, 2)
+
+
 def over_groups(count, per, body, done):
+    span = span_of(per)
+
     def step(i, carry):
         for g in range(per):
             body(g, pl.multiple_of((i * per + g) * ROWS, ROWS))
-        done(i)
+            if (g + 1) % span == 0:
+                done(i * (per // span) + g // span)
         return carry
 
     lax.fori_loop(0, count // per, step, 0)
@@ -250,8 +257,8 @@
         put_slabs(out_ref, row, slabs.at[g])
 
     def done(i):
-        for g in range(per):
-            sent(i * per + g)
+        for g in range(span_of(per)):
+            sent(i * span_of(per) + g)
 
     over_groups(groups, per, body, done)
     for part in range(parts):
@@ -398,7 +405,7 @@
     work = pltpu.VMEM((per, 2, slabs * ROWS, 2 * LANES), jnp.float32)
     outs = pltpu.VMEM((per, slabs, ROWS, LANES), jnp.float32)
     flops = 2 * 3 * 4 * groups * slabs * ROWS * 256 * 256
-    pieces = groups // per
+    pieces = groups // span_of(per)
     result = ((parts, chans, width), jnp.bfloat16, 1, pieces)
     spec = ((groups, slabs * ROWS, 2 * LANES), jnp.float32, 0, pieces)
 

time: 134 us -> 134 us (level)
  no operation moved by 1% of the time
where the time goes in v4:
time: 134 us; the launch traced here: 133 us
  waiting for transfers between devices  47 us (35%)
  Pallas kernels  46.7 us (35%)
  starting transfers between devices  29.4 us (22%)
  local copies, waits for them, and re-layouts  6.56 us (5%)
  other arithmetic  2.66 us (2%)
    pallas_call x10, Pallas kernels, place(): pl.pallas_call(body, in_specs=[away if k in drawn else near for k in rang...  44.6 us
    all_to_all x4, waiting for transfers between devices, exchange(): return lax.all_to_all(value, 'ctx', split_axis=0, concat_axis=0, tiled=True)  34.6 us
    all_to_all x4, starting transfers between devices, exchange(): return lax.all_to_all(value, 'ctx', split_axis=0, concat_axis=0, tiled=True)  20.8 us
    ppermute x3, waiting for transfers between devices, shifted(): lax.ppermute(value, axis, [(source, source + steps) for source in range(f...  10.6 us
    ppermute x3, starting transfers between devices, shifted(): lax.ppermute(value, axis, [(source, source + steps) for source in range(f...  6.65 us
    unnamed x58, local copies, waits for them, and re-layouts  4.96 us
  transfers between devices with their start and end apart: 10, of which 8 were waited for; matrix products, arithmetic and copies ran while one was open for 1% of the time, Pallas kernels for 23%

profile of v4, /device:TPU:0, one launch (start us, length us, event | category | flops | bytes accessed | tf_op | source)
XLA Modules:
  0.0 133.5 jit_solution(11378452457564593036)
XLA Ops:
  0.6 2.6 %pad_maximum_fusion = bf16[8,384,256]{2,1,0:T(8,128)(2,1)} fusion(bf16[8,128,256]{2,1,0:T(8,128)(2,1)} %bitcast.19, bf16[8,128,256]{2,1,0:T(8,128)(2,1)} %bitcast.20, bf16[8,128,256]{2,1,0:T(8,128)(2,1)} %bitcast.21), kind=kLoop, calls=%fused_computation | loop fusion | flops 4718592 | bytes 3145728 | tf_op jit(solution)/shard_map/concatenate | solution.py:664
  3.3 7.4 %all-to-all-start = ((bf16[8,384,256]{2,1,0:T(8,128)(2,1)}), bf16[8,384,256]{2,1,0:T(8,128)(2,1)S(1)}, u32[]{:S(2)}, u32[]{:S(2)}) async-start(bf16[8,384,256]{2,1,0:T(8,128)(2,1)} %pad_maximum_fusion), calls=%async_computation | async-start | bytes 3145728 | tf_op jit(solution)/shard_map/all_to_all | solution.py:645
  10.7 2.1 %edge.1 = bf16[16,1024]{1,0:T(8,128)(2,1)} custom-call(bf16[1024,256]{1,0:T(8,128)(2,1)} %refs_9_.1, bf16[1024,256]{1,0:T(8,128)(2,1)} %refs_1_.1, bf16[1024,256]{1,0:T(8,128)(2,1)} %refs_2_.3), custom_call_target="tpu_custom_call" | custom-call | tf_op jit(solution)/shard_map/edge/pallas_call | solution.py:666
  12.8 3.9 %collective-permute-start = (bf16[16,1024]{1,0:T(8,128)(2,1)}, bf16[16,1024]{1,0:T(8,128)(2,1)S(1)}, u32[]{:S(2)}, u32[]{:S(2)}) collective-permute-start(bf16[16,1024]{1,0:T(8,128)(2,1)} %edge.1), channel_id=1, source_target_pairs={{0,4},{4,8},{8,12},{12,16},{16,20},{20,24},{24,28},{1,5},{5,9},{9,... | collective-permute-start | bytes 98312 | tf_op jit(solution)/shard_map/ppermute | solution.py:32
  17.0 7.3 %collective-permute-done.refs_5_.refs_3_.refs_10_ = bf16[16,1024]{1,0:T(8,128)(2,1)S(1)} collective-permute-done((bf16[16,1024]{1,0:T(8,128)(2,1)}, bf16[16,1024]{1,0:T(8,128)(2,1)S(1)}, u32[]{:S(2)}, u32[]{:S(2)}) %collective-permute-start) | collective-permute-done | bytes 32800 | tf_op jit(solution)/shard_map/ppermute | solution.py:32
  24.3 23.4 %all-to-all-done.refs_0_.refs_2_ = bf16[8,384,256]{2,1,0:T(8,128)(2,1)S(1)} async-done(((bf16[8,384,256]{2,1,0:T(8,128)(2,1)}), bf16[8,384,256]{2,1,0:T(8,128)(2,1)S(1)}, u32[]{:S(2)}, u32[]{:S(2)}) %all-to-all-start) | async-done | bytes 1572896 | tf_op jit(solution)/shard_map/all_to_all | solution.py:645
  47.7 7.6 %convolve.1 = (bf16[8,128,256]{2,1,0:T(8,128)(2,1)}, f32[8,256,256]{2,1,0:T(8,128)}, bf16[8,128,256]{2,1,0:T(8,128)(2,1)S(1)}, f32[8,128]{1,0:T(8,128)S(1)}) custom-call(bf16[8,384,256]{2,1,0:T(8,128)(2,1)S(1)} %all-to-all-done.refs_0_.refs_2_, f32[128,16]{1,0:T(8,128)S(1)} %fusion.refs_1_.refs_4_, f32[2,16,2,128]{3,2,1,0:T(2,128)S(1)} %copy-done.21, ...), custom_call_target="tpu_custom_call" | custom-call | flops 9663676416 | bytes 4194304 | tf_op jit(solution)/shard_map/convolve/pallas_call | solution.py:380
  55.3 3.9 %all-to-all-start.1 = ((bf16[8,128,256]{2,1,0:T(8,128)(2,1)}), bf16[8,128,256]{2,1,0:T(8,128)(2,1)S(1)}, u32[]{:S(2)}, u32[]{:S(2)}) async-start(bf16[8,128,256]{2,1,0:T(8,128)(2,1)} %get-tuple-element.29), calls=%async_computation.1 | async-start | bytes 1048576 | tf_op jit(solution)/shard_map/all_to_all | solution.py:645
  59.2 0.8 pad_bitcast_fusion.refs_4_.refs_8_.refs_2_
  60.0 6.1 %gate.1 = (bf16[1024,256]{1,0:T(8,128)(2,1)}, bf16[1024,256]{1,0:T(8,128)(2,1)}, bf16[1024,256]{1,0:T(8,128)(2,1)}, bf16[1024,256]{1,0:T(8,128)(2,1)}, bf16[16,1024]{1,0:T(8,128)(2,1)}) custom-call(bf16[1024,256]{1,0:T(8,128)(2,1)} %refs_9_.1, bf16[1024,256]{1,0:T(8,128)(2,1)} %refs_1_.1, bf16[1024,256]{1,0:T(8,128)(2,1)} %refs_2_.3, ...), custom_call_target="tpu_custom_call" | custom-call | flops 1000000 | bytes 4194304 | tf_op jit(solution)/shard_map/gate/pallas_call | solution.py:380
  66.2 7.6 %all-to-all-done.1 = bf16[8,128,256]{2,1,0:T(8,128)(2,1)S(1)} async-done(((bf16[8,128,256]{2,1,0:T(8,128)(2,1)}), bf16[8,128,256]{2,1,0:T(8,128)(2,1)S(1)}, u32[]{:S(2)}, u32[]{:S(2)}) %all-to-all-start.1) | async-done | bytes 524320 | tf_op jit(solution)/shard_map/all_to_all | solution.py:645
  73.8 1.0 copy-done.3
  74.8 1.0 copy-done.5
  76.5 1.6 %collective-permute-start.2 = (f32[2,256]{1,0:T(2,128)S(1)}, f32[2,256]{1,0:T(2,128)S(1)}, u32[]{:S(2)}, u32[]{:S(2)}) collective-permute-start(f32[2,256]{1,0:T(2,128)S(1)} %sums.1.refs_0_), channel_id=1, source_target_pairs={{0,2},{1,3},{2,0},{3,1},{4,6},{5,7},{6,4},{7,5},{8,10},{9,11},{10,... | collective-permute-start | bytes 6152 | tf_op jit(solution)/shard_map/ppermute | solution.py:688
  78.3 1.1 collective-permute-done.3.refs_3_
  79.5 0.7 collective-permute-done.2.refs_2_
  80.2 1.2 inner.1.refs_11_.refs_1_
  81.4 4.7 %all-to-all-start.2 = ((bf16[8,128,256]{2,1,0:T(8,128)(2,1)}), bf16[8,128,256]{2,1,0:T(8,128)(2,1)}, u32[]{:S(2)}, u32[]{:S(2)}) async-start(bf16[8,128,256]{2,1,0:T(8,128)(2,1)} %bitcast.8), calls=%async_computation.2 | async-start | bytes 1048576 | tf_op jit(solution)/shard_map/all_to_all | solution.py:645
  86.1 4.1 %output.1 = (bf16[1024,256]{1,0:T(8,128)(2,1)}, bf16[1024,256]{1,0:T(8,128)(2,1)S(1)}, f32[8,1024]{1,0:T(8,128)S(1)}, bf16[16,1024]{1,0:T(8,128)(2,1)S(1)}) custom-call(f32[2,256]{1,0:T(2,128)S(1)} %sums.1.refs_0_, f32[2,256]{1,0:T(2,128)S(1)} %collective-permute-done.1.refs_1_, f32[2,256]{1,0:T(2,128)S(1)} %collective-permute-done.2.refs_2_, ...), custom_call_target="tpu_custom_call" | custom-call | flops 1000000 | bytes 4194304 | tf_op jit(solution)/shard_map/output/pallas_call | solution.py:380
  90.8 1.3 collective-permute-start.4
  92.1 1.5 %collective-permute-start.5 = (bf16[16,1024]{1,0:T(8,128)(2,1)S(1)}, bf16[16,1024]{1,0:T(8,128)(2,1)S(1)}, u32[]{:S(2)}, u32[]{:S(2)}) collective-permute-start(bf16[16,1024]{1,0:T(8,128)(2,1)S(1)} %copy-done.28), channel_id=1, source_target_pairs={{4,0},{8,4},{12,8},{16,12},{20,16},{24,20},{28,24},{5,1},{9,5},{13... | collective-permute-start | bytes 98312 | tf_op jit(solution)/shard_map/ppermute | solution.py:32
  93.6 3.3 %collective-permute-done.4.refs_1_.refs_6_ = bf16[16,1024]{1,0:T(8,128)(2,1)S(1)} collective-permute-done((bf16[16,1024]{1,0:T(8,128)(2,1)S(1)}, bf16[16,1024]{1,0:T(8,128)(2,1)S(1)}, u32[]{:S(2)}, u32[]{:S(2)}) %collective-permute-start.4) | collective-permute-done | bytes 32800 | tf_op jit(solution)/shard_map/ppermute | solution.py:32
  97.0 1.8 %first.1 = (bf16[1024,256]{1,0:T(8,128)(2,1)}, f32[8,128]{1,0:T(8,128)S(1)}) custom-call(bf16[1024,256]{1,0:T(8,128)(2,1)S(1)} %get-tuple-element.34.refs_0_, bf16[16,1024]{1,0:T(8,128)(2,1)S(1)} %collective-permute-done.4.refs_1_.refs_6_, f32[1024,16]{1,0:T(8,128)S(1)} %copy-done), custom_call_target="tpu_custom_call" | custom-call | flops 1000000 | bytes 4194304 | tf_op jit(solution)/shard_map/first/pallas_call | solution.py:380
  98.8 2.8 %all-to-all-done.2.refs_0_.refs_1_ = bf16[8,128,256]{2,1,0:T(8,128)(2,1)} async-done(((bf16[8,128,256]{2,1,0:T(8,128)(2,1)}), bf16[8,128,256]{2,1,0:T(8,128)(2,1)}, u32[]{:S(2)}, u32[]{:S(2)}) %all-to-all-start.2) | async-done | bytes 524320 | tf_op jit(solution)/shard_map/all_to_all | solution.py:645
  101.6 6.0 %correlate.1.refs_0_ = bf16[8,144,256]{2,1,0:T(8,128)(2,1)} custom-call(bf16[8,128,256]{2,1,0:T(8,128)(2,1)} %all-to-all-done.2.refs_0_.refs_1_, f32[8,256,256]{2,1,0:T(8,128)} %get-tuple-element.37.refs_1_, f32[8,1024]{1,0:T(8,128)} %copy-done.16, f32[2,16,2,128]{3,2,1,0:T(2,128)} %constant.20.clone.refs_2_.refs_3_, ...), custom_call_target="tpu_custom_call" | custom-call | flops 6442450944 | bytes 4194304 | tf_op jit(solution)/shard_map/correlate/pallas_call | solution.py:380
  107.6 4.9 %all-to-all-start.3 = ((bf16[8,144,256]{2,1,0:T(8,128)(2,1)}), bf16[8,144,256]{2,1,0:T(8,128)(2,1)S(1)}, u32[]{:S(2)}, u32[]{:S(2)}) async-start(bf16[8,144,256]{2,1,0:T(8,128)(2,1)} %correlate.1.refs_0_), calls=%async_computation.3 | async-start | bytes 1179648 | tf_op jit(solution)/shard_map/all_to_all | solution.py:645
  112.5 1.1 copy-done.9
  113.6 1.0 copy-done.24
  114.7 3.4 %grads.1.refs_8_ = f32[8,128]{1,0:T(8,128)S(1)} custom-call(bf16[8,144,256]{2,1,0:T(8,128)(2,1)S(1)} %copy-done.9, bf16[8,128,256]{2,1,0:T(8,128)(2,1)} %all-to-all-done.2.refs_0_.refs_1_, bf16[8,384,256]{2,1,0:T(8,128)(2,1)S(1)} %copy-done.8, bf16[8,128,256]{2,1,0:T(8,128)(2,1)S(1)} %copy-done.24, f32[128,16]{1,0:T(8,128)S(1)} %fusion.refs_1_.refs_4_), custom_call_target="tpu_custom_call" | custom-call | flops 3221225472 | bytes 4194304 | tf_op jit(solution)/shard_map/grads/pallas_call | solution.py:380
  118.1 7.2 %lags.1 = (f32[128,2048]{1,0:T(8,128)}, f32[8,128]{1,0:T(8,128)S(1)}) custom-call(bf16[8,128,256]{2,1,0:T(8,128)(2,1)S(1)} %copy-done.25, bf16[8,128,256]{2,1,0:T(8,128)(2,1)} %all-to-all-done.2.refs_0_.refs_1_, f32[2,16,2,128]{3,2,1,0:T(2,128)S(1)} %copy-done.22, bf16[2,256,256]{2,1,0:T(8,128)(2,1)S(1)} %copy-done.20, bf16[2,256,256]{2,1,0:T(8,128)(2,1)S(1)} %copy-done.18), custom_call_target="tpu_custom_call" | custom-call | flops 9663676416 | bytes 4194304 | tf_op jit(solution)/shard_map/lags/pallas_call | solution.py:380
  125.9 0.9 all-to-all-done.3.refs_0_
  126.8 6.5 %pair.1 = (bf16[1024,256]{1,0:T(8,128)(2,1)}, bf16[1024,256]{1,0:T(8,128)(2,1)}, f32[3,3,128]{2,1,0:T(4,128)}, f32[1,128]{1,0:T(1,128)}) custom-call(bf16[8,144,256]{2,1,0:T(8,128)(2,1)S(1)} %all-to-all-done.3.refs_0_, bf16[1024,256]{1,0:T(8,128)(2,1)} %inner.1.refs_11_.refs_1_, bf16[1024,256]{1,0:T(8,128)(2,1)S(1)} %copy-done.10, ...), custom_call_target="tpu_custom_call" | custom-call | flops 1000000 | bytes 4194304 | tf_op jit(solution)/shard_map/pair/pallas_call | solution.py:380
  (64 shorter events, 2.4 us)
Async XLA Ops:
  3.3 13.4 %copy-start.26 = (f32[3,3,1024]{2,1,0:T(4,128)S(1)}, f32[3,3,1024]{2,1,0:T(4,128)}, u32[]{:S(2)}) copy-start(f32[3,3,1024]{2,1,0:T(4,128)} %param.14) | copy-start | bytes 110596
  3.3 13.5 %copy-start.14 = (f32[1024]{0:T(1024)S(1)}, f32[1024]{0:T(1024)}, u32[]{:S(2)}) copy-start(f32[1024]{0:T(1024)} %param.16) | copy-start | bytes 12292
  3.3 13.5 %copy-start.27 = (f32[1024]{0:T(1024)S(1)}, f32[1024]{0:T(1024)}, u32[]{:S(2)}) copy-start(f32[1024]{0:T(1024)} %param.17) | copy-start | bytes 12292
  3.3 44.4 %all-to-all-start = ((bf16[8,384,256]{2,1,0:T(8,128)(2,1)}), bf16[8,384,256]{2,1,0:T(8,128)(2,1)S(1)}, u32[]{:S(2)}, u32[]{:S(2)}) async-start(bf16[8,384,256]{2,1,0:T(8,128)(2,1)} %pad_maximum_fusion), calls=%async_computation | async-start | bytes 3145728 | tf_op jit(solution)/shard_map/all_to_all | solution.py:645
  10.7 37.0 %copy-start.17 = (bf16[2,256,256]{2,1,0:T(8,128)(2,1)S(1)}, bf16[2,256,256]{2,1,0:T(8,128)(2,1)}, u32[]{:S(2)}) copy-start(bf16[2,256,256]{2,1,0:T(8,128)(2,1)} %constant.22.clone.refs_4_.refs_5_) | copy-start | bytes 786436
  10.7 37.0 %copy-start.19 = (bf16[2,256,256]{2,1,0:T(8,128)(2,1)S(1)}, bf16[2,256,256]{2,1,0:T(8,128)(2,1)}, u32[]{:S(2)}) copy-start(bf16[2,256,256]{2,1,0:T(8,128)(2,1)} %constant.21.clone.refs_3_.refs_4_) | copy-start | bytes 786436
  10.7 37.0 %copy-start.21 = (f32[2,16,2,128]{3,2,1,0:T(2,128)S(1)}, f32[2,16,2,128]{3,2,1,0:T(2,128)}, u32[]{:S(2)}) copy-start(f32[2,16,2,128]{3,2,1,0:T(2,128)} %constant.20.clone.refs_2_.refs_3_) | copy-start | bytes 98308
  12.8 11.5 %collective-permute-start = (bf16[16,1024]{1,0:T(8,128)(2,1)}, bf16[16,1024]{1,0:T(8,128)(2,1)S(1)}, u32[]{:S(2)}, u32[]{:S(2)}) collective-permute-start(bf16[16,1024]{1,0:T(8,128)(2,1)} %edge.1), channel_id=1, source_target_pairs={{0,4},{4,8},{8,12},{12,16},{16,20},{20,24},{24,28},{1,5},{5,9},{9,... | collective-permute-start | bytes 98312 | tf_op jit(solution)/shard_map/ppermute | solution.py:32
  24.3 31.0 %copy-start.12 = (bf16[16,1024]{1,0:T(8,128)(2,1)}, bf16[16,1024]{1,0:T(8,128)(2,1)S(1)}, u32[]{:S(2)}) copy-start(bf16[16,1024]{1,0:T(8,128)(2,1)S(1)} %collective-permute-done.refs_5_.refs_3_.refs_10_) | copy-start | bytes 98308
  47.7 7.6 %copy-start.7 = (bf16[8,384,256]{2,1,0:T(8,128)(2,1)}, bf16[8,384,256]{2,1,0:T(8,128)(2,1)S(1)}, u32[]{:S(2)}) copy-start(bf16[8,384,256]{2,1,0:T(8,128)(2,1)S(1)} %all-to-all-done.refs_0_.refs_2_) | copy-start | bytes 4718596
  55.3 4.7 %copy-start.15 = (f32[8,128]{1,0:T(8,128)}, f32[8,128]{1,0:T(8,128)S(1)}, u32[]{:S(2)}) copy-start(f32[8,128]{1,0:T(8,128)S(1)} %get-tuple-element.30.refs_5_) | copy-start | bytes 12292
  55.3 10.9 %copy-start.23 = (bf16[8,128,256]{2,1,0:T(8,128)(2,1)}, bf16[8,128,256]{2,1,0:T(8,128)(2,1)S(1)}, u32[]{:S(2)}) copy-start(bf16[8,128,256]{2,1,0:T(8,128)(2,1)S(1)} %get-tuple-element.42.refs_3_.refs_0_) | copy-start | bytes 1572868
  55.3 18.5 %copy-start.2 = (bf16[1024,256]{1,0:T(8,128)(2,1)S(1)}, bf16[1024,256]{1,0:T(8,128)(2,1)}, u32[]{:S(2)}) copy-start(bf16[1024,256]{1,0:T(8,128)(2,1)} %refs_7_.3) | copy-start | bytes 1572868
  55.3 18.5 %all-to-all-start.1 = ((bf16[8,128,256]{2,1,0:T(8,128)(2,1)}), bf16[8,128,256]{2,1,0:T(8,128)(2,1)S(1)}, u32[]{:S(2)}, u32[]{:S(2)}) async-start(bf16[8,128,256]{2,1,0:T(8,128)(2,1)} %get-tuple-element.29), calls=%async_computation.1 | async-start | bytes 1048576 | tf_op jit(solution)/shard_map/all_to_all | solution.py:645
  60.0 13.8 %copy-start = (f32[1024,16]{1,0:T(8,128)S(1)}, f32[1024,16]{1,0:T(8,128)}, u32[]{:S(2)}) copy-start(f32[1024,16]{1,0:T(8,128)} %pad_bitcast_fusion.refs_4_.refs_8_.refs_2_) | copy-start | bytes 196612
  75.9 4.3 %copy-start.4 = (bf16[1024,256]{1,0:T(8,128)(2,1)S(1)}, bf16[1024,256]{1,0:T(8,128)(2,1)}, u32[]{:S(2)}) copy-start(bf16[1024,256]{1,0:T(8,128)(2,1)} %get-tuple-element.31.refs_1_.refs_5_) | copy-start | bytes 1572868
  76.4 9.7 %copy-start.1 = (bf16[1024,256]{1,0:T(8,128)(2,1)S(1)}, bf16[1024,256]{1,0:T(8,128)(2,1)}, u32[]{:S(2)}) copy-start(bf16[1024,256]{1,0:T(8,128)(2,1)} %refs_9_.1) | copy-start | bytes 1572868
  76.4 9.7 %copy-start.6 = (bf16[1024,256]{1,0:T(8,128)(2,1)S(1)}, bf16[1024,256]{1,0:T(8,128)(2,1)}, u32[]{:S(2)}) copy-start(bf16[1024,256]{1,0:T(8,128)(2,1)} %get-tuple-element.32.refs_2_.refs_6_) | copy-start | bytes 1572868
  76.4 9.7 %copy-start.13 = (bf16[16,1024]{1,0:T(8,128)(2,1)S(1)}, bf16[16,1024]{1,0:T(8,128)(2,1)}, u32[]{:S(2)}) copy-start(bf16[16,1024]{1,0:T(8,128)(2,1)} %copy-done.12) | copy-start | bytes 98308
  76.4 3.1 %collective-permute-start.3 = (f32[2,256]{1,0:T(2,128)S(1)}, f32[2,256]{1,0:T(2,128)S(1)}, u32[]{:S(2)}, u32[]{:S(2)}) collective-permute-start(f32[2,256]{1,0:T(2,128)S(1)} %sums.1.refs_0_), channel_id=1, source_target_pairs={{0,3},{1,2},{2,1},{3,0},{4,7},{5,6},{6,5},{7,4},{8,11},{9,10},{10,... | collective-permute-start | bytes 6152 | tf_op jit(solution)/shard_map/ppermute | solution.py:688
  76.5 3.7 %collective-permute-start.2 = (f32[2,256]{1,0:T(2,128)S(1)}, f32[2,256]{1,0:T(2,128)S(1)}, u32[]{:S(2)}, u32[]{:S(2)}) collective-permute-start(f32[2,256]{1,0:T(2,128)S(1)} %sums.1.refs_0_), channel_id=1, source_target_pairs={{0,2},{1,3},{2,0},{3,1},{4,6},{5,7},{6,4},{7,5},{8,10},{9,11},{10,... | collective-permute-start | bytes 6152 | tf_op jit(solution)/shard_map/ppermute | solution.py:688
  78.1 2.1 %collective-permute-start.1 = (f32[2,256]{1,0:T(2,128)S(1)}, f32[2,256]{1,0:T(2,128)S(1)}, u32[]{:S(2)}, u32[]{:S(2)}) collective-permute-start(f32[2,256]{1,0:T(2,128)S(1)} %sums.1.refs_0_), channel_id=1, source_target_pairs={{0,1},{1,0},{2,3},{3,2},{4,5},{5,4},{6,7},{7,6},{8,9},{9,8},{10,11... | collective-permute-start | bytes 6152 | tf_op jit(solution)/shard_map/ppermute | solution.py:688
  81.4 20.2 %all-to-all-start.2 = ((bf16[8,128,256]{2,1,0:T(8,128)(2,1)}), bf16[8,128,256]{2,1,0:T(8,128)(2,1)}, u32[]{:S(2)}, u32[]{:S(2)}) async-start(bf16[8,128,256]{2,1,0:T(8,128)(2,1)} %bitcast.8), calls=%async_computation.2 | async-start | bytes 1048576 | tf_op jit(solution)/shard_map/all_to_all | solution.py:645
  86.1 6.0 %copy-start.28 = (bf16[16,1024]{1,0:T(8,128)(2,1)S(1)}, bf16[16,1024]{1,0:T(8,128)(2,1)}, u32[]{:S(2)}) copy-start(bf16[16,1024]{1,0:T(8,128)(2,1)} %get-tuple-element.41) | copy-start | bytes 98308
  90.8 6.1 %collective-permute-start.4 = (bf16[16,1024]{1,0:T(8,128)(2,1)S(1)}, bf16[16,1024]{1,0:T(8,128)(2,1)S(1)}, u32[]{:S(2)}, u32[]{:S(2)}) collective-permute-start(bf16[16,1024]{1,0:T(8,128)(2,1)S(1)} %get-tuple-element.35), channel_id=1, source_target_pairs={{4,0},{8,4},{12,8},{16,12},{20,16},{24,20},{28,24},{5,1},{9,5},{13... | collective-permute-start | bytes 98312 | tf_op jit(solution)/shard_map/ppermute | solution.py:32
  92.1 33.8 %collective-permute-start.5 = (bf16[16,1024]{1,0:T(8,128)(2,1)S(1)}, bf16[16,1024]{1,0:T(8,128)(2,1)S(1)}, u32[]{:S(2)}, u32[]{:S(2)}) collective-permute-start(bf16[16,1024]{1,0:T(8,128)(2,1)S(1)} %copy-done.28), channel_id=1, source_target_pairs={{4,0},{8,4},{12,8},{16,12},{20,16},{24,20},{28,24},{5,1},{9,5},{13... | collective-permute-start | bytes 98312 | tf_op jit(solution)/shard_map/ppermute | solution.py:32
  101.6 10.9 %copy-start.8 = (bf16[8,384,256]{2,1,0:T(8,128)(2,1)S(1)}, bf16[8,384,256]{2,1,0:T(8,128)(2,1)}, u32[]{:S(2)}) copy-start(bf16[8,384,256]{2,1,0:T(8,128)(2,1)} %copy-done.7) | copy-start | bytes 4718596
  107.6 19.1 %all-to-all-start.3 = ((bf16[8,144,256]{2,1,0:T(8,128)(2,1)}), bf16[8,144,256]{2,1,0:T(8,128)(2,1)S(1)}, u32[]{:S(2)}, u32[]{:S(2)}) async-start(bf16[8,144,256]{2,1,0:T(8,128)(2,1)} %correlate.1.refs_0_), calls=%async_computation.3 | async-start | bytes 1179648 | tf_op jit(solution)/shard_map/all_to_all | solution.py:645
  114.7 3.5 %copy-start.22 = (f32[2,16,2,128]{3,2,1,0:T(2,128)S(1)}, f32[2,16,2,128]{3,2,1,0:T(2,128)}, u32[]{:S(2)}) copy-start(f32[2,16,2,128]{3,2,1,0:T(2,128)} %constant.20.clone.refs_2_.refs_3_) | copy-start | bytes 98308
  114.7 3.5 %copy-start.25 = (bf16[8,128,256]{2,1,0:T(8,128)(2,1)S(1)}, bf16[8,128,256]{2,1,0:T(8,128)(2,1)}, u32[]{:S(2)}) copy-start(bf16[8,128,256]{2,1,0:T(8,128)(2,1)} %copy-done.23) | copy-start | bytes 1572868
  118.1 8.7 %copy-start.10 = (bf16[1024,256]{1,0:T(8,128)(2,1)S(1)}, bf16[1024,256]{1,0:T(8,128)(2,1)}, u32[]{:S(2)}) copy-start(bf16[1024,256]{1,0:T(8,128)(2,1)} %get-tuple-element.39.refs_2_) | copy-start | bytes 1572868
  118.1 8.7 %copy-start.11 = (bf16[1024,256]{1,0:T(8,128)(2,1)S(1)}, bf16[1024,256]{1,0:T(8,128)(2,1)}, u32[]{:S(2)}) copy-start(bf16[1024,256]{1,0:T(8,128)(2,1)} %get-tuple-element.40.refs_3_) | copy-start | bytes 1572868
  (7 other events, 11.7 us)
